TPU v7x, 256 devices: a whole 4x4x8 slice. The times are simulated.
256 devices in a mesh: pole: 4 (over y_lo, core), grid: 64 (over x, y_hi, z).
Axes of the slice: x: 4, y: 4 (y_hi: 2, y_lo: 2; y = y_hi * 2 + y_lo), z: 8, core: 2. Of those that a mesh axis runs over, the one named last changes fastest.
Arguments:
- ainv_anc: bfloat16 [4, 2, 1024, 1024], P('pole', None, 'grid'), may hold values from -6 to 6
- lower_panels: bfloat16 [4, 2, 1024, 16384], P('pole', None, None, 'grid'), may hold values from -0.125 to 0.125
- fill_pattern: int32 [64, 4], P('grid'), may hold values 0 or 1
- diag_inverse: bfloat16 [4, 2, 256, 16384], P('pole', None, None, 'grid'), may hold values from -6 to 6
- pole_weights: float32 [4, 2], P('pole'), may hold values from -4 to 4
- hamiltonian: bfloat16 [1280, 16384], P(None, 'grid'), may hold values from -0.15625 to 0.15625
- margin: bfloat16 [1280, 16384], P(None, 'grid'), may hold values from -0.15625 to 0.15625
- dft_column: int32 [16384], replicated, may hold values from 0 to 16383, as said below
Outputs:
- ainv_off: bfloat16 [4, 2, 1024, 16384], P('pole', None, None, 'grid')
- ainv_diag: bfloat16 [4, 2, 256, 16384], P('pole', None, None, 'grid')
- charges: float32 [16384], P('grid')
- band_energy: float32 [16384], P('grid')
Inputs may be any that keep to these rules, and one draw needn't show every extreme that they name: dft_column is a permutation of the 16384 columns. The 256 columns that one index of grid holds, columns g * 256 to (g + 1) * 256 - 1, land on exactly 32 indices of grid in the column order, exactly 8 on each.
All inputs are finite; a program needn't handle non-finite values. No bound on the sum of `fill_pattern` on one device may be relied on, other than what follows from the above.
Results may differ from a plain program's by a relative error of at most 0.0054.
Values may be sent and summed in bfloat16 or wider, within the bound.
No kernel may reach another device: no remote copies, remote signals or barrier semaphores. Data moves between devices by JAX's collectives and lax.ppermute only.
A program may use at most 64 MiB of HBM per device.

v0:
```python
import math

import jax
import jax.numpy as jnp
from jax import lax
from jax.sharding import PartitionSpec as P


def complex_rows(ainv_real, ainv_imag, stacked, local_cols):
    first_product = jnp.dot(ainv_real, stacked, preferred_element_type=jnp.float32)
    second_product = jnp.dot(ainv_imag, stacked, preferred_element_type=jnp.float32)
    real_part = first_product[:, :local_cols] - second_product[:, local_cols:]
    imag_part = first_product[:, local_cols:] + second_product[:, :local_cols]
    return (real_part, imag_part)


def contract(left_side, right_side):
    return jnp.einsum("mkb,mkc->kbc", left_side, right_side, preferred_element_type=jnp.float32)


def flatten_blocks(values):
    supernodes, block_size, block_cols = values.shape
    return values.transpose(1, 0, 2).reshape(block_size, supernodes * block_cols)


def body(
    ainv_anc,
    lower_panels,
    fill_pattern,
    diag_inverse,
    pole_weights,
    hamiltonian,
    margin,
    dft_column,
):
    ancestors = ainv_anc.shape[3]
    local_cols = lower_panels.shape[3]
    block_size = diag_inverse.shape[2]
    per_device = local_cols // block_size
    groups = lax.axis_size("grid")
    capacity = 2 * local_cols // groups
    mask_low = jnp.repeat(
        jnp.repeat(fill_pattern.T, block_size, axis=0), block_size, axis=1
    ).astype(jnp.bfloat16)
    lower = lower_panels[0] * mask_low[None]
    stacked = jnp.concatenate([lower[0], lower[1]], axis=1)
    row_piece = lax.all_gather(ainv_anc, "grid", axis=2, tiled=True)
    real_part, imag_part = complex_rows(row_piece[0, 0], row_piece[0, 1], stacked, local_cols)
    row_keep = mask_low.astype(jnp.float32)
    upper = (-jnp.stack([real_part, imag_part]) * row_keep[None]).astype(jnp.bfloat16)[None]
    lower_split = lower.reshape(2, ancestors, per_device, block_size)
    upper_split = upper[0].reshape(2, ancestors, per_device, block_size)
    real_diag = contract(lower_split[0], upper_split[0]) - contract(lower_split[1], upper_split[1])
    imag_diag = contract(lower_split[0], upper_split[1]) + contract(lower_split[1], upper_split[0])
    diag = diag_inverse[0].astype(jnp.float32) - jnp.stack(
        [flatten_blocks(real_diag), flatten_blocks(imag_diag)]
    )
    weight_real = pole_weights[0, 0]
    weight_imag = pole_weights[0, 1]
    upper_float = upper[0].astype(jnp.float32)
    own_rows = weight_real * diag[1] + weight_imag * diag[0]
    far_rows = weight_real * upper_float[1] + weight_imag * upper_float[0]
    density = jnp.concatenate([own_rows, far_rows], axis=0)
    position = lax.axis_index("grid")
    own_columns = lax.dynamic_slice_in_dim(dft_column, position * local_cols, local_cols, 0)
    target = own_columns // local_cols
    onehot = (target[:, None] == jnp.arange(groups, dtype=jnp.int32)[None, :]).astype(jnp.int32)
    slot_rank = jnp.sum((jnp.cumsum(onehot, axis=0) - 1) * onehot, axis=1)
    send_slot = target * capacity + slot_rank
    slot_match = (
        send_slot[:, None] == jnp.arange(groups * capacity, dtype=jnp.int32)[None, :]
    ).astype(jnp.int32)
    local_index = jnp.arange(local_cols, dtype=jnp.int32)
    filled = jnp.sum(slot_match, axis=0)
    send_source = jnp.sum(slot_match * local_index[:, None], axis=0) + (1 - filled) * local_cols
    everyone = dft_column.reshape(groups, local_cols)
    arriving = (everyone // local_cols == position).astype(jnp.int32)
    arrive_rank = jnp.cumsum(arriving, axis=1) - 1
    source_slot = jnp.arange(groups, dtype=jnp.int32)[:, None] * capacity + arrive_rank
    place_index = jnp.where(arriving > 0, everyone % local_cols, local_cols)
    steps_count = math.gcd(groups, 8)
    place_blocks = place_index.reshape(steps_count, groups // steps_count, local_cols)
    slot_blocks = source_slot.reshape(steps_count, groups // steps_count, local_cols)

    def add_slots(total, pieces):
        place_piece, slot_piece = pieces
        match = (place_piece[:, :, None] == local_index[None, None, :]).astype(jnp.int32)
        return (total + jnp.sum(match * slot_piece[:, :, None], axis=(0, 1)), None)

    slot_of_local, unused = lax.scan(
        add_slots, jnp.zeros((local_cols,), jnp.int32), (place_blocks, slot_blocks)
    )
    density_part = lax.psum(density, "pole")
    row_count = density_part.shape[0]
    column_major = jnp.concatenate([density_part.T, jnp.zeros((1, row_count), jnp.float32)], axis=0)
    outgoing = column_major[send_source]
    arrived = lax.all_to_all(outgoing, "grid", split_axis=0, concat_axis=0, tiled=True)
    placed = arrived[slot_of_local].T
    charges = jnp.sum(placed * margin.astype(jnp.float32), axis=0)
    band_energy = jnp.sum(placed * hamiltonian.astype(jnp.float32), axis=0)
    return (upper, diag.astype(jnp.bfloat16)[None], charges, band_energy)


def solution(mesh):
    return jax.shard_map(
        body,
        mesh=mesh,
        in_specs=(
            P("pole", None, "grid", None),
            P("pole", None, None, "grid"),
            P("grid", None),
            P("pole", None, None, "grid"),
            P("pole", None),
            P(None, "grid"),
            P(None, "grid"),
            P(),
        ),
        out_specs=(
            P("pole", None, None, "grid"),
            P("pole", None, None, "grid"),
            P("grid"),
            P("grid"),
        ),
        check_vma=False,
    )
```

profile of v0, /device:TPU:1, one launch (start us, length us, event | category | flops | bytes accessed | tf_op | source)
XLA Modules:
  0.0 290.0 jit_solution(17733642843153408906)
XLA Ops:
  7.2 0.7 all-gather.2.cloned.1.call-update
  8.7 1.1 copy.36
  9.8 1.5 reshape.228
  11.3 0.8 fusion.39
  12.9 0.9 fusion.33
  14.6 1.3 fusion.38
  16.0 1.4 bitcast_multiply_fusion.2
  17.4 1.0 slice_bitcast_fusion.11
  18.4 120.7 %all-gather.2.cloned.1.call-done = bf16[1,2,1024,1024]{3,2,1,0:T(8,128)(2,1)} async-done(((bf16[1,2,16,1024]{3,2,1,0:T(8,128)(2,1)}), bf16[1,2,1024,1024]{3,2,1,0:T(8,128)(2,1)}) %all-gather.2.cloned.1.call-update) | async-done | bytes 4194320 | tf_op jit(solution)/shard_map/all_gather | solution.py:47
  139.1 3.4 %fusion.8 = f32[1024,512]{0,1:T(8,128)S(1)} fusion(bf16[1,2,1024,1024]{3,2,1,0:T(8,128)(2,1)} %all-gather.2.cloned.1.call-done, bf16[1024,256]{1,0:T(8,128)(2,1)} %get-tuple-element.82, bf16[1024,256]{1,0:T(8,128)(2,1)} %get-tuple-element.81), kind=kOutput, calls=%fused_computation.18 | convolution fusion | flops 1075838976 | bytes 5242880 | tf_op jit(solution)/shard_map/dot_general | solution.py:10
  142.6 1.3 fusion.9
  143.9 1.9 fusion.18
  147.4 1.4 fusion.23
  148.8 1.5 fusion.13
  150.3 1.2 maximum_bitcast_fusion
  151.7 0.7 sub.71
  152.6 1.1 copy.48
  153.7 0.8 and_select_fusion
  154.6 0.8 multiply_add_fusion.1
  155.6 46.1 %all-reduce.3.cloned.1.call-done = f32[256,1280]{1,0:T(8,128)} async-done(((f32[256,1280]{1,0:T(8,128)}), f32[256,1280]{1,0:T(8,128)}) %all-reduce.3.cloned.1.call-update) | async-done | bytes 1310736 | tf_op jit(solution)/shard_map/psum | solution.py:93
  201.7 1.4 concatenate.19
  203.1 2.9 %gather_fusion = f32[512,1280]{1,0:T(8,128)} fusion(f32[257,1280]{1,0:T(8,128)S(1)} %concatenate.19, s32[1024]{0:T(1024)S(1)} %pad_clamp_fusion.1), kind=kCustom, calls=%fused_computation | custom fusion | bytes 5244928 | tf_op jit(solution)/shard_map/gather | solution.py:96
  206.0 12.3 %all-to-all-start = ((f32[64,8,1280]{2,1,0:T(8,128)}), f32[64,8,1280]{2,1,0:T(8,128)S(1)}, u32[]{:S(2)}, u32[]{:S(2)}) async-start(f32[64,8,1280]{2,1,0:T(8,128)} %bitcast.97), calls=%async_computation | async-start | bytes 5242880 | tf_op jit(solution)/shard_map/all_to_all | solution.py:97
  218.3 1.6 fusion.25
  219.9 11.6 %while.11 = (s32[]{:T(128)}, s32[256]{0:T(256)S(1)}, s32[8,8,256]{2,1,0:T(8,128)}, s32[8,8,256]{2,1,0:T(8,128)}, s32[]{:T(128)}, /*index=5*/s32[]{:T(128)}) while((s32[]{:T(128)}, s32[256]{0:T(256)S(1)}, s32[8,8,256]{2,1,0:T(8,128)}, s32[8,8,256]{2,1,0:T(8,128)}, s32[]{:T(128)}, /*index=5*/s32[]{:T(128)}) %tuple.41), condition=%wide.region_10.11_spmd.clone, body=%wide.region_8.10_spmd.clone.sunk | while | flops 1573123 | bytes 53331 | solution.py:90
  219.9 0.7 dynamic-slice_bitcast_fusion.3
  220.6 0.7 select_reduce_fusion.3
  221.4 0.7 dynamic-slice_bitcast_fusion.3
  222.1 0.7 select_reduce_fusion.3
  222.8 0.7 dynamic-slice_bitcast_fusion.3
  223.5 0.7 select_reduce_fusion.3
  224.3 0.7 dynamic-slice_bitcast_fusion.3
  225.0 0.7 select_reduce_fusion.3
  225.7 0.7 dynamic-slice_bitcast_fusion.3
  226.5 0.7 select_reduce_fusion.3
  227.2 0.7 dynamic-slice_bitcast_fusion.3
  227.9 0.7 select_reduce_fusion.3
  228.6 0.7 dynamic-slice_bitcast_fusion.3
  229.4 0.7 select_reduce_fusion.3
  230.1 0.7 dynamic-slice_bitcast_fusion.3
  230.8 0.7 select_reduce_fusion.3
  231.6 1.8 fusion.14
  233.4 1.8 copy.50
  235.2 2.8 fusion.5
  237.9 2.3 copy.49
  240.2 38.3 %all-to-all-done = f32[64,8,1280]{2,1,0:T(8,128)S(1)} async-done(((f32[64,8,1280]{2,1,0:T(8,128)}), f32[64,8,1280]{2,1,0:T(8,128)S(1)}, u32[]{:S(2)}, u32[]{:S(2)}) %all-to-all-start) | async-done | bytes 2621472 | tf_op jit(solution)/shard_map/all_to_all | solution.py:97
  278.5 2.2 gather_fusion.1
  280.7 2.4 fusion.11
  (66 shorter events, 5.0 us)
Async XLA Ops:
  7.2 131.9 %all-gather.2.cloned.1.call-start = ((), (), s32[]{:S(2)}) async-start(), calls=%async_computation.1 | async-start | bytes 4259840 | tf_op jit(solution)/shard_map/all_gather | solution.py:47
  7.9 193.8 %all-reduce.3.cloned.1.call-start = ((), (), s32[]{:S(2)}) async-start(), calls=%async_computation.2 | async-start | bytes 2621440 | tf_op jit(solution)/shard_map/psum | solution.py:93
  12.7 2.0 copy-start.4
  12.9 5.5 %copy-start.8 = (s32[64,3]{0,1:T(4,128)}, s32[64,3]{0,1:T(4,128)S(1)}, u32[]{:S(2)}) copy-start(s32[64,3]{0,1:T(4,128)S(1)} %reduce-window.15) | copy-start | bytes 2308
  14.6 3.8 %copy-start.9 = (s32[64,3]{0,1:T(4,128)}, s32[64,3]{0,1:T(4,128)S(1)}, u32[]{:S(2)}) copy-start(s32[64,3]{0,1:T(4,128)S(1)} %reduce-window.19) | copy-start | bytes 2308
  139.1 3.4 %copy-start.6 = (bf16[1024,256]{1,0:T(8,128)(2,1)S(1)}, bf16[1024,256]{1,0:T(8,128)(2,1)}, u32[]{:S(2)}) copy-start(bf16[1024,256]{1,0:T(8,128)(2,1)} %get-tuple-element.81) | copy-start | bytes 1572868
  139.1 3.4 %copy-start.7 = (bf16[1024,256]{1,0:T(8,128)(2,1)S(1)}, bf16[1024,256]{1,0:T(8,128)(2,1)}, u32[]{:S(2)}) copy-start(bf16[1024,256]{1,0:T(8,128)(2,1)} %get-tuple-element.82) | copy-start | bytes 1572868
  139.1 3.5 %copy-start.10 = (bf16[1,2,1024,1024]{3,2,1,0:T(8,128)(2,1)S(1)}, bf16[1,2,1024,1024]{3,2,1,0:T(8,128)(2,1)}, u32[]{:S(2)}) copy-start(bf16[1,2,1024,1024]{3,2,1,0:T(8,128)(2,1)} %all-gather.2.cloned.1.call-done) | copy-start | bytes 12582916
  147.0 3.2 %copy-start = (f32[256,256]{0,1:T(8,128)}, f32[256,256]{0,1:T(8,128)S(1)}, u32[]{:S(2)}) copy-start(f32[256,256]{0,1:T(8,128)S(1)} %convolution_subtract_fusion) | copy-start | bytes 786436
  147.4 2.9 %copy-start.1 = (f32[256,256]{0,1:T(8,128)}, f32[256,256]{0,1:T(8,128)S(1)}, u32[]{:S(2)}) copy-start(f32[256,256]{0,1:T(8,128)S(1)} %convolution_add_fusion) | copy-start | bytes 786436
  150.3 1.2 slice-start.1
  150.3 2.1 copy-start.2
  151.5 1.1 copy-start.3
  151.5 3.0 %copy-start.5 = (s32[64,2,128]{2,0,1:T(8,128)S(1)}, s32[64,2,128]{2,0,1:T(8,128)}, u32[]{:S(2)}) copy-start(s32[64,2,128]{2,0,1:T(8,128)} %copy-done.4) | copy-start | bytes 196612
  151.5 3.0 %slice-start = ((s32[64,3]{0,1:T(4,128)}), s32[64,2]{0,1:T(2,128)S(1)}, s32[]{:S(2)}) async-start(s32[64,3]{0,1:T(4,128)} %copy-done.8), calls=%async_computation.3 | async-start | bytes 2048 | tf_op jit(solution)/shard_map/slice.1
  206.0 72.5 %all-to-all-start = ((f32[64,8,1280]{2,1,0:T(8,128)}), f32[64,8,1280]{2,1,0:T(8,128)S(1)}, u32[]{:S(2)}, u32[]{:S(2)}) async-start(f32[64,8,1280]{2,1,0:T(8,128)} %bitcast.97), calls=%async_computation | async-start | bytes 5242880 | tf_op jit(solution)/shard_map/all_to_all | solution.py:97
Sparse Core Ops, SparseCore 0:
  11.5 127.5 all-gather.1
  151.7 49.9 all-reduce.2
where the time goes:
time: 294 us; the launch traced here: 290 us
  waiting for transfers between devices  206 us (70%)
  other arithmetic  27.5 us (9%)
  local copies, waits for them, and re-layouts  23.9 us (8%)
  between operations  14.3 us (5%)
  starting transfers between devices  12.4 us (4%)
  matrix products  5.85 us (2%)
    all_gather x1, waiting for transfers between devices, body(): row_piece = lax.all_gather(ainv_anc, 'grid', axis=2, tiled=True)  121 us
    psum x1, waiting for transfers between devices, body(): density_part = lax.psum(density, 'pole')  46.1 us
    all_to_all x1, waiting for transfers between devices, body(): lax.all_to_all(outgoing, 'grid', split_axis=0, concat_axis=0, tiled=True)  38.3 us
    all_to_all x1, starting transfers between devices, body(): lax.all_to_all(outgoing, 'grid', split_axis=0, concat_axis=0, tiled=True)  12.3 us
    unnamed x29, local copies, waits for them, and re-layouts  6.66 us
  transfers between devices with their start and end apart: 3, of which 3 were waited for; matrix products, arithmetic and copies ran while one was open for 12% of the time, Pallas kernels for 0%

commit v1 on v0

v1 whole, which is shorter than its diff:
```python
import functools

import jax
import jax.numpy as jnp
from jax import lax
from jax.experimental import pallas as pl
from jax.experimental.pallas import tpu as pltpu
from jax.sharding import PartitionSpec as P

F32 = jnp.float32
BF16 = jnp.bfloat16
I32 = jnp.int32
NX, NY, NZ = 4, 2, 8
GROUPS = NX * NY * NZ
POLES = 4
CAP = 8
SLOTS = GROUPS * CAP
COLS = 256
ANC = 1024
ROWS = 1280
QUARTER = ROWS // POLES
SHARD = ANC // GROUPS
VMEM_LIMIT = 50 * 1024 * 1024
SMEM_SPEC = pl.BlockSpec(memory_space=pltpu.SMEM)
VMEM_SPEC = pl.BlockSpec(memory_space=pltpu.VMEM)


def params():
    return pltpu.CompilerParams(vmem_limit_bytes=VMEM_LIMIT)


def mm(a, b, contract=((1,), (0,))):
    return lax.dot_general(a, b, (contract, ((), ())), preferred_element_type=F32)


def iota(shape, dim):
    return lax.broadcasted_iota(I32, shape, dim)


def flag(condition):
    return jnp.where(condition, 1.0, 0.0).astype(BF16)


def split_matmul(values, onehot, contract):
    high = values.astype(BF16)
    rest = values - high.astype(F32)
    middle = rest.astype(BF16)
    low = (rest - middle.astype(F32)).astype(BF16)
    return mm(high, onehot, contract) + mm(middle, onehot, contract) + mm(low, onehot, contract)


def pack_kernel(index, dft, margin, hamiltonian, out, slot_onehot):
    entries = dft[...]
    side = entries.shape[0]
    hit = (entries >> 8) == index[1]
    row, col = iota((side, side), 0), iota((side, side), 1)
    hit_flag = flag(hit)
    rank = mm(hit_flag, flag(row < col))
    previous = mm(flag(((row & 1) == 1) & (col == row - 1)), hit_flag).astype(BF16)
    rank = rank + mm(previous, jnp.ones((side, side), BF16))
    place = ((entries & 255) + 1).astype(F32)
    pair = flag((iota((GROUPS, side), 1) >> 1) == iota((GROUPS, side), 0))
    target = (iota((GROUPS, COLS), 1) + 1).astype(F32)
    pieces = []
    for r in range(CAP):
        picked = jnp.where(hit & (rank == float(r)), place, 0.0).astype(BF16)
        local = jnp.sum(mm(pair, picked), axis=1, keepdims=True)
        pieces.append(flag(local == target))
    by_rank = jnp.concatenate(pieces, axis=0)
    s, t = iota((SLOTS, SLOTS), 0), iota((SLOTS, SLOTS), 1)
    order = flag((s & (CAP - 1)) * GROUPS + (s >> 3) == t)
    onehot = mm(order, by_rank).astype(BF16)
    slot_onehot[...] = onehot
    both = jnp.concatenate([margin[...], hamiltonian[...]], axis=0)
    out[...] = mm(onehot, both, ((1,), (1,))).astype(BF16)


def pack(index, dft, margin, hamiltonian):
    quarter = pl.BlockSpec((QUARTER, COLS), lambda i, index: (index[0], 0))
    whole = lambda *shape: pl.BlockSpec(shape, lambda i, index: (0,) * len(shape))
    return pl.pallas_call(
        pack_kernel,
        grid_spec=pltpu.PrefetchScalarGridSpec(
            num_scalar_prefetch=1,
            grid=(1,),
            in_specs=[whole(*dft.shape), quarter, quarter],
            out_specs=[whole(SLOTS, 2 * QUARTER), whole(SLOTS, COLS)],
        ),
        out_shape=[
            jax.ShapeDtypeStruct((SLOTS, 2 * QUARTER), BF16),
            jax.ShapeDtypeStruct((SLOTS, COLS), BF16),
        ],
        compiler_params=params(),
        name="pack",
    )(index, dft, margin, hamiltonian)


def unpack_kernel(own_col, own_row, arrived, out, column_onehot):
    group_col, group_row = own_col[...] >> 8, own_row[...] >> 8
    before = iota((COLS, COLS), 0) < iota((COLS, COLS), 1)
    rank = jnp.sum(jnp.where((group_col == group_row) & before, 1, 0), axis=0, keepdims=True)
    slot = group_row * CAP + rank
    onehot = flag(iota((SLOTS, COLS), 0) == slot)
    column_onehot[...] = onehot
    out[...] = mm(arrived[...], onehot, ((0,), (0,))).astype(BF16)


def unpack(own_col, own_row, arrived):
    return pl.pallas_call(
        unpack_kernel,
        in_specs=[VMEM_SPEC] * 3,
        out_specs=[VMEM_SPEC] * 2,
        out_shape=[
            jax.ShapeDtypeStruct((2 * QUARTER, COLS), BF16),
            jax.ShapeDtypeStruct((SLOTS, COLS), BF16),
        ],
        compiler_params=params(),
        name="unpack",
    )(own_col, own_row, arrived)


def factor_kernel(index, weights, fill, lower, diag_inverse, own, mate, others, out, base, rows, masked):
    pole = index[0]
    for part in range(2):
        for block in range(ANC // COLS):
            keep = fill[0, block].astype(F32).astype(BF16)
            span = slice(block * COLS, (block + 1) * COLS)
            masked[part, span, :] = lower[part, span, :] * keep
    pieces = [own[...], mate[...], others[0], others[1]]
    for shift, piece in enumerate(pieces):
        start = pl.multiple_of((pole ^ shift) * QUARTER, QUARTER)
        for which in range(2):
            rows[which, pl.ds(start, QUARTER), :] = piece[which * QUARTER : (which + 1) * QUARTER, :]
    real, imag = weights[0, 0], weights[0, 1]
    for which in range(2):
        near = rows[which, 0:COLS, :]
        near_float = near.astype(F32)
        sums = real * diag_inverse[1].astype(F32) + imag * diag_inverse[0].astype(F32)
        base[which : which + 1, :] = jnp.sum(sums * near_float, axis=0, keepdims=True)
        for block in range(ANC // COLS):
            span = slice(block * COLS, (block + 1) * COLS)
            far = rows[which, (block + 1) * COLS : (block + 2) * COLS, :].astype(F32)
            direct = far - mm(masked[0, span, :], near)
            cross = mm(masked[1, span, :], near)
            out[2 * which, span, :] = imag * direct - real * cross
            out[2 * which + 1, span, :] = real * direct + imag * cross
    base[2:8, :] = jnp.zeros((6, COLS), F32)


def factors(index, weights, fill, lower, diag_inverse, own, mate, others):
    return pl.pallas_call(
        factor_kernel,
        in_specs=[SMEM_SPEC] * 3 + [VMEM_SPEC] * 5,
        out_specs=[VMEM_SPEC] * 2,
        out_shape=[
            jax.ShapeDtypeStruct((4, ANC, COLS), F32),
            jax.ShapeDtypeStruct((8, COLS), F32),
        ],
        scratch_shapes=[pltpu.VMEM((2, ROWS, COLS), BF16), pltpu.VMEM((2, ANC, COLS), BF16)],
        compiler_params=params(),
        name="factors",
    )(index, weights, fill, lower, diag_inverse, own, mate, others)


def upper_kernel(index, fill, lower, first, first_y, second, s1, s2, s3, factor, base, onehot, out, slots, both):
    grid = index[1]
    x, y, z = grid >> 4, (grid >> 3) & 1, grid & 7
    for block in range(ANC // COLS):
        keep = fill[0, block].astype(F32).astype(BF16)
        span = slice(block * COLS, (block + 1) * COLS)
        for part in range(2):
            both[span, part * COLS : (part + 1) * COLS] = lower[part, span, :] * keep
    rhs = both[...]

    def store(pair, places):
        left = mm(pair[0], rhs)
        right = mm(pair[1], rhs)
        real = right[:, COLS:] - left[:, :COLS]
        imag = -left[:, COLS:] - right[:, :COLS]
        for n, (px, py, pz) in enumerate(places):
            keep = fill[0, px].astype(F32)
            start = pl.multiple_of(px * (NY * NZ * SHARD) + py * (NZ * SHARD) + pz * SHARD, SHARD)
            span = slice(n * SHARD, (n + 1) * SHARD)
            out[0, pl.ds(start, SHARD), :] = (real[span] * keep).astype(BF16)
            out[1, pl.ds(start, SHARD), :] = (imag[span] * keep).astype(BF16)

    half = NZ // 2
    for dy, ref in ((0, first), (1, first_y)):
        pair = [ref[:, part].reshape(NX * half * SHARD, ANC) for part in range(2)]
        store(pair, [((x - dx) & 3, (y - dy) & 1, (z - k) & 7) for dx in range(NX) for k in range(half)])
    for dx, ref in enumerate((second, s1, s2, s3)):
        pair = [ref[:, part].reshape(NY * half * SHARD, ANC) for part in range(2)]
        store(pair, [((x - dx) & 3, (y - dy) & 1, (z - k) & 7) for dy in range(NY) for k in range(half, NZ)])
    rows = [base[which : which + 1, :] for which in range(2)]
    for block in range(ANC // COLS):
        span = slice(block * COLS, (block + 1) * COLS)
        real, imag = out[0, span, :].astype(F32), out[1, span, :].astype(F32)
        for which in range(2):
            term = real * factor[2 * which, span, :] + imag * factor[2 * which + 1, span, :]
            rows[which] = rows[which] + jnp.sum(term, axis=0, keepdims=True)
    values = jnp.concatenate(rows + [jnp.zeros((6, COLS), F32)], axis=0)
    slots[...] = split_matmul(values, onehot[...], ((1,), (1,)))


def upper_rows(index, fill, lower, pieces, factor, base, onehot):
    return pl.pallas_call(
        upper_kernel,
        in_specs=[SMEM_SPEC] * 2 + [VMEM_SPEC] * (4 + len(pieces)),
        out_specs=[VMEM_SPEC] * 2,
        out_shape=[
            jax.ShapeDtypeStruct((2, ANC, COLS), BF16),
            jax.ShapeDtypeStruct((8, SLOTS), F32),
        ],
        scratch_shapes=[pltpu.VMEM((ANC, 2 * COLS), BF16)],
        compiler_params=params(),
        name="upper",
    )(index, fill, lower, *pieces, factor, base, onehot)


def diag_kernel(fill, lower, upper, diag_inverse, out):
    real = diag_inverse[0].astype(F32)
    imag = diag_inverse[1].astype(F32)
    turn = ((0,), (0,))
    for block in range(ANC // COLS):
        keep = fill[0, block].astype(F32).astype(BF16)
        span = slice(block * COLS, (block + 1) * COLS)
        low_real, low_imag = lower[0, span, :] * keep, lower[1, span, :] * keep
        up_real, up_imag = upper[0, span, :], upper[1, span, :]
        real = real - mm(low_real, up_real, turn) + mm(low_imag, up_imag, turn)
        imag = imag - mm(low_real, up_imag, turn) - mm(low_imag, up_real, turn)
    out[0] = real.astype(BF16)
    out[1] = imag.astype(BF16)


def diag_block(fill, lower, upper, diag_inverse):
    return pl.pallas_call(
        diag_kernel,
        in_specs=[SMEM_SPEC] + [VMEM_SPEC] * 3,
        out_specs=VMEM_SPEC,
        out_shape=jax.ShapeDtypeStruct((2, COLS, COLS), BF16),
        compiler_params=params(),
        name="diag",
    )(fill, lower, upper, diag_inverse)


def place_kernel(slots, onehot, out):
    out[...] = split_matmul(slots[...], onehot[...], ((1,), (0,)))


def place(slots, onehot):
    return pl.pallas_call(
        place_kernel,
        in_specs=[VMEM_SPEC] * 2,
        out_specs=VMEM_SPEC,
        out_shape=jax.ShapeDtypeStruct((2, COLS), F32),
        compiler_params=params(),
        name="place",
    )(slots, onehot)


def position(x, y, z):
    return ((x % NX) * NY + y % NY) * NZ + z % NZ


def shift(value, dx=0, dy=0, dz=0):
    pairs = [
        (position(x, y, z), position(x + dx, y + dy, z + dz))
        for x in range(NX)
        for y in range(NY)
        for z in range(NZ)
    ]
    return lax.ppermute(value, "grid", pairs)


def swap_pole(value, bit):
    return lax.ppermute(value, "pole", [(p, p ^ bit) for p in range(POLES)])


def body(ainv_anc, lower_panels, fill_pattern, diag_inverse, pole_weights, hamiltonian, margin, dft_column):
    index = jnp.stack([lax.axis_index("pole"), lax.axis_index("grid")]).astype(I32)
    lower, inverse = lower_panels[0], diag_inverse[0]
    shard = ainv_anc[0]

    along = [shard] + [shift(shard, dz=k) for k in range(1, NZ)]
    first = jnp.concatenate(along[: NZ // 2], axis=1)
    second = jnp.concatenate(along[NZ // 2 :], axis=1)
    first = jnp.stack([first] + [shift(first, dx=d) for d in range(1, NX)])
    second = jnp.stack([second, shift(second, dy=1)])
    first_y = shift(first, dy=1)
    others = [shift(second, dx=d) for d in range(1, NX)]

    table = dft_column.reshape(128, 128)
    packed, slot_onehot = pack(index, table, margin, hamiltonian)
    arrived = lax.all_to_all(packed, "grid", split_axis=0, concat_axis=0, tiled=True)
    own = lax.dynamic_slice_in_dim(table, 2 * index[1], 2, 0)
    mine, column_onehot = unpack(own.reshape(COLS, 1), own.reshape(1, COLS), arrived)
    mate = swap_pole(mine, 1)
    far = swap_pole(jnp.stack([mine, mate]), 2)
    factor, base = factors(index, pole_weights, fill_pattern, lower, inverse, mine, mate, far)

    upper, slots = upper_rows(
        index, fill_pattern, lower, [first, first_y, second] + others, factor, base, column_onehot
    )
    diag = diag_block(fill_pattern, lower, upper, inverse)
    total = lax.psum(slots[:2], "pole")
    outgoing = total.reshape(2, GROUPS, CAP).transpose(1, 0, 2).reshape(GROUPS, 2 * CAP)
    incoming = lax.all_to_all(outgoing, "grid", split_axis=0, concat_axis=0, tiled=True)
    incoming = incoming.reshape(GROUPS, 2, CAP).transpose(1, 0, 2).reshape(2, SLOTS)
    placed = place(incoming, slot_onehot)
    return (upper[None], diag[None], placed[0], placed[1])


def solution(mesh):
    return jax.shard_map(
        body,
        mesh=mesh,
        in_specs=(
            P("pole", None, "grid", None),
            P("pole", None, None, "grid"),
            P("grid", None),
            P("pole", None, None, "grid"),
            P("pole", None),
            P(None, "grid"),
            P(None, "grid"),
            P(),
        ),
        out_specs=(
            P("pole", None, None, "grid"),
            P("pole", None, None, "grid"),
            P("grid"),
            P("grid"),
        ),
        check_vma=False,
    )
```

time: 294 us -> 163 us (0.55)
  waiting for transfers between devices: 206 us -> 49.6 us
  starting transfers between devices: 12.4 us -> 71.3 us
  other arithmetic: 27.5 us -> 4.06 us
  Pallas kernels: 0 us -> 15.6 us
  local copies, waits for them, and re-layouts: 23.9 us -> 9.6 us
  between operations: 14.3 us -> 0.79 us
  blocking collectives: 0 us -> 10.6 us
  matrix products: 5.85 us -> 0 us
    all_gather x1 -> x0, waiting for transfers between devices: 121 us -> none  [body(): row_piece = lax.all_gather(ainv_anc, 'grid', axis=2, tiled=True)]
    psum x1 -> x0, waiting for transfers between devices: 46.1 us -> none  [body(): density_part = lax.psum(density, 'pole')]
    ppermute x0 -> x17, waiting for transfers between devices: none -> 42.2 us  [the longest x15 37.3 us: shift(): return lax.ppermute(value, 'grid', pairs)]
    ppermute x0 -> x17, starting transfers between devices: none -> 38 us  [the longest x15 32.5 us: shift(): return lax.ppermute(value, 'grid', pairs)]
    all_to_all x1, waiting for transfers between devices: 38.3 us -> 7.46 us  [body(): lax.all_to_all(outgoing, 'grid', split_axis=0, concat_axis=0, tiled=True)]
    pallas_call x0 -> x6, Pallas kernels: none -> 15.6 us  [the longest x1 6.76 us: upper_rows(): pl.pallas_call(upper_kernel, in_specs=[SMEM_SPEC] * 2 + [VMEM_SPEC] * (4...]
    all_to_all x0 -> x1, starting transfers between devices: none -> 15.3 us  [body(): lax.all_to_all(packed, 'grid', split_axis=0, concat_axis=0, tiled=True)]
    psum x0 -> x1, blocking collectives: none -> 10.6 us  [body(): total = lax.psum(slots[:2], 'pole')]
  transfers between devices with their start and end apart: 3 -> 19, of which waited for: 3 -> 9; matrix products, arithmetic and copies ran while one was open for 12% -> 4% of each run, Pallas kernels for 0% -> 4%
where the time goes in v1:
time: 163 us; the launch traced here: 162 us
  starting transfers between devices  71.3 us (44%)
  waiting for transfers between devices  49.6 us (30%)
  Pallas kernels  15.6 us (10%)
  blocking collectives  10.6 us (7%)
  local copies, waits for them, and re-layouts  9.6 us (6%)
  other arithmetic  4.06 us (2%)
    ppermute x15, waiting for transfers between devices, shift(): return lax.ppermute(value, 'grid', pairs)  37.3 us
    ppermute x15, starting transfers between devices, shift(): return lax.ppermute(value, 'grid', pairs)  32.5 us
    all_to_all x1, starting transfers between devices, body(): lax.all_to_all(outgoing, 'grid', split_axis=0, concat_axis=0, tiled=True)  18 us
    all_to_all x1, starting transfers between devices, body(): lax.all_to_all(packed, 'grid', split_axis=0, concat_axis=0, tiled=True)  15.3 us
    psum x1, blocking collectives, body(): total = lax.psum(slots[:2], 'pole')  10.6 us
    all_to_all x1, waiting for transfers between devices, body(): lax.all_to_all(outgoing, 'grid', split_axis=0, concat_axis=0, tiled=True)  7.46 us
    pallas_call x1, Pallas kernels, upper_rows(): pl.pallas_call(upper_kernel, in_specs=[SMEM_SPEC] * 2 + [VMEM_SPEC] * (4...  6.76 us
    unnamed x27, local copies, waits for them, and re-layouts  6.44 us
  transfers between devices with their start and end apart: 19, of which 9 were waited for; matrix products, arithmetic and copies ran while one was open for 4% of the time, Pallas kernels for 4%

profile of v1, /device:TPU:1, one launch (start us, length us, event | category | flops | bytes accessed | tf_op | source)
XLA Modules:
  0.0 161.5 jit_solution(1141708527069238188)
XLA Ops:
  0.7 1.1 copy-done.3
  1.8 1.1 copy-done.4
  2.9 0.8 copy-done.5
  3.7 2.6 %pack.1 = (bf16[512,640]{1,0:T(8,128)(2,1)}, bf16[512,256]{1,0:T(8,128)(2,1)S(1)}) custom-call(s32[2]{0:T(128)S(1)} %pad_add_fusion.index, s32[128,128]{1,0:T(8,128)S(1)} %bitcast.38, bf16[1280,256]{1,0:T(8,128)(2,1)S(1)} %copy-done.3, bf16[1280,256]{1,0:T(8,128)(2,1)S(1)} %copy-done.4), custom_call_target="tpu_custom_call" | custom-call | tf_op jit(solution)/shard_map/pack/pallas_call | solution.py:81
  6.3 15.3 %all-to-all-start = ((bf16[64,8,640]{2,1,0:T(8,128)(2,1)}), bf16[64,8,640]{2,1,0:T(8,128)(2,1)S(1)}, u32[]{:S(2)}, u32[]{:S(2)}) async-start(bf16[64,8,640]{2,1,0:T(8,128)(2,1)} %bitcast.14), calls=%async_computation | async-start | bytes 1310720 | tf_op jit(solution)/shard_map/all_to_all | solution.py:294
  21.6 1.1 collective-permute-start
  22.7 2.1 %collective-permute-start.1 = (bf16[2,16,1024]{2,1,0:T(8,128)(2,1)}, bf16[2,16,1024]{2,1,0:T(8,128)(2,1)S(1)}, u32[]{:S(2)}, u32[]{:S(2)}) collective-permute-start(bf16[2,16,1024]{2,1,0:T(8,128)(2,1)} %bitcast.48), channel_id=1, source_target_pairs={{0,2},{1,3},{2,4},{3,5},{4,6},{5,7},{6,0},{7,1},{8,10},{9,11},{10,... | collective-permute-start | bytes 196616 | tf_op jit(solution)/shard_map/ppermute | solution.py:272
  24.8 2.4 %collective-permute-start.2 = (bf16[2,16,1024]{2,1,0:T(8,128)(2,1)}, bf16[2,16,1024]{2,1,0:T(8,128)(2,1)S(1)}, u32[]{:S(2)}, u32[]{:S(2)}) collective-permute-start(bf16[2,16,1024]{2,1,0:T(8,128)(2,1)} %bitcast.49), channel_id=1, source_target_pairs={{0,3},{1,4},{2,5},{3,6},{4,7},{5,0},{6,1},{7,2},{8,11},{9,12},{10,... | collective-permute-start | bytes 196616 | tf_op jit(solution)/shard_map/ppermute | solution.py:272
  27.2 2.1 %collective-permute-start.7 = (bf16[2,16,1024]{2,1,0:T(8,128)(2,1)}, bf16[2,16,1024]{2,1,0:T(8,128)(2,1)S(1)}, u32[]{:S(2)}, u32[]{:S(2)}) collective-permute-start(bf16[2,16,1024]{2,1,0:T(8,128)(2,1)} %bitcast.50), channel_id=1, source_target_pairs={{0,4},{1,5},{2,6},{3,7},{4,0},{5,1},{6,2},{7,3},{8,12},{9,13},{10,... | collective-permute-start | bytes 196616 | tf_op jit(solution)/shard_map/ppermute | solution.py:272
  29.3 2.4 %collective-permute-start.8 = (bf16[2,16,1024]{2,1,0:T(8,128)(2,1)}, bf16[2,16,1024]{2,1,0:T(8,128)(2,1)S(1)}, u32[]{:S(2)}, u32[]{:S(2)}) collective-permute-start(bf16[2,16,1024]{2,1,0:T(8,128)(2,1)} %bitcast.51), channel_id=1, source_target_pairs={{0,5},{1,6},{2,7},{3,0},{4,1},{5,2},{6,3},{7,4},{8,13},{9,14},{10,... | collective-permute-start | bytes 196616 | tf_op jit(solution)/shard_map/ppermute | solution.py:272
  31.7 6.3 %collective-permute-done = bf16[2,16,1024]{2,1,0:T(8,128)(2,1)S(1)} collective-permute-done((bf16[2,16,1024]{2,1,0:T(8,128)(2,1)}, bf16[2,16,1024]{2,1,0:T(8,128)(2,1)S(1)}, u32[]{:S(2)}, u32[]{:S(2)}) %collective-permute-start) | collective-permute-done | bytes 65568 | tf_op jit(solution)/shard_map/ppermute | solution.py:272
  38.0 3.9 %collective-permute-done.1 = bf16[2,16,1024]{2,1,0:T(8,128)(2,1)S(1)} collective-permute-done((bf16[2,16,1024]{2,1,0:T(8,128)(2,1)}, bf16[2,16,1024]{2,1,0:T(8,128)(2,1)S(1)}, u32[]{:S(2)}, u32[]{:S(2)}) %collective-permute-start.1) | collective-permute-done | bytes 65568 | tf_op jit(solution)/shard_map/ppermute | solution.py:272
  41.9 2.8 %collective-permute-done.2 = bf16[2,16,1024]{2,1,0:T(8,128)(2,1)S(1)} collective-permute-done((bf16[2,16,1024]{2,1,0:T(8,128)(2,1)}, bf16[2,16,1024]{2,1,0:T(8,128)(2,1)S(1)}, u32[]{:S(2)}, u32[]{:S(2)}) %collective-permute-start.2) | collective-permute-done | bytes 65568 | tf_op jit(solution)/shard_map/ppermute | solution.py:272
  44.7 1.6 fusion
  46.3 1.2 collective-permute-start.3
  47.5 2.4 %collective-permute-start.4 = (bf16[2,64,1024]{2,1,0:T(8,128)(2,1)S(1)}, bf16[2,64,1024]{2,1,0:T(8,128)(2,1)S(1)}, u32[]{:S(2)}, u32[]{:S(2)}) collective-permute-start(bf16[2,64,1024]{2,1,0:T(8,128)(2,1)S(1)} %get-tuple-element.21), channel_id=1, source_target_pairs={{0,32},{1,33},{2,34},{3,35},{4,36},{5,37},{6,38},{7,39},{8,40},{9,... | collective-permute-start | bytes 786440 | tf_op jit(solution)/shard_map/ppermute | solution.py:272
  50.0 1.0 collective-permute-start.5
  50.9 0.7 constant_dynamic-slice_fusion
  51.8 4.0 %collective-permute-start.9 = (bf16[2,16,1024]{2,1,0:T(8,128)(2,1)}, bf16[2,16,1024]{2,1,0:T(8,128)(2,1)}, u32[]{:S(2)}, u32[]{:S(2)}) collective-permute-start(bf16[2,16,1024]{2,1,0:T(8,128)(2,1)} %bitcast.53), channel_id=1, source_target_pairs={{0,6},{1,7},{2,0},{3,1},{4,2},{5,3},{6,4},{7,5},{8,14},{9,15},{10,... | collective-permute-start | bytes 196616 | tf_op jit(solution)/shard_map/ppermute | solution.py:272
  55.8 2.2 %collective-permute-start.10 = (bf16[2,16,1024]{2,1,0:T(8,128)(2,1)}, bf16[2,16,1024]{2,1,0:T(8,128)(2,1)S(1)}, u32[]{:S(2)}, u32[]{:S(2)}) collective-permute-start(bf16[2,16,1024]{2,1,0:T(8,128)(2,1)} %bitcast.54), channel_id=1, source_target_pairs={{0,7},{1,0},{2,1},{3,2},{4,3},{5,4},{6,5},{7,6},{8,15},{9,8},{10,9... | collective-permute-start | bytes 196616 | tf_op jit(solution)/shard_map/ppermute | solution.py:272
  58.0 0.2 collective-permute-done.4
  58.2 0.5 copy-done.9
  58.9 1.3 pad_maximum_fusion.first
  60.2 2.8 %collective-permute-start.6 = (bf16[4,2,64,1024]{3,2,1,0:T(8,128)(2,1)S(1)}, bf16[4,2,64,1024]{3,2,1,0:T(8,128)(2,1)}, u32[]{:S(2)}, u32[]{:S(2)}) collective-permute-start(bf16[4,2,64,1024]{3,2,1,0:T(8,128)(2,1)S(1)} %pad_maximum_fusion.first), channel_id=1, source_target_pairs={{0,8},{1,9},{2,10},{3,11},{4,12},{5,13},{6,14},{7,15},{8,0},{9,1},... | collective-permute-start | bytes 3145736 | tf_op jit(solution)/shard_map/ppermute | solution.py:272
  63.1 0.5 unpack.1
  63.5 4.9 %collective-permute-start.15 = (bf16[640,256]{1,0:T(8,128)(2,1)S(1)}, bf16[640,256]{1,0:T(8,128)(2,1)S(1)}, u32[]{:S(2)}, u32[]{:S(2)}) collective-permute-start(bf16[640,256]{1,0:T(8,128)(2,1)S(1)} %get-tuple-element.13.own), channel_id=1, source_target_pairs={{0,64},{64,0},{128,192},{192,128},{1,65},{65,1},{129,193},{193,129... | collective-permute-start | bytes 983048 | tf_op jit(solution)/shard_map/ppermute | solution.py:276
  68.4 1.5 constant_dynamic-update-slice_fusion.1
  69.9 0.6 constant_dynamic-update-slice_fusion
  70.6 0.4 collective-permute-start.11
  71.0 0.7 collective-permute-start.16
  71.7 15.8 %collective-permute-done.11 = bf16[2,64,1024]{2,1,0:T(8,128)(2,1)S(1)} collective-permute-done((bf16[2,64,1024]{2,1,0:T(8,128)(2,1)}, bf16[2,64,1024]{2,1,0:T(8,128)(2,1)S(1)}, u32[]{:S(2)}, u32[]{:S(2)}) %collective-permute-start.11) | collective-permute-done | bytes 262176 | tf_op jit(solution)/shard_map/ppermute | solution.py:272
  87.5 1.0 pad_maximum_fusion.2.second
  88.5 5.9 %collective-permute-start.12 = (bf16[2,2,64,1024]{3,2,1,0:T(8,128)(2,1)S(1)}, bf16[2,2,64,1024]{3,2,1,0:T(8,128)(2,1)S(1)}, u32[]{:S(2)}, u32[]{:S(2)}) collective-permute-start(bf16[2,2,64,1024]{3,2,1,0:T(8,128)(2,1)S(1)} %pad_maximum_fusion.2.second), channel_id=1, source_target_pairs={{0,16},{1,17},{2,18},{3,19},{4,20},{5,21},{6,22},{7,23},{8,24},{9,... | collective-permute-start | bytes 1572872 | tf_op jit(solution)/shard_map/ppermute | solution.py:272
  94.4 0.4 collective-permute-start.13
  94.9 2.1 %collective-permute-start.14 = (bf16[2,2,64,1024]{3,2,1,0:T(8,128)(2,1)S(1)}, bf16[2,2,64,1024]{3,2,1,0:T(8,128)(2,1)S(1)}, u32[]{:S(2)}, u32[]{:S(2)}) collective-permute-start(bf16[2,2,64,1024]{3,2,1,0:T(8,128)(2,1)S(1)} %pad_maximum_fusion.2.second), channel_id=1, source_target_pairs={{0,48},{1,49},{2,50},{3,51},{4,52},{5,53},{6,54},{7,55},{8,56},{9,... | collective-permute-start | bytes 1572872 | tf_op jit(solution)/shard_map/ppermute | solution.py:272
  96.9 4.8 %collective-permute-done.16.others = bf16[2,640,256]{2,1,0:T(8,128)(2,1)S(1)} collective-permute-done((bf16[2,640,256]{2,1,0:T(8,128)(2,1)S(1)}, bf16[2,640,256]{2,1,0:T(8,128)(2,1)S(1)}, u32[]{:S(2)}, u32[]{:S(2)}) %collective-permute-start.16) | collective-permute-done | bytes 655392 | tf_op jit(solution)/shard_map/ppermute | solution.py:276
  101.8 3.5 %factors.1 = (f32[4,1024,256]{2,1,0:T(8,128)}, f32[8,256]{1,0:T(8,128)S(1)}) custom-call(s32[2]{0:T(128)S(1)} %pad_add_fusion.index, f32[1,2]{1,0:T(1,128)S(1)} %copy-done.7, s32[1,4]{1,0:T(1,128)S(1)} %copy-done.6, bf16[2,1024,256]{2,1,0:T(8,128)(2,1)S(1)} %bitcast.28, bf16[2,256,256]{2,1,0:T(8,128)(2,1)S(1)} %bitcast.35, ...), custom_call_target="tpu_custom_call" | custom-call | tf_op jit(solution)/shard_map/factors/pallas_call | solution.py:151
  105.3 6.3 %collective-permute-done.13.s2 = bf16[2,2,64,1024]{3,2,1,0:T(8,128)(2,1)S(1)} collective-permute-done((bf16[2,2,64,1024]{3,2,1,0:T(8,128)(2,1)S(1)}, bf16[2,2,64,1024]{3,2,1,0:T(8,128)(2,1)S(1)}, u32[]{:S(2)}, u32[]{:S(2)}) %collective-permute-start.13) | collective-permute-done | bytes 524320 | tf_op jit(solution)/shard_map/ppermute | solution.py:272
  111.6 1.9 %collective-permute-done.14.s3 = bf16[2,2,64,1024]{3,2,1,0:T(8,128)(2,1)S(1)} collective-permute-done((bf16[2,2,64,1024]{3,2,1,0:T(8,128)(2,1)S(1)}, bf16[2,2,64,1024]{3,2,1,0:T(8,128)(2,1)S(1)}, u32[]{:S(2)}, u32[]{:S(2)}) %collective-permute-start.14) | collective-permute-done | bytes 524320 | tf_op jit(solution)/shard_map/ppermute | solution.py:272
  113.5 6.8 %upper.1 = (bf16[2,1024,256]{2,1,0:T(8,128)(2,1)}, f32[8,512]{1,0:T(8,128)S(1)}) custom-call(s32[2]{0:T(128)S(1)} %pad_add_fusion.index, s32[1,4]{1,0:T(1,128)S(1)} %copy-done.6, bf16[2,1024,256]{2,1,0:T(8,128)(2,1)S(1)} %bitcast.29, bf16[4,2,64,1024]{3,2,1,0:T(8,128)(2,1)} %copy-done.8, bf16[4,2,64,1024]{3,2,1,0:T(8,128)(2,1)} %collective-permute-done.6.first_y, ...), custom_call_target="tpu_custom_call" | custom-call | tf_op jit(solution)/shard_map/upper/pallas_call | solution.py:206
  120.5 10.6 %psum.7 = f32[64,1,16]{0,2,1:T(8,128)S(1)} all-reduce(f32[64,1,16]{0,2,1:T(8,128)S(1)} %bitcast.56), channel_id=1, replica_groups=mesh['pole'=4,'grid'=64] {'pole'}, use_global_device_ids=true, to_apply=%region_0.0 | all-reduce | flops 1024 | bytes 8192 | tf_op jit(solution)/shard_map/psum | solution.py:305
  131.0 0.7 copy.17
  131.7 18.0 %all-to-all-start.1 = ((f32[64,1,16]{2,1,0:T(1,128)}), f32[64,1,16]{2,1,0:T(1,128)S(1)}, u32[]{:S(2)}, u32[]{:S(2)}) async-start(f32[64,1,16]{2,1,0:T(1,128)} %copy.17), calls=%async_computation.1 | async-start | bytes 65536 | tf_op jit(solution)/shard_map/all_to_all | solution.py:307
  149.7 1.2 copy-done.1
  151.0 2.1 %diag.1 = bf16[2,256,256]{2,1,0:T(8,128)(2,1)} custom-call(s32[1,4]{1,0:T(1,128)S(1)} %copy-done.6, bf16[2,1024,256]{2,1,0:T(8,128)(2,1)S(1)} %bitcast.30, bf16[2,1024,256]{2,1,0:T(8,128)(2,1)S(1)} %copy-done.1, bf16[2,256,256]{2,1,0:T(8,128)(2,1)S(1)} %bitcast.36), custom_call_target="tpu_custom_call" | custom-call | tf_op jit(solution)/shard_map/diag/pallas_call | solution.py:236
  153.0 7.5 %all-to-all-done.1 = f32[64,1,16]{2,1,0:T(1,128)S(1)} async-done(((f32[64,1,16]{2,1,0:T(1,128)}), f32[64,1,16]{2,1,0:T(1,128)S(1)}, u32[]{:S(2)}, u32[]{:S(2)}) %all-to-all-start.1) | async-done | bytes 4128 | tf_op jit(solution)/shard_map/all_to_all | solution.py:307
  160.8 0.2 place.1
  161.0 0.6 fusion.1
  (40 shorter events, 1.0 us)
Async XLA Ops:
  0.7 1.1 copy-start.3
  1.8 1.1 copy-start.4
  2.9 0.8 copy-start.5
  6.3 95.4 %copy-start = (bf16[1,2,1024,256]{3,2,1,0:T(8,128)(2,1)S(1)}, bf16[1,2,1024,256]{3,2,1,0:T(8,128)(2,1)}, u32[]{:S(2)}) copy-start(bf16[1,2,1024,256]{3,2,1,0:T(8,128)(2,1)} %param.9) | copy-start | bytes 3145732
  6.3 95.4 %copy-start.2 = (bf16[1,2,256,256]{3,2,1,0:T(8,128)(2,1)S(1)}, bf16[1,2,256,256]{3,2,1,0:T(8,128)(2,1)}, u32[]{:S(2)}) copy-start(bf16[1,2,256,256]{3,2,1,0:T(8,128)(2,1)} %param.11) | copy-start | bytes 786436
  6.3 95.4 %copy-start.6 = (s32[1,4]{1,0:T(1,128)S(1)}, s32[1,4]{1,0:T(1,128)}, u32[]{:S(2)}) copy-start(s32[1,4]{1,0:T(1,128)} %fill.5) | copy-start | bytes 52
  6.3 95.4 %copy-start.7 = (f32[1,2]{1,0:T(1,128)S(1)}, f32[1,2]{1,0:T(1,128)}, u32[]{:S(2)}) copy-start(f32[1,2]{1,0:T(1,128)} %weights.1) | copy-start | bytes 28
  6.3 56.7 %all-to-all-start = ((bf16[64,8,640]{2,1,0:T(8,128)(2,1)}), bf16[64,8,640]{2,1,0:T(8,128)(2,1)S(1)}, u32[]{:S(2)}, u32[]{:S(2)}) async-start(bf16[64,8,640]{2,1,0:T(8,128)(2,1)} %bitcast.14), calls=%async_computation | async-start | bytes 1310720 | tf_op jit(solution)/shard_map/all_to_all | solution.py:294
  21.6 16.4 %collective-permute-start = (bf16[2,16,1024]{2,1,0:T(8,128)(2,1)}, bf16[2,16,1024]{2,1,0:T(8,128)(2,1)S(1)}, u32[]{:S(2)}, u32[]{:S(2)}) collective-permute-start(bf16[2,16,1024]{2,1,0:T(8,128)(2,1)} %bitcast.47), channel_id=1, source_target_pairs={{0,1},{1,2},{2,3},{3,4},{4,5},{5,6},{6,7},{7,0},{8,9},{9,10},{10,1... | collective-permute-start | bytes 196616 | tf_op jit(solution)/shard_map/ppermute | solution.py:272
  22.7 19.2 %collective-permute-start.1 = (bf16[2,16,1024]{2,1,0:T(8,128)(2,1)}, bf16[2,16,1024]{2,1,0:T(8,128)(2,1)S(1)}, u32[]{:S(2)}, u32[]{:S(2)}) collective-permute-start(bf16[2,16,1024]{2,1,0:T(8,128)(2,1)} %bitcast.48), channel_id=1, source_target_pairs={{0,2},{1,3},{2,4},{3,5},{4,6},{5,7},{6,0},{7,1},{8,10},{9,11},{10,... | collective-permute-start | bytes 196616 | tf_op jit(solution)/shard_map/ppermute | solution.py:272
  24.8 19.9 %collective-permute-start.2 = (bf16[2,16,1024]{2,1,0:T(8,128)(2,1)}, bf16[2,16,1024]{2,1,0:T(8,128)(2,1)S(1)}, u32[]{:S(2)}, u32[]{:S(2)}) collective-permute-start(bf16[2,16,1024]{2,1,0:T(8,128)(2,1)} %bitcast.49), channel_id=1, source_target_pairs={{0,3},{1,4},{2,5},{3,6},{4,7},{5,0},{6,1},{7,2},{8,11},{9,12},{10,... | collective-permute-start | bytes 196616 | tf_op jit(solution)/shard_map/ppermute | solution.py:272
  27.2 24.6 %collective-permute-start.7 = (bf16[2,16,1024]{2,1,0:T(8,128)(2,1)}, bf16[2,16,1024]{2,1,0:T(8,128)(2,1)S(1)}, u32[]{:S(2)}, u32[]{:S(2)}) collective-permute-start(bf16[2,16,1024]{2,1,0:T(8,128)(2,1)} %bitcast.50), channel_id=1, source_target_pairs={{0,4},{1,5},{2,6},{3,7},{4,0},{5,1},{6,2},{7,3},{8,12},{9,13},{10,... | collective-permute-start | bytes 196616 | tf_op jit(solution)/shard_map/ppermute | solution.py:272
  29.3 26.6 %collective-permute-start.8 = (bf16[2,16,1024]{2,1,0:T(8,128)(2,1)}, bf16[2,16,1024]{2,1,0:T(8,128)(2,1)S(1)}, u32[]{:S(2)}, u32[]{:S(2)}) collective-permute-start(bf16[2,16,1024]{2,1,0:T(8,128)(2,1)} %bitcast.51), channel_id=1, source_target_pairs={{0,5},{1,6},{2,7},{3,0},{4,1},{5,2},{6,3},{7,4},{8,13},{9,14},{10,... | collective-permute-start | bytes 196616 | tf_op jit(solution)/shard_map/ppermute | solution.py:272
  46.3 11.7 %collective-permute-start.3 = (bf16[2,64,1024]{2,1,0:T(8,128)(2,1)S(1)}, bf16[2,64,1024]{2,1,0:T(8,128)(2,1)S(1)}, u32[]{:S(2)}, u32[]{:S(2)}) collective-permute-start(bf16[2,64,1024]{2,1,0:T(8,128)(2,1)S(1)} %get-tuple-element.21), channel_id=1, source_target_pairs={{0,16},{1,17},{2,18},{3,19},{4,20},{5,21},{6,22},{7,23},{8,24},{9,... | collective-permute-start | bytes 786440 | tf_op jit(solution)/shard_map/ppermute | solution.py:272
  47.5 10.7 %collective-permute-start.4 = (bf16[2,64,1024]{2,1,0:T(8,128)(2,1)S(1)}, bf16[2,64,1024]{2,1,0:T(8,128)(2,1)S(1)}, u32[]{:S(2)}, u32[]{:S(2)}) collective-permute-start(bf16[2,64,1024]{2,1,0:T(8,128)(2,1)S(1)} %get-tuple-element.21), channel_id=1, source_target_pairs={{0,32},{1,33},{2,34},{3,35},{4,36},{5,37},{6,38},{7,39},{8,40},{9,... | collective-permute-start | bytes 786440 | tf_op jit(solution)/shard_map/ppermute | solution.py:272
  50.0 8.2 %collective-permute-start.5 = (bf16[2,64,1024]{2,1,0:T(8,128)(2,1)S(1)}, bf16[2,64,1024]{2,1,0:T(8,128)(2,1)}, u32[]{:S(2)}, u32[]{:S(2)}) collective-permute-start(bf16[2,64,1024]{2,1,0:T(8,128)(2,1)S(1)} %get-tuple-element.21), channel_id=1, source_target_pairs={{0,48},{1,49},{2,50},{3,51},{4,52},{5,53},{6,54},{7,55},{8,56},{9,... | collective-permute-start | bytes 786440 | tf_op jit(solution)/shard_map/ppermute | solution.py:272
  51.8 16.7 %collective-permute-start.9 = (bf16[2,16,1024]{2,1,0:T(8,128)(2,1)}, bf16[2,16,1024]{2,1,0:T(8,128)(2,1)}, u32[]{:S(2)}, u32[]{:S(2)}) collective-permute-start(bf16[2,16,1024]{2,1,0:T(8,128)(2,1)} %bitcast.53), channel_id=1, source_target_pairs={{0,6},{1,7},{2,0},{3,1},{4,2},{5,3},{6,4},{7,5},{8,14},{9,15},{10,... | collective-permute-start | bytes 196616 | tf_op jit(solution)/shard_map/ppermute | solution.py:272
  55.8 14.1 %collective-permute-start.10 = (bf16[2,16,1024]{2,1,0:T(8,128)(2,1)}, bf16[2,16,1024]{2,1,0:T(8,128)(2,1)S(1)}, u32[]{:S(2)}, u32[]{:S(2)}) collective-permute-start(bf16[2,16,1024]{2,1,0:T(8,128)(2,1)} %bitcast.54), channel_id=1, source_target_pairs={{0,7},{1,0},{2,1},{3,2},{4,3},{5,4},{6,5},{7,6},{8,15},{9,8},{10,9... | collective-permute-start | bytes 196616 | tf_op jit(solution)/shard_map/ppermute | solution.py:272
  58.0 0.7 copy-start.9
  58.0 0.8 copy-start.10
  58.2 0.7 copy-start.11
  60.2 53.3 %copy-start.8 = (bf16[4,2,64,1024]{3,2,1,0:T(8,128)(2,1)}, bf16[4,2,64,1024]{3,2,1,0:T(8,128)(2,1)S(1)}, u32[]{:S(2)}) copy-start(bf16[4,2,64,1024]{3,2,1,0:T(8,128)(2,1)S(1)} %pad_maximum_fusion.first) | copy-start | bytes 3145732
  60.2 53.3 %collective-permute-start.6 = (bf16[4,2,64,1024]{3,2,1,0:T(8,128)(2,1)S(1)}, bf16[4,2,64,1024]{3,2,1,0:T(8,128)(2,1)}, u32[]{:S(2)}, u32[]{:S(2)}) collective-permute-start(bf16[4,2,64,1024]{3,2,1,0:T(8,128)(2,1)S(1)} %pad_maximum_fusion.first), channel_id=1, source_target_pairs={{0,8},{1,9},{2,10},{3,11},{4,12},{5,13},{6,14},{7,15},{8,0},{9,1},... | collective-permute-start | bytes 3145736 | tf_op jit(solution)/shard_map/ppermute | solution.py:272
  63.5 7.4 %collective-permute-start.15 = (bf16[640,256]{1,0:T(8,128)(2,1)S(1)}, bf16[640,256]{1,0:T(8,128)(2,1)S(1)}, u32[]{:S(2)}, u32[]{:S(2)}) collective-permute-start(bf16[640,256]{1,0:T(8,128)(2,1)S(1)} %get-tuple-element.13.own), channel_id=1, source_target_pairs={{0,64},{64,0},{128,192},{192,128},{1,65},{65,1},{129,193},{193,129... | collective-permute-start | bytes 983048 | tf_op jit(solution)/shard_map/ppermute | solution.py:276
  70.6 17.0 %collective-permute-start.11 = (bf16[2,64,1024]{2,1,0:T(8,128)(2,1)}, bf16[2,64,1024]{2,1,0:T(8,128)(2,1)S(1)}, u32[]{:S(2)}, u32[]{:S(2)}) collective-permute-start(bf16[2,64,1024]{2,1,0:T(8,128)(2,1)} %constant_dynamic-update-slice_fusion), channel_id=1, source_target_pairs={{0,8},{1,9},{2,10},{3,11},{4,12},{5,13},{6,14},{7,15},{8,0},{9,1},... | collective-permute-start | bytes 786440 | tf_op jit(solution)/shard_map/ppermute | solution.py:272
  71.0 30.7 %collective-permute-start.16 = (bf16[2,640,256]{2,1,0:T(8,128)(2,1)S(1)}, bf16[2,640,256]{2,1,0:T(8,128)(2,1)S(1)}, u32[]{:S(2)}, u32[]{:S(2)}) collective-permute-start(bf16[2,640,256]{2,1,0:T(8,128)(2,1)S(1)} %pad_maximum_fusion.1), channel_id=1, source_target_pairs={{0,128},{64,192},{128,0},{192,64},{1,129},{65,193},{129,1},{193,65... | collective-permute-start | bytes 1966088 | tf_op jit(solution)/shard_map/ppermute | solution.py:276
  88.5 16.8 %collective-permute-start.12 = (bf16[2,2,64,1024]{3,2,1,0:T(8,128)(2,1)S(1)}, bf16[2,2,64,1024]{3,2,1,0:T(8,128)(2,1)S(1)}, u32[]{:S(2)}, u32[]{:S(2)}) collective-permute-start(bf16[2,2,64,1024]{3,2,1,0:T(8,128)(2,1)S(1)} %pad_maximum_fusion.2.second), channel_id=1, source_target_pairs={{0,16},{1,17},{2,18},{3,19},{4,20},{5,21},{6,22},{7,23},{8,24},{9,... | collective-permute-start | bytes 1572872 | tf_op jit(solution)/shard_map/ppermute | solution.py:272
  94.4 17.1 %collective-permute-start.13 = (bf16[2,2,64,1024]{3,2,1,0:T(8,128)(2,1)S(1)}, bf16[2,2,64,1024]{3,2,1,0:T(8,128)(2,1)S(1)}, u32[]{:S(2)}, u32[]{:S(2)}) collective-permute-start(bf16[2,2,64,1024]{3,2,1,0:T(8,128)(2,1)S(1)} %pad_maximum_fusion.2.second), channel_id=1, source_target_pairs={{0,32},{1,33},{2,34},{3,35},{4,36},{5,37},{6,38},{7,39},{8,40},{9,... | collective-permute-start | bytes 1572872 | tf_op jit(solution)/shard_map/ppermute | solution.py:272
  94.9 18.6 %collective-permute-start.14 = (bf16[2,2,64,1024]{3,2,1,0:T(8,128)(2,1)S(1)}, bf16[2,2,64,1024]{3,2,1,0:T(8,128)(2,1)S(1)}, u32[]{:S(2)}, u32[]{:S(2)}) collective-permute-start(bf16[2,2,64,1024]{3,2,1,0:T(8,128)(2,1)S(1)} %pad_maximum_fusion.2.second), channel_id=1, source_target_pairs={{0,48},{1,49},{2,50},{3,51},{4,52},{5,53},{6,54},{7,55},{8,56},{9,... | collective-permute-start | bytes 1572872 | tf_op jit(solution)/shard_map/ppermute | solution.py:272
  131.7 28.7 %all-to-all-start.1 = ((f32[64,1,16]{2,1,0:T(1,128)}), f32[64,1,16]{2,1,0:T(1,128)S(1)}, u32[]{:S(2)}, u32[]{:S(2)}) async-start(f32[64,1,16]{2,1,0:T(1,128)} %copy.17), calls=%async_computation.1 | async-start | bytes 65536 | tf_op jit(solution)/shard_map/all_to_all | solution.py:307
  149.7 1.2 copy-start.1

commit v2 on v1

v2 whole, which is shorter than its diff:
```python
import jax
import jax.numpy as jnp
from jax import lax
from jax.experimental import pallas as pl
from jax.experimental.pallas import tpu as pltpu
from jax.sharding import PartitionSpec as P

F32 = jnp.float32
BF16 = jnp.bfloat16
I32 = jnp.int32
NX, NY, NZ = 4, 2, 8
GROUPS = NX * NY * NZ
POLES = 4
CAP = 8
SLOTS = GROUPS * CAP
PLANE = NY * NZ
COLS = 256
ANC = 1024
ROWS = 1280
QUARTER = ROWS // POLES
SHARD = ANC // GROUPS
LATE = 384
EARLY = ANC - LATE
VMEM_LIMIT = 50 * 1024 * 1024
SMEM_SPEC = pl.BlockSpec(memory_space=pltpu.SMEM)
VMEM_SPEC = pl.BlockSpec(memory_space=pltpu.VMEM)
ANY_SPEC = pl.BlockSpec(memory_space=pl.ANY)


def params():
    return pltpu.CompilerParams(vmem_limit_bytes=VMEM_LIMIT)


def mm(a, b, contract=((1,), (0,))):
    return lax.dot_general(a, b, (contract, ((), ())), preferred_element_type=F32)


def iota(shape, dim):
    return lax.broadcasted_iota(I32, shape, dim)


def flag(condition):
    return jnp.where(condition, 1.0, 0.0).astype(BF16)


def split_matmul(values, onehot, contract):
    high = values.astype(BF16)
    rest = values - high.astype(F32)
    middle = rest.astype(BF16)
    low = (rest - middle.astype(F32)).astype(BF16)
    return mm(high, onehot, contract) + mm(middle, onehot, contract) + mm(low, onehot, contract)


def pack_kernel(index, dft, margin, hamiltonian, out0, out1, out2, out3, slot_onehot, both, sems):
    start = pl.multiple_of(index[0] * QUARTER, QUARTER)
    copies = [
        pltpu.make_async_copy(ref.at[pl.ds(start, QUARTER), :], both.at[pl.ds(n * QUARTER, QUARTER), :], sems.at[n])
        for n, ref in enumerate((margin, hamiltonian))
    ]
    for copy in copies:
        copy.start()
    entries = dft[...]
    side = entries.shape[0]
    hit = (entries >> 8) == index[1]
    row, col = iota((side, side), 0), iota((side, side), 1)
    hit_flag = flag(hit)
    rank = mm(hit_flag, flag(row < col))
    previous = mm(flag(((row & 1) == 1) & (col == row - 1)), hit_flag).astype(BF16)
    rank = rank + mm(previous, jnp.ones((side, side), BF16))
    place = ((entries & 255) + 1).astype(F32)
    pair = flag((iota((GROUPS, side), 1) >> 1) == iota((GROUPS, side), 0))
    target = (iota((GROUPS, COLS), 1) + 1).astype(F32)
    pieces = []
    for r in range(CAP):
        picked = jnp.where(hit & (rank == float(r)), place, 0.0).astype(BF16)
        local = jnp.sum(mm(pair, picked), axis=1, keepdims=True)
        pieces.append(flag(local == target))
    by_rank = jnp.concatenate(pieces, axis=0)
    s, t = iota((SLOTS, SLOTS), 0), iota((SLOTS, SLOTS), 1)
    order = flag((s & (CAP - 1)) * GROUPS + (s >> 3) == t)
    slot_onehot[...] = mm(order, by_rank).astype(BF16)
    for copy in copies:
        copy.wait()
    rows = both[...]
    x = index[1] >> 4
    for turn, out in enumerate((out0, out1, out2, out3)):
        first = pl.multiple_of(((x + turn) & (NX - 1)) * (PLANE * CAP), PLANE * CAP)
        out[...] = mm(slot_onehot[pl.ds(first, PLANE * CAP), :], rows, ((1,), (1,))).astype(BF16)


def pack(index, dft, margin, hamiltonian):
    return pl.pallas_call(
        pack_kernel,
        in_specs=[SMEM_SPEC, VMEM_SPEC, ANY_SPEC, ANY_SPEC],
        out_specs=[VMEM_SPEC] * (NX + 1),
        out_shape=[jax.ShapeDtypeStruct((PLANE * CAP, 2 * QUARTER), BF16)] * NX
        + [jax.ShapeDtypeStruct((SLOTS, COLS), BF16)],
        scratch_shapes=[pltpu.VMEM((2 * QUARTER, COLS), BF16), pltpu.SemaphoreType.DMA((2,))],
        compiler_params=params(),
        name="pack",
    )(index, dft, margin, hamiltonian)


def unpack_kernel(index, dft, arrived, out, column_onehot):
    grid = index[1]
    group_row = jnp.concatenate([dft[pl.ds(2 * grid, 1), :], dft[pl.ds(2 * grid + 1, 1), :]], axis=1) >> 8
    above, across = iota((COLS, COLS), 0), iota((COLS, COLS), 1)
    group_col = jnp.sum(jnp.where(above == across, group_row, 0), axis=1, keepdims=True)
    rank = jnp.sum(jnp.where((group_col == group_row) & (above < across), 1, 0), axis=0, keepdims=True)
    place = iota((SLOTS, COLS), 0)
    column_onehot[...] = flag(place == group_row * CAP + rank)
    turn = ((grid >> 4) - (group_row >> 4)) & (NX - 1)
    slot = (group_row & (PLANE - 1)) * (NX * CAP) + turn * CAP + rank
    out[...] = mm(arrived[...], flag(place == slot), ((0,), (0,))).astype(BF16)


def unpack(index, dft, arrived):
    return pl.pallas_call(
        unpack_kernel,
        in_specs=[SMEM_SPEC] + [VMEM_SPEC] * 2,
        out_specs=[VMEM_SPEC] * 2,
        out_shape=[
            jax.ShapeDtypeStruct((2 * QUARTER, COLS), BF16),
            jax.ShapeDtypeStruct((SLOTS, COLS), BF16),
        ],
        compiler_params=params(),
        name="unpack",
    )(index, dft, arrived)


def factor_kernel(index, weights, fill, lower, diag_inverse, own, mates, out, base, rows, masked):
    pole = index[0]
    for part in range(2):
        for block in range(ANC // COLS):
            keep = fill[0, block].astype(F32).astype(BF16)
            span = slice(block * COLS, (block + 1) * COLS)
            masked[part, span, :] = lower[part, span, :] * keep
    for bits, ref, n in ((0, own, 0), (2, own, 1), (1, mates, 0), (3, mates, 1)):
        start = pl.multiple_of((pole ^ bits) * QUARTER, QUARTER)
        for which in range(2):
            rows[which, pl.ds(start, QUARTER), :] = ref[n, which * QUARTER : (which + 1) * QUARTER, :]
    real, imag = weights[0, 0], weights[0, 1]
    for which in range(2):
        near = rows[which, 0:COLS, :]
        near_float = near.astype(F32)
        sums = real * diag_inverse[1].astype(F32) + imag * diag_inverse[0].astype(F32)
        base[which : which + 1, :] = jnp.sum(sums * near_float, axis=0, keepdims=True)
        for block in range(ANC // COLS):
            span = slice(block * COLS, (block + 1) * COLS)
            far = rows[which, (block + 1) * COLS : (block + 2) * COLS, :].astype(F32)
            direct = far - mm(masked[0, span, :], near)
            cross = mm(masked[1, span, :], near)
            out[2 * which, span, :] = imag * direct - real * cross
            out[2 * which + 1, span, :] = real * direct + imag * cross
    base[2:8, :] = jnp.zeros((6, COLS), F32)


def factors(index, weights, fill, lower, diag_inverse, own, mates):
    return pl.pallas_call(
        factor_kernel,
        in_specs=[SMEM_SPEC] * 3 + [VMEM_SPEC] * 4,
        out_specs=[VMEM_SPEC] * 2,
        out_shape=[
            jax.ShapeDtypeStruct((4, ANC, COLS), F32),
            jax.ShapeDtypeStruct((8, COLS), F32),
        ],
        scratch_shapes=[pltpu.VMEM((2, ROWS, COLS), BF16), pltpu.VMEM((2, ANC, COLS), BF16)],
        compiler_params=params(),
        name="factors",
    )(index, weights, fill, lower, diag_inverse, own, mates)


def upper_kernel(index, fill, lower, *refs):
    early, late, (factor, base, onehot, out, slots, both, real_sum, imag_sum) = refs[:6], refs[6:10], refs[10:]
    first, first_y, second, second_x1, second_x2, second_x3 = early
    grid = index[1]
    x, y, z = grid >> 4, (grid >> 3) & 1, grid & 7
    for block in range(ANC // COLS):
        keep = fill[0, block].astype(F32).astype(BF16)
        span = slice(block * COLS, (block + 1) * COLS)
        for part in range(2):
            both[span, part * COLS : (part + 1) * COLS] = lower[part, span, :] * keep

    def product(ref, rhs):
        left, right = [mm(ref[:, part].reshape(-1, ref.shape[-1]), rhs) for part in range(2)]
        return right[:, COLS:] - left[:, :COLS], -left[:, COLS:] - right[:, :COLS]

    def start_of(dx, dy, dz):
        px, py, pz = (x - dx) & (NX - 1), (y - dy) & (NY - 1), (z - dz) & (NZ - 1)
        return pl.multiple_of(((px * NY + py) * NZ + pz) * SHARD, SHARD)

    def scatter(ref, places):
        real, imag = product(ref, both[0:EARLY, :])
        for n, place in enumerate(places):
            span = slice(n * SHARD, (n + 1) * SHARD)
            start = start_of(*place)
            real_sum[pl.ds(start, SHARD), :] = real[span]
            imag_sum[pl.ds(start, SHARD), :] = imag[span]

    for dy, ref in ((0, first), (1, first_y)):
        scatter(ref, [(dx, dy, dz) for dx in range(NX) for dz in (0, 4, 1, 5)])
    for dx, ref in enumerate((second, second_x1, second_x2, second_x3)):
        scatter(ref, [(dx, dy, dz) for dy in range(NY) for dz in (7, 3, 2, 6)])
    rows = [base[which : which + 1, :] for which in range(2)]
    tail = both[EARLY:ANC, :]
    for n, dzs in enumerate(((0, 4), (1, 5), (7, 3), (2, 6))):
        real, imag = product(late[n], tail)
        places = [(dx, dy, dz) for dz in dzs for dy in range(NY) for dx in range(NX)]
        for m, place in enumerate(places):
            span = slice(m * SHARD, (m + 1) * SHARD)
            start = start_of(*place)
            keep = fill[0, (x - place[0]) & (NX - 1)].astype(F32)
            here = pl.ds(start, SHARD)
            out[0, here, :] = ((real[span] + real_sum[here, :]) * keep).astype(BF16)
            out[1, here, :] = ((imag[span] + imag_sum[here, :]) * keep).astype(BF16)
    for block in range(ANC // COLS):
        span = slice(block * COLS, (block + 1) * COLS)
        real, imag = out[0, span, :].astype(F32), out[1, span, :].astype(F32)
        for which in range(2):
            term = real * factor[2 * which, span, :] + imag * factor[2 * which + 1, span, :]
            rows[which] = rows[which] + jnp.sum(term, axis=0, keepdims=True)
    line = iota((8, COLS), 0)
    values = jnp.where(line == 2 * x, rows[0], jnp.where(line == 2 * x + 1, rows[1], 0.0))
    sums = split_matmul(values, onehot[...], ((1,), (1,)))
    width = PLANE * CAP
    for px in range(NX):
        for pole in range(POLES):
            slots[pole * NX + px] = sums[:, px * width : (px + 1) * width]


def upper_rows(index, fill, lower, early, late, factor, base, onehot):
    return pl.pallas_call(
        upper_kernel,
        in_specs=[SMEM_SPEC] * 2 + [VMEM_SPEC] * (4 + len(early) + len(late)),
        out_specs=[VMEM_SPEC] * 2,
        out_shape=[
            jax.ShapeDtypeStruct((2, ANC, COLS), BF16),
            jax.ShapeDtypeStruct((POLES * NX, 8, PLANE * CAP), F32),
        ],
        scratch_shapes=[
            pltpu.VMEM((ANC, 2 * COLS), BF16),
            pltpu.VMEM((ANC, COLS), F32),
            pltpu.VMEM((ANC, COLS), F32),
        ],
        compiler_params=params(),
        name="upper",
    )(index, fill, lower, *early, *late, factor, base, onehot)


def diag_kernel(fill, lower, upper, diag_inverse, out):
    real = diag_inverse[0].astype(F32)
    imag = diag_inverse[1].astype(F32)
    turn = ((0,), (0,))
    for block in range(ANC // COLS):
        keep = fill[0, block].astype(F32).astype(BF16)
        span = slice(block * COLS, (block + 1) * COLS)
        low_real, low_imag = lower[0, span, :] * keep, lower[1, span, :] * keep
        up_real, up_imag = upper[0, span, :], upper[1, span, :]
        real = real - mm(low_real, up_real, turn) + mm(low_imag, up_imag, turn)
        imag = imag - mm(low_real, up_imag, turn) - mm(low_imag, up_real, turn)
    out[0] = real.astype(BF16)
    out[1] = imag.astype(BF16)


def diag_block(fill, lower, upper, diag_inverse):
    return pl.pallas_call(
        diag_kernel,
        in_specs=[SMEM_SPEC] + [VMEM_SPEC] * 3,
        out_specs=VMEM_SPEC,
        out_shape=jax.ShapeDtypeStruct((2, COLS, COLS), BF16),
        compiler_params=params(),
        name="diag",
    )(fill, lower, upper, diag_inverse)


def turn_kernel(arrived, out):
    total = jnp.sum(arrived[...], axis=0)
    width = PLANE * CAP
    for n in range(PLANE):
        out[n] = total if n == 0 else pltpu.roll(total, width - n * CAP, 1)


def turn(arrived):
    return pl.pallas_call(
        turn_kernel,
        in_specs=[VMEM_SPEC],
        out_specs=VMEM_SPEC,
        out_shape=jax.ShapeDtypeStruct((PLANE, 8, PLANE * CAP), F32),
        compiler_params=params(),
        name="turn",
    )(arrived)


def place_kernel(arrived, onehot, out):
    width = PLANE * CAP
    line, lane = iota((8, width), 0), iota((8, width), 1)
    total = jnp.zeros((8, width), F32)
    for n in range(PLANE):
        piece = jnp.where(lane < CAP, arrived[n], 0.0)
        total = total + (piece if n == 0 else pltpu.roll(piece, n * CAP, 1))
    wide = jnp.concatenate([jnp.where((line >> 1) == px, total, 0.0) for px in range(NX)], axis=1)
    result = split_matmul(wide, onehot[...], ((1,), (0,)))
    for which in range(2):
        out[which : which + 1, :] = jnp.sum(
            jnp.where((iota((8, COLS), 0) & 1) == which, result, 0.0), axis=0, keepdims=True
        )


def place(arrived, onehot):
    return pl.pallas_call(
        place_kernel,
        in_specs=[VMEM_SPEC] * 2,
        out_specs=VMEM_SPEC,
        out_shape=jax.ShapeDtypeStruct((2, COLS), F32),
        compiler_params=params(),
        name="place",
    )(arrived, onehot)


SIZES = {"ylo": 2, "core": 2, "x": NX, "yhi": NY, "z": NZ}


def shift(value, axis, by):
    size = SIZES[axis]
    return lax.ppermute(value, axis, [(n, (n + by) % size) for n in range(size)])


def all_of_z(value):
    pair = jnp.stack([value, shift(value, "z", 4)])
    return [pair, shift(pair, "z", 1), shift(pair, "z", -1), shift(pair, "z", 2)]


def body(ainv_anc, lower_panels, fill_pattern, diag_inverse, pole_weights, hamiltonian, margin, dft_column):
    pole = lax.axis_index("ylo") * 2 + lax.axis_index("core")
    grid = (lax.axis_index("x") * NY + lax.axis_index("yhi")) * NZ + lax.axis_index("z")
    index = jnp.stack([pole, grid]).astype(I32)
    lower, inverse = lower_panels[0], diag_inverse[0]
    early, late = ainv_anc[0, :, :, :EARLY], ainv_anc[0, :, :, EARLY:]

    near, near_up, near_down, near_two = all_of_z(early)
    first = jnp.concatenate([near, near_up])
    second = jnp.concatenate([near_down, near_two])
    first = jnp.concatenate([first] + [shift(first, "x", d) for d in (1, 2, 3)])
    second = jnp.concatenate([second, shift(second, "yhi", 1)])
    first_y = shift(first, "yhi", 1)
    second_x = [shift(second, "x", d) for d in (1, 2, 3)]

    late = jnp.stack([late] + [shift(late, "x", d) for d in (1, 2, 3)])
    late = jnp.concatenate([late, shift(late, "yhi", 1)])
    late = [value.reshape(2 * NX * NY, 2, SHARD, LATE) for value in all_of_z(late)]

    table = dft_column.reshape(128, 128)
    packed = pack(index, table, margin, hamiltonian)
    slot_onehot = packed[NX]
    packed = [value.reshape(PLANE, CAP, 2 * QUARTER) for value in packed[:NX]]
    outgoing = jnp.stack([packed[0]] + [shift(packed[d], "x", d) for d in (1, 2, 3)], axis=1)
    arrived = lax.all_to_all(outgoing, ("yhi", "z"), split_axis=0, concat_axis=0, tiled=True)
    mine, column_onehot = unpack(index, table, arrived.reshape(SLOTS, 2 * QUARTER))
    mine = jnp.stack([mine, shift(mine, "ylo", 1)])
    mates = shift(mine, "core", 1)
    factor, base = factors(index, pole_weights, fill_pattern, lower, inverse, mine, mates)

    upper, slots = upper_rows(
        index, fill_pattern, lower, [first, first_y, second] + second_x, late, factor, base, column_onehot
    )
    diag = diag_block(fill_pattern, lower, upper, inverse)
    sums = lax.all_to_all(slots, ("ylo", "core", "x"), split_axis=0, concat_axis=0, tiled=True)
    sums = lax.all_to_all(turn(sums), ("yhi", "z"), split_axis=0, concat_axis=0, tiled=True)
    placed = place(sums, slot_onehot)
    return (upper[None], diag[None], placed[0], placed[1])


def solution(mesh):
    fine = jax.sharding.Mesh(mesh.devices.reshape(2, 2, NX, NY, NZ), ("ylo", "core", "x", "yhi", "z"))
    pole, grid = ("ylo", "core"), ("x", "yhi", "z")
    return jax.shard_map(
        body,
        mesh=fine,
        in_specs=(
            P(pole, None, grid, None),
            P(pole, None, None, grid),
            P(grid, None),
            P(pole, None, None, grid),
            P(pole, None),
            P(None, grid),
            P(None, grid),
            P(),
        ),
        out_specs=(
            P(pole, None, None, grid),
            P(pole, None, None, grid),
            P(grid),
            P(grid),
        ),
        check_vma=False,
    )
```

time: 163 us -> 146 us (0.90)
  waiting for transfers between devices: 49.6 us -> 28.6 us
  blocking collectives: 10.6 us -> 17.4 us
  starting transfers between devices: 71.3 us -> 65.8 us
  Pallas kernels: 15.6 us -> 17.7 us
  local copies, waits for them, and re-layouts: 9.6 us -> 11.7 us
    all_to_all x2, starting transfers between devices: 33.2 us -> 13.3 us  [the longest x1 7.04 us: body(): lax.all_to_all(turn(sums), ('yhi', 'z'), split_axis=0, concat_axis=0, til...]
    ppermute x17 -> x25, waiting for transfers between devices: 42.2 us -> 23.1 us  [shift(): lax.ppermute(value, axis, [(n, (n + by) % size) for n in range(size)])]
    all_to_all x0 -> x1, blocking collectives: none -> 17.4 us  [body(): lax.all_to_all(slots, ('ylo', 'core', 'x'), split_axis=0, concat_axis=0,...]
    ppermute x17 -> x25, starting transfers between devices: 38 us -> 52.5 us  [shift(): lax.ppermute(value, axis, [(n, (n + by) % size) for n in range(size)])]
    psum x1 -> x0, blocking collectives: 10.6 us -> none  [body(): total = lax.psum(slots[:2], 'pole')]
    all_to_all x2, waiting for transfers between devices: 7.46 us -> 5.52 us  [the longest x1 5.52 us: body(): lax.all_to_all(turn(sums), ('yhi', 'z'), split_axis=0, concat_axis=0, til...]
    concatenate x1 -> x3, local copies, waits for them, and re-layouts: 0.64 us -> 2.5 us  [the longest x1 1.54 us: body(): late = jnp.concatenate([late, shift(late, 'yhi', 1)])]
    another operation x5 -> x6, other arithmetic: 4.06 us -> 2.72 us  [the longest x2 0.99 us: all_of_z(): pair = jnp.stack([value, shift(value, 'z', 4)])]
  transfers between devices with their start and end apart: 19 -> 27, of which waited for: 9 -> 5; matrix products, arithmetic and copies ran while one was open for 4% -> 6% of each run, Pallas kernels for 4% -> 6%
where the time goes in v2:
time: 146 us
  starting transfers between devices  65.8 us (45%)
  waiting for transfers between devices  28.6 us (20%)
  Pallas kernels  17.7 us (12%)
  blocking collectives  17.4 us (12%)
  local copies, waits for them, and re-layouts  11.7 us (8%)
  other arithmetic  3.43 us (2%)
    ppermute x25, starting transfers between devices, shift(): lax.ppermute(value, axis, [(n, (n + by) % size) for n in range(size)])  52.5 us
    ppermute x25, waiting for transfers between devices, shift(): lax.ppermute(value, axis, [(n, (n + by) % size) for n in range(size)])  23.1 us
    all_to_all x1, blocking collectives, body(): lax.all_to_all(slots, ('ylo', 'core', 'x'), split_axis=0, concat_axis=0,...  17.4 us
    pallas_call x1, Pallas kernels, upper_rows(): pl.pallas_call(upper_kernel, in_specs=[SMEM_SPEC] * 2 + [VMEM_SPEC] * (4...  7.4 us
    unnamed x33, local copies, waits for them, and re-layouts  7.08 us
    all_to_all x1, starting transfers between devices, body(): lax.all_to_all(turn(sums), ('yhi', 'z'), split_axis=0, concat_axis=0, til...  7.04 us
    all_to_all x1, starting transfers between devices, body(): lax.all_to_all(outgoing, ('yhi', 'z'), split_axis=0, concat_axis=0, tiled...  6.3 us
    all_to_all x1, waiting for transfers between devices, body(): lax.all_to_all(turn(sums), ('yhi', 'z'), split_axis=0, concat_axis=0, til...  5.52 us
  transfers between devices with their start and end apart: 27, of which 5 were waited for; matrix products, arithmetic and copies ran while one was open for 6% of the time, Pallas kernels for 6%

profile of v2, /device:TPU:1, one launch (start us, length us, event | category | flops | bytes accessed | tf_op | source)
XLA Modules:
  0.0 145.6 jit_solution(11043096353180881977)
XLA Ops:
  0.6 0.8 fusion
  1.4 2.0 %collective-permute-start.12 = (bf16[2,16,384]{2,1,0:T(8,128)(2,1)S(1)}, bf16[2,16,384]{2,1,0:T(8,128)(2,1)S(1)}, u32[]{:S(2)}, u32[]{:S(2)}) collective-permute-start(bf16[2,16,384]{2,1,0:T(8,128)(2,1)S(1)} %get-tuple-element.27), channel_id=1, source_target_pairs={{0,16},{16,32},{32,48},{48,0},{1,17},{17,33},{33,49},{49,1},{2,18}... | collective-permute-start | bytes 73736 | tf_op jit(solution)/shard_map/ppermute | solution.py:325
  3.5 2.5 %collective-permute-start.13 = (bf16[2,16,384]{2,1,0:T(8,128)(2,1)S(1)}, bf16[2,16,384]{2,1,0:T(8,128)(2,1)S(1)}, u32[]{:S(2)}, u32[]{:S(2)}) collective-permute-start(bf16[2,16,384]{2,1,0:T(8,128)(2,1)S(1)} %get-tuple-element.27), channel_id=1, source_target_pairs={{0,32},{16,48},{32,0},{48,16},{1,33},{17,49},{33,1},{49,17},{2,34}... | collective-permute-start | bytes 73736 | tf_op jit(solution)/shard_map/ppermute | solution.py:325
  5.9 1.2 collective-permute-start.14
  7.1 1.1 copy-done.4
  8.2 1.1 copy-done.5
  9.3 0.8 copy-done.6
  10.2 2.6 %pack.1 = (bf16[128,640]{1,0:T(8,128)(2,1)S(1)}, bf16[128,640]{1,0:T(8,128)(2,1)S(1)}, bf16[128,640]{1,0:T(8,128)(2,1)S(1)}, bf16[128,640]{1,0:T(8,128)(2,1)S(1)}, bf16[512,256]{1,0:T(8,128)(2,1)S(1)}) custom-call(s32[2]{0:T(128)S(1)} %pad_add_fusion.index, s32[128,128]{1,0:T(8,128)S(1)} %bitcast.51, bf16[1280,256]{1,0:T(8,128)(2,1)S(1)} %copy-done.4, ...), custom_call_target="tpu_custom_call" | custom-call | tf_op jit(solution)/shard_map/pack/pallas_call | solution.py:92
  13.1 0.9 collective-permute-start.21
  14.0 0.8 fusion.1
  14.8 1.7 %collective-permute-start.22 = (bf16[16,8,640]{2,1,0:T(8,128)(2,1)S(1)}, bf16[16,8,640]{2,1,0:T(8,128)(2,1)S(1)}, u32[]{:S(2)}, u32[]{:S(2)}) collective-permute-start(bf16[16,8,640]{2,1,0:T(8,128)(2,1)S(1)} %bitcast.54), channel_id=1, source_target_pairs={{0,48},{16,0},{32,16},{48,32},{1,49},{17,1},{33,17},{49,33},{2,50}... | collective-permute-start | bytes 491528 | tf_op jit(solution)/shard_map/ppermute | solution.py:325
  16.5 6.9 %collective-permute-start = (bf16[2,16,640]{2,1,0:T(8,128)(2,1)S(1)}, bf16[2,16,640]{2,1,0:T(8,128)(2,1)S(1)}, u32[]{:S(2)}, u32[]{:S(2)}) collective-permute-start(bf16[2,16,640]{2,1,0:T(8,128)(2,1)S(1)} %get-tuple-element.30), channel_id=1, source_target_pairs={{0,4},{1,5},{2,6},{3,7},{4,0},{5,1},{6,2},{7,3},{8,12},{9,13},{10,... | collective-permute-start | bytes 122888 | tf_op jit(solution)/shard_map/ppermute | solution.py:325
  24.1 2.9 %collective-permute-start.15 = (bf16[4,2,16,384]{3,2,1,0:T(8,128)(2,1)}, bf16[4,2,16,384]{3,2,1,0:T(8,128)(2,1)}, u32[]{:S(2)}, u32[]{:S(2)}) collective-permute-start(bf16[4,2,16,384]{3,2,1,0:T(8,128)(2,1)} %pad_maximum_fusion.5), channel_id=1, source_target_pairs={{0,8},{8,0},{1,9},{9,1},{2,10},{10,2},{3,11},{11,3},{4,12},{12,4},... | collective-permute-start | bytes 294920 | tf_op jit(solution)/shard_map/ppermute | solution.py:325
  27.1 0.9 pad_maximum_fusion
  28.0 6.3 %all-to-all-start = ((bf16[16,4,8,640]{3,2,1,0:T(8,128)(2,1)}), bf16[16,4,8,640]{3,2,1,0:T(8,128)(2,1)S(1)}, u32[]{:S(2)}, u32[]{:S(2)}) async-start(bf16[16,4,8,640]{3,2,1,0:T(8,128)(2,1)} %pad_maximum_fusion), calls=%async_computation | async-start | bytes 1310720 | tf_op jit(solution)/shard_map/all_to_all | solution.py:357
  34.4 1.4 collective-permute-start.1
  35.8 1.3 collective-permute-start.6
  37.1 1.0 collective-permute-start.7
  38.2 13.2 %collective-permute-done.1 = bf16[2,2,16,640]{3,2,1,0:T(8,128)(2,1)S(1)} collective-permute-done((bf16[2,2,16,640]{3,2,1,0:T(8,128)(2,1)S(1)}, bf16[2,2,16,640]{3,2,1,0:T(8,128)(2,1)S(1)}, u32[]{:S(2)}, u32[]{:S(2)}) %collective-permute-start.1) | collective-permute-done | bytes 81952 | tf_op jit(solution)/shard_map/ppermute | solution.py:325
  51.4 1.2 collective-permute-start.2
  52.6 3.9 %collective-permute-start.3 = (bf16[4,2,16,640]{3,2,1,0:T(8,128)(2,1)S(1)}, bf16[4,2,16,640]{3,2,1,0:T(8,128)(2,1)}, u32[]{:S(2)}, u32[]{:S(2)}) collective-permute-start(bf16[4,2,16,640]{3,2,1,0:T(8,128)(2,1)S(1)} %pad_maximum_fusion.3), channel_id=1, source_target_pairs={{0,32},{16,48},{32,0},{48,16},{1,33},{17,49},{33,1},{49,17},{2,34}... | collective-permute-start | bytes 491528 | tf_op jit(solution)/shard_map/ppermute | solution.py:325
  57.2 2.3 %collective-permute-start.8 = (bf16[4,2,16,640]{3,2,1,0:T(8,128)(2,1)}, bf16[4,2,16,640]{3,2,1,0:T(8,128)(2,1)}, u32[]{:S(2)}, u32[]{:S(2)}) collective-permute-start(bf16[4,2,16,640]{3,2,1,0:T(8,128)(2,1)} %pad_maximum_fusion.4), channel_id=1, source_target_pairs={{0,8},{8,0},{1,9},{9,1},{2,10},{10,2},{3,11},{11,3},{4,12},{12,4},... | collective-permute-start | bytes 491528 | tf_op jit(solution)/shard_map/ppermute | solution.py:325
  59.6 1.1 unpack.1
  61.4 3.0 %collective-permute-start.4 = (bf16[4,2,16,640]{3,2,1,0:T(8,128)(2,1)S(1)}, bf16[4,2,16,640]{3,2,1,0:T(8,128)(2,1)S(1)}, u32[]{:S(2)}, u32[]{:S(2)}) collective-permute-start(bf16[4,2,16,640]{3,2,1,0:T(8,128)(2,1)S(1)} %pad_maximum_fusion.3), channel_id=1, source_target_pairs={{0,48},{16,0},{32,16},{48,32},{1,49},{17,1},{33,17},{49,33},{2,50}... | collective-permute-start | bytes 491528 | tf_op jit(solution)/shard_map/ppermute | solution.py:325
  64.4 1.5 %constant_dynamic-update-slice_fusion.9 = bf16[8,2,16,384]{3,2,1,0:T(8,128)(2,1)} fusion(bf16[8,2,16,384]{3,2,1,0:T(8,128)(2,1)} %copy-done.11, bf16[4,2,16,384]{3,2,1,0:T(8,128)(2,1)} %collective-permute-done.15), kind=kLoop, calls=%fused_computation.16 | loop fusion | bytes 196608 | tf_op jit(solution)/shard_map/concatenate | solution.py:349
  65.9 3.1 %collective-permute-start.16 = (bf16[8,2,16,384]{3,2,1,0:T(8,128)(2,1)}, bf16[8,2,16,384]{3,2,1,0:T(8,128)(2,1)S(1)}, u32[]{:S(2)}, u32[]{:S(2)}) collective-permute-start(bf16[8,2,16,384]{3,2,1,0:T(8,128)(2,1)} %constant_dynamic-update-slice_fusion.9), channel_id=1, source_target_pairs={{0,4},{1,5},{2,6},{3,7},{4,0},{5,1},{6,2},{7,3},{8,12},{9,13},{10,... | collective-permute-start | bytes 589832 | tf_op jit(solution)/shard_map/ppermute | solution.py:325
  69.0 0.9 constant_dynamic-update-slice_fusion.6.refs_2_
  70.4 5.3 %collective-permute-start.24 = (bf16[2,640,256]{2,1,0:T(8,128)(2,1)S(1)}, bf16[2,640,256]{2,1,0:T(8,128)(2,1)S(1)}, u32[]{:S(2)}, u32[]{:S(2)}) collective-permute-start(bf16[2,640,256]{2,1,0:T(8,128)(2,1)S(1)} %pad_maximum_fusion.1.own), channel_id=1, source_target_pairs={{0,64},{64,0},{1,65},{65,1},{2,66},{66,2},{3,67},{67,3},{4,68},{68... | collective-permute-start | bytes 1966088 | tf_op jit(solution)/shard_map/ppermute | solution.py:325
  75.7 0.9 constant_dynamic-update-slice_fusion.2
  76.7 2.9 %collective-permute-start.11 = (bf16[8,2,16,640]{3,2,1,0:T(8,128)(2,1)S(1)}, bf16[8,2,16,640]{3,2,1,0:T(8,128)(2,1)S(1)}, u32[]{:S(2)}, u32[]{:S(2)}) collective-permute-start(bf16[8,2,16,640]{3,2,1,0:T(8,128)(2,1)S(1)} %constant_dynamic-update-slice_fusion.6.refs_2_), channel_id=1, source_target_pairs={{0,48},{16,0},{32,16},{48,32},{1,49},{17,1},{33,17},{49,33},{2,50}... | collective-permute-start | bytes 983048 | tf_op jit(solution)/shard_map/ppermute | solution.py:325
  79.6 0.9 constant_dynamic-update-slice_fusion.1
  80.6 1.4 collective-permute-start.5
  82.0 1.0 pad_maximum_fusion.2
  83.0 1.2 collective-permute-start.17
  84.2 1.5 %collective-permute-start.18 = (bf16[2,8,2,16,384]{4,3,2,1,0:T(8,128)(2,1)S(1)}, bf16[2,8,2,16,384]{4,3,2,1,0:T(8,128)(2,1)S(1)}, u32[]{:S(2)}, u32[]{:S(2)}) collective-permute-start(bf16[2,8,2,16,384]{4,3,2,1,0:T(8,128)(2,1)S(1)} %pad_maximum_fusion.2), channel_id=1, source_target_pairs={{0,7},{1,0},{2,1},{3,2},{4,3},{5,4},{6,5},{7,6},{8,15},{9,8},{10,9... | collective-permute-start | bytes 1179656 | tf_op jit(solution)/shard_map/ppermute | solution.py:325
  85.7 2.1 %collective-permute-done.11.refs_5_ = bf16[8,2,16,640]{3,2,1,0:T(8,128)(2,1)S(1)} collective-permute-done((bf16[8,2,16,640]{3,2,1,0:T(8,128)(2,1)S(1)}, bf16[8,2,16,640]{3,2,1,0:T(8,128)(2,1)S(1)}, u32[]{:S(2)}, u32[]{:S(2)}) %collective-permute-start.11) | collective-permute-done | bytes 327712 | tf_op jit(solution)/shard_map/ppermute | solution.py:325
  87.8 1.5 %collective-permute-start.19 = (bf16[2,8,2,16,384]{4,3,2,1,0:T(8,128)(2,1)S(1)}, bf16[2,8,2,16,384]{4,3,2,1,0:T(8,128)(2,1)S(1)}, u32[]{:S(2)}, u32[]{:S(2)}) collective-permute-start(bf16[2,8,2,16,384]{4,3,2,1,0:T(8,128)(2,1)S(1)} %pad_maximum_fusion.2), channel_id=1, source_target_pairs={{0,2},{1,3},{2,4},{3,5},{4,6},{5,7},{6,0},{7,1},{8,10},{9,11},{10,... | collective-permute-start | bytes 1179656 | tf_op jit(solution)/shard_map/ppermute | solution.py:325
  89.3 1.7 %collective-permute-start.9 = (bf16[8,2,16,640]{3,2,1,0:T(8,128)(2,1)S(1)}, bf16[8,2,16,640]{3,2,1,0:T(8,128)(2,1)S(1)}, u32[]{:S(2)}, u32[]{:S(2)}) collective-permute-start(bf16[8,2,16,640]{3,2,1,0:T(8,128)(2,1)S(1)} %constant_dynamic-update-slice_fusion.6.refs_2_), channel_id=1, source_target_pairs={{0,16},{16,32},{32,48},{48,0},{1,17},{17,33},{33,49},{49,1},{2,18}... | collective-permute-start | bytes 983048 | tf_op jit(solution)/shard_map/ppermute | solution.py:325
  91.1 3.5 %factors.1 = (f32[4,1024,256]{2,1,0:T(8,128)}, f32[8,256]{1,0:T(8,128)S(1)}) custom-call(s32[2]{0:T(128)S(1)} %pad_add_fusion.index, f32[1,2]{1,0:T(1,128)S(1)} %copy-done.9, s32[1,4]{1,0:T(1,128)S(1)} %copy-done.8, bf16[2,1024,256]{2,1,0:T(8,128)(2,1)S(1)} %bitcast.40, bf16[2,256,256]{2,1,0:T(8,128)(2,1)S(1)} %bitcast.45, ...), custom_call_target="tpu_custom_call" | custom-call | tf_op jit(solution)/shard_map/factors/pallas_call | solution.py:159
  94.6 5.1 %collective-permute-done.9.refs_3_ = bf16[8,2,16,640]{3,2,1,0:T(8,128)(2,1)S(1)} collective-permute-done((bf16[8,2,16,640]{3,2,1,0:T(8,128)(2,1)S(1)}, bf16[8,2,16,640]{3,2,1,0:T(8,128)(2,1)S(1)}, u32[]{:S(2)}, u32[]{:S(2)}) %collective-permute-start.9) | collective-permute-done | bytes 327712 | tf_op jit(solution)/shard_map/ppermute | solution.py:325
  99.7 2.7 %collective-permute-done.19 = bf16[2,8,2,16,384]{4,3,2,1,0:T(8,128)(2,1)S(1)} collective-permute-done((bf16[2,8,2,16,384]{4,3,2,1,0:T(8,128)(2,1)S(1)}, bf16[2,8,2,16,384]{4,3,2,1,0:T(8,128)(2,1)S(1)}, u32[]{:S(2)}, u32[]{:S(2)}) %collective-permute-start.19) | collective-permute-done | bytes 393248 | tf_op jit(solution)/shard_map/ppermute | solution.py:325
  102.4 0.8 copy-done.10
  103.3 7.4 %upper.1 = (bf16[2,1024,256]{2,1,0:T(8,128)(2,1)}, f32[16,8,128]{2,1,0:T(8,128)S(1)}) custom-call(s32[2]{0:T(128)S(1)} %pad_add_fusion.index, s32[1,4]{1,0:T(1,128)S(1)} %copy-done.8, bf16[2,1024,256]{2,1,0:T(8,128)(2,1)} %bitcast.39, bf16[16,2,16,640]{3,2,1,0:T(8,128)(2,1)S(1)} %constant_dynamic-update-slice_fusion.refs_0_, ...), custom_call_target="tpu_custom_call" | custom-call | tf_op jit(solution)/shard_map/upper/pallas_call | solution.py:232
  110.7 17.4 %all_to_all.15.arrived = f32[16,8,128]{2,1,0:T(8,128)S(1)} all-to-all(f32[16,8,128]{2,1,0:T(8,128)S(1)} %get-tuple-element.24), channel_id=1, replica_groups=mesh['ylo'=2,'core'=2,'x'=4,'yhi'=2,'z'=8] {'ylo','core','x'}, dimensions={0} | all-to-all | bytes 131072 | tf_op jit(solution)/shard_map/all_to_all | solution.py:367
  128.8 7.0 %all-to-all-start.2 = ((f32[16,8,128]{2,1,0:T(8,128)}), f32[16,8,128]{2,1,0:T(8,128)S(1)}, u32[]{:S(2)}, u32[]{:S(2)}) async-start(f32[16,8,128]{2,1,0:T(8,128)} %turn.1), calls=%async_computation.2 | async-start | bytes 131072 | tf_op jit(solution)/shard_map/all_to_all | solution.py:368
  135.9 1.2 copy-done.2
  137.1 2.1 %diag.1 = bf16[2,256,256]{2,1,0:T(8,128)(2,1)} custom-call(s32[1,4]{1,0:T(1,128)S(1)} %copy-done.8, bf16[2,1024,256]{2,1,0:T(8,128)(2,1)S(1)} %bitcast.41, bf16[2,1024,256]{2,1,0:T(8,128)(2,1)S(1)} %copy-done.2, bf16[2,256,256]{2,1,0:T(8,128)(2,1)S(1)} %bitcast.46), custom_call_target="tpu_custom_call" | custom-call | tf_op jit(solution)/shard_map/diag/pallas_call | solution.py:266
  139.3 5.5 %all-to-all-done.2.arrived = f32[16,8,128]{2,1,0:T(8,128)S(1)} async-done(((f32[16,8,128]{2,1,0:T(8,128)}), f32[16,8,128]{2,1,0:T(8,128)S(1)}, u32[]{:S(2)}, u32[]{:S(2)}) %all-to-all-start.2) | async-done | bytes 65568 | tf_op jit(solution)/shard_map/all_to_all | solution.py:368
  (61 shorter events, 4.7 us)
Async XLA Ops:
  0.6 58.9 %copy-start.7 = (s32[16384]{0:T(1024)S(1)}, s32[16384]{0:T(1024)}, u32[]{:S(2)}) copy-start(s32[16384]{0:T(1024)} %param.15) | copy-start | bytes 196612
  1.4 13.4 %collective-permute-start.12 = (bf16[2,16,384]{2,1,0:T(8,128)(2,1)S(1)}, bf16[2,16,384]{2,1,0:T(8,128)(2,1)S(1)}, u32[]{:S(2)}, u32[]{:S(2)}) collective-permute-start(bf16[2,16,384]{2,1,0:T(8,128)(2,1)S(1)} %get-tuple-element.27), channel_id=1, source_target_pairs={{0,16},{16,32},{32,48},{48,0},{1,17},{17,33},{33,49},{49,1},{2,18}... | collective-permute-start | bytes 73736 | tf_op jit(solution)/shard_map/ppermute | solution.py:325
  3.5 13.0 %collective-permute-start.13 = (bf16[2,16,384]{2,1,0:T(8,128)(2,1)S(1)}, bf16[2,16,384]{2,1,0:T(8,128)(2,1)S(1)}, u32[]{:S(2)}, u32[]{:S(2)}) collective-permute-start(bf16[2,16,384]{2,1,0:T(8,128)(2,1)S(1)} %get-tuple-element.27), channel_id=1, source_target_pairs={{0,32},{16,48},{32,0},{48,16},{1,33},{17,49},{33,1},{49,17},{2,34}... | collective-permute-start | bytes 73736 | tf_op jit(solution)/shard_map/ppermute | solution.py:325
  5.9 17.5 %collective-permute-start.14 = (bf16[2,16,384]{2,1,0:T(8,128)(2,1)S(1)}, bf16[2,16,384]{2,1,0:T(8,128)(2,1)S(1)}, u32[]{:S(2)}, u32[]{:S(2)}) collective-permute-start(bf16[2,16,384]{2,1,0:T(8,128)(2,1)S(1)} %get-tuple-element.27), channel_id=1, source_target_pairs={{0,48},{16,0},{32,16},{48,32},{1,49},{17,1},{33,17},{49,33},{2,50}... | collective-permute-start | bytes 73736 | tf_op jit(solution)/shard_map/ppermute | solution.py:325
  7.1 1.1 copy-start.4
  8.2 1.1 copy-start.5
  9.3 0.8 copy-start.6
  12.7 14.3 %collective-permute-start.20 = (bf16[16,8,640]{2,1,0:T(8,128)(2,1)S(1)}, bf16[16,8,640]{2,1,0:T(8,128)(2,1)S(1)}, u32[]{:S(2)}, u32[]{:S(2)}) collective-permute-start(bf16[16,8,640]{2,1,0:T(8,128)(2,1)S(1)} %bitcast.56), channel_id=1, source_target_pairs={{0,16},{16,32},{32,48},{48,0},{1,17},{17,33},{33,49},{49,1},{2,18}... | collective-permute-start | bytes 491528 | tf_op jit(solution)/shard_map/ppermute | solution.py:325
  13.1 13.9 %collective-permute-start.21 = (bf16[16,8,640]{2,1,0:T(8,128)(2,1)S(1)}, bf16[16,8,640]{2,1,0:T(8,128)(2,1)S(1)}, u32[]{:S(2)}, u32[]{:S(2)}) collective-permute-start(bf16[16,8,640]{2,1,0:T(8,128)(2,1)S(1)} %bitcast.55), channel_id=1, source_target_pairs={{0,32},{16,48},{32,0},{48,16},{1,33},{17,49},{33,1},{49,17},{2,34}... | collective-permute-start | bytes 491528 | tf_op jit(solution)/shard_map/ppermute | solution.py:325
  14.8 12.2 %collective-permute-start.22 = (bf16[16,8,640]{2,1,0:T(8,128)(2,1)S(1)}, bf16[16,8,640]{2,1,0:T(8,128)(2,1)S(1)}, u32[]{:S(2)}, u32[]{:S(2)}) collective-permute-start(bf16[16,8,640]{2,1,0:T(8,128)(2,1)S(1)} %bitcast.54), channel_id=1, source_target_pairs={{0,48},{16,0},{32,16},{48,32},{1,49},{17,1},{33,17},{49,33},{2,50}... | collective-permute-start | bytes 491528 | tf_op jit(solution)/shard_map/ppermute | solution.py:325
  16.5 17.9 %collective-permute-start = (bf16[2,16,640]{2,1,0:T(8,128)(2,1)S(1)}, bf16[2,16,640]{2,1,0:T(8,128)(2,1)S(1)}, u32[]{:S(2)}, u32[]{:S(2)}) collective-permute-start(bf16[2,16,640]{2,1,0:T(8,128)(2,1)S(1)} %get-tuple-element.30), channel_id=1, source_target_pairs={{0,4},{1,5},{2,6},{3,7},{4,0},{5,1},{6,2},{7,3},{8,12},{9,13},{10,... | collective-permute-start | bytes 122888 | tf_op jit(solution)/shard_map/ppermute | solution.py:325
  24.1 37.3 %collective-permute-start.15 = (bf16[4,2,16,384]{3,2,1,0:T(8,128)(2,1)}, bf16[4,2,16,384]{3,2,1,0:T(8,128)(2,1)}, u32[]{:S(2)}, u32[]{:S(2)}) collective-permute-start(bf16[4,2,16,384]{3,2,1,0:T(8,128)(2,1)} %pad_maximum_fusion.5), channel_id=1, source_target_pairs={{0,8},{8,0},{1,9},{9,1},{2,10},{10,2},{3,11},{11,3},{4,12},{12,4},... | collective-permute-start | bytes 294920 | tf_op jit(solution)/shard_map/ppermute | solution.py:325
  27.0 64.1 %copy-start = (bf16[1,2,1024,256]{3,2,1,0:T(8,128)(2,1)S(1)}, bf16[1,2,1024,256]{3,2,1,0:T(8,128)(2,1)}, u32[]{:S(2)}) copy-start(bf16[1,2,1024,256]{3,2,1,0:T(8,128)(2,1)} %param.9) | copy-start | bytes 3145732
  27.0 64.1 %copy-start.3 = (bf16[1,2,256,256]{3,2,1,0:T(8,128)(2,1)S(1)}, bf16[1,2,256,256]{3,2,1,0:T(8,128)(2,1)}, u32[]{:S(2)}) copy-start(bf16[1,2,256,256]{3,2,1,0:T(8,128)(2,1)} %param.11) | copy-start | bytes 786436
  27.0 64.1 %copy-start.8 = (s32[1,4]{1,0:T(1,128)S(1)}, s32[1,4]{1,0:T(1,128)}, u32[]{:S(2)}) copy-start(s32[1,4]{1,0:T(1,128)} %fill.5) | copy-start | bytes 52
  27.0 64.1 %copy-start.9 = (f32[1,2]{1,0:T(1,128)S(1)}, f32[1,2]{1,0:T(1,128)}, u32[]{:S(2)}) copy-start(f32[1,2]{1,0:T(1,128)} %weights.1) | copy-start | bytes 28
  28.0 31.6 %all-to-all-start = ((bf16[16,4,8,640]{3,2,1,0:T(8,128)(2,1)}), bf16[16,4,8,640]{3,2,1,0:T(8,128)(2,1)S(1)}, u32[]{:S(2)}, u32[]{:S(2)}) async-start(bf16[16,4,8,640]{3,2,1,0:T(8,128)(2,1)} %pad_maximum_fusion), calls=%async_computation | async-start | bytes 1310720 | tf_op jit(solution)/shard_map/all_to_all | solution.py:357
  34.3 22.8 %copy-start.11 = (bf16[8,2,16,384]{3,2,1,0:T(8,128)(2,1)}, bf16[8,2,16,384]{3,2,1,0:T(8,128)(2,1)S(1)}, u32[]{:S(2)}) copy-start(bf16[8,2,16,384]{3,2,1,0:T(8,128)(2,1)S(1)} %constant_dynamic-update-slice_fusion.10) | copy-start | bytes 589828
  34.4 17.0 %collective-permute-start.1 = (bf16[2,2,16,640]{3,2,1,0:T(8,128)(2,1)S(1)}, bf16[2,2,16,640]{3,2,1,0:T(8,128)(2,1)S(1)}, u32[]{:S(2)}, u32[]{:S(2)}) collective-permute-start(bf16[2,2,16,640]{3,2,1,0:T(8,128)(2,1)S(1)} %pad_maximum_fusion.6), channel_id=1, source_target_pairs={{0,1},{1,2},{2,3},{3,4},{4,5},{5,6},{6,7},{7,0},{8,9},{9,10},{10,1... | collective-permute-start | bytes 245768 | tf_op jit(solution)/shard_map/ppermute | solution.py:325
  35.8 20.7 %collective-permute-start.6 = (bf16[2,2,16,640]{3,2,1,0:T(8,128)(2,1)S(1)}, bf16[2,2,16,640]{3,2,1,0:T(8,128)(2,1)S(1)}, u32[]{:S(2)}, u32[]{:S(2)}) collective-permute-start(bf16[2,2,16,640]{3,2,1,0:T(8,128)(2,1)S(1)} %pad_maximum_fusion.6), channel_id=1, source_target_pairs={{0,7},{1,0},{2,1},{3,2},{4,3},{5,4},{6,5},{7,6},{8,15},{9,8},{10,9... | collective-permute-start | bytes 245768 | tf_op jit(solution)/shard_map/ppermute | solution.py:325
  37.1 19.3 %collective-permute-start.7 = (bf16[2,2,16,640]{3,2,1,0:T(8,128)(2,1)S(1)}, bf16[2,2,16,640]{3,2,1,0:T(8,128)(2,1)S(1)}, u32[]{:S(2)}, u32[]{:S(2)}) collective-permute-start(bf16[2,2,16,640]{3,2,1,0:T(8,128)(2,1)S(1)} %pad_maximum_fusion.6), channel_id=1, source_target_pairs={{0,2},{1,3},{2,4},{3,5},{4,6},{5,7},{6,0},{7,1},{8,10},{9,11},{10,... | collective-permute-start | bytes 245768 | tf_op jit(solution)/shard_map/ppermute | solution.py:325
  51.4 19.0 %collective-permute-start.2 = (bf16[4,2,16,640]{3,2,1,0:T(8,128)(2,1)S(1)}, bf16[4,2,16,640]{3,2,1,0:T(8,128)(2,1)}, u32[]{:S(2)}, u32[]{:S(2)}) collective-permute-start(bf16[4,2,16,640]{3,2,1,0:T(8,128)(2,1)S(1)} %pad_maximum_fusion.3), channel_id=1, source_target_pairs={{0,16},{16,32},{32,48},{48,0},{1,17},{17,33},{33,49},{49,1},{2,18}... | collective-permute-start | bytes 491528 | tf_op jit(solution)/shard_map/ppermute | solution.py:325
  52.6 24.1 %collective-permute-start.3 = (bf16[4,2,16,640]{3,2,1,0:T(8,128)(2,1)S(1)}, bf16[4,2,16,640]{3,2,1,0:T(8,128)(2,1)}, u32[]{:S(2)}, u32[]{:S(2)}) collective-permute-start(bf16[4,2,16,640]{3,2,1,0:T(8,128)(2,1)S(1)} %pad_maximum_fusion.3), channel_id=1, source_target_pairs={{0,32},{16,48},{32,0},{48,16},{1,33},{17,49},{33,1},{49,17},{2,34}... | collective-permute-start | bytes 491528 | tf_op jit(solution)/shard_map/ppermute | solution.py:325
  57.2 8.7 %collective-permute-start.8 = (bf16[4,2,16,640]{3,2,1,0:T(8,128)(2,1)}, bf16[4,2,16,640]{3,2,1,0:T(8,128)(2,1)}, u32[]{:S(2)}, u32[]{:S(2)}) collective-permute-start(bf16[4,2,16,640]{3,2,1,0:T(8,128)(2,1)} %pad_maximum_fusion.4), channel_id=1, source_target_pairs={{0,8},{8,0},{1,9},{9,1},{2,10},{10,2},{3,11},{11,3},{4,12},{12,4},... | collective-permute-start | bytes 491528 | tf_op jit(solution)/shard_map/ppermute | solution.py:325
  60.7 9.3 %collective-permute-start.23 = (bf16[640,256]{1,0:T(8,128)(2,1)S(1)}, bf16[640,256]{1,0:T(8,128)(2,1)S(1)}, u32[]{:S(2)}, u32[]{:S(2)}) collective-permute-start(bf16[640,256]{1,0:T(8,128)(2,1)S(1)} %get-tuple-element.19), channel_id=1, source_target_pairs={{0,128},{128,0},{1,129},{129,1},{2,130},{130,2},{3,131},{131,3},{4... | collective-permute-start | bytes 983048 | tf_op jit(solution)/shard_map/ppermute | solution.py:325
  61.4 19.2 %collective-permute-start.4 = (bf16[4,2,16,640]{3,2,1,0:T(8,128)(2,1)S(1)}, bf16[4,2,16,640]{3,2,1,0:T(8,128)(2,1)S(1)}, u32[]{:S(2)}, u32[]{:S(2)}) collective-permute-start(bf16[4,2,16,640]{3,2,1,0:T(8,128)(2,1)S(1)} %pad_maximum_fusion.3), channel_id=1, source_target_pairs={{0,48},{16,0},{32,16},{48,32},{1,49},{17,1},{33,17},{49,33},{2,50}... | collective-permute-start | bytes 491528 | tf_op jit(solution)/shard_map/ppermute | solution.py:325
  65.9 16.1 %collective-permute-start.16 = (bf16[8,2,16,384]{3,2,1,0:T(8,128)(2,1)}, bf16[8,2,16,384]{3,2,1,0:T(8,128)(2,1)S(1)}, u32[]{:S(2)}, u32[]{:S(2)}) collective-permute-start(bf16[8,2,16,384]{3,2,1,0:T(8,128)(2,1)} %constant_dynamic-update-slice_fusion.9), channel_id=1, source_target_pairs={{0,4},{1,5},{2,6},{3,7},{4,0},{5,1},{6,2},{7,3},{8,12},{9,13},{10,... | collective-permute-start | bytes 589832 | tf_op jit(solution)/shard_map/ppermute | solution.py:325
  70.0 14.2 %collective-permute-start.10 = (bf16[8,2,16,640]{3,2,1,0:T(8,128)(2,1)S(1)}, bf16[8,2,16,640]{3,2,1,0:T(8,128)(2,1)S(1)}, u32[]{:S(2)}, u32[]{:S(2)}) collective-permute-start(bf16[8,2,16,640]{3,2,1,0:T(8,128)(2,1)S(1)} %constant_dynamic-update-slice_fusion.6.refs_2_), channel_id=1, source_target_pairs={{0,32},{16,48},{32,0},{48,16},{1,33},{17,49},{33,1},{49,17},{2,34}... | collective-permute-start | bytes 983048 | tf_op jit(solution)/shard_map/ppermute | solution.py:325
  70.4 18.9 %collective-permute-start.24 = (bf16[2,640,256]{2,1,0:T(8,128)(2,1)S(1)}, bf16[2,640,256]{2,1,0:T(8,128)(2,1)S(1)}, u32[]{:S(2)}, u32[]{:S(2)}) collective-permute-start(bf16[2,640,256]{2,1,0:T(8,128)(2,1)S(1)} %pad_maximum_fusion.1.own), channel_id=1, source_target_pairs={{0,64},{64,0},{1,65},{65,1},{2,66},{66,2},{3,67},{67,3},{4,68},{68... | collective-permute-start | bytes 1966088 | tf_op jit(solution)/shard_map/ppermute | solution.py:325
  76.7 11.1 %collective-permute-start.11 = (bf16[8,2,16,640]{3,2,1,0:T(8,128)(2,1)S(1)}, bf16[8,2,16,640]{3,2,1,0:T(8,128)(2,1)S(1)}, u32[]{:S(2)}, u32[]{:S(2)}) collective-permute-start(bf16[8,2,16,640]{3,2,1,0:T(8,128)(2,1)S(1)} %constant_dynamic-update-slice_fusion.6.refs_2_), channel_id=1, source_target_pairs={{0,48},{16,0},{32,16},{48,32},{1,49},{17,1},{33,17},{49,33},{2,50}... | collective-permute-start | bytes 983048 | tf_op jit(solution)/shard_map/ppermute | solution.py:325
  80.6 21.8 %collective-permute-start.5 = (bf16[16,2,16,640]{3,2,1,0:T(8,128)(2,1)S(1)}, bf16[16,2,16,640]{3,2,1,0:T(8,128)(2,1)S(1)}, u32[]{:S(2)}, u32[]{:S(2)}) collective-permute-start(bf16[16,2,16,640]{3,2,1,0:T(8,128)(2,1)S(1)} %constant_dynamic-update-slice_fusion.refs_0_), channel_id=1, source_target_pairs={{0,8},{8,0},{1,9},{9,1},{2,10},{10,2},{3,11},{11,3},{4,12},{12,4},... | collective-permute-start | bytes 1966088 | tf_op jit(solution)/shard_map/ppermute | solution.py:325
  83.0 16.8 %collective-permute-start.17 = (bf16[2,8,2,16,384]{4,3,2,1,0:T(8,128)(2,1)S(1)}, bf16[2,8,2,16,384]{4,3,2,1,0:T(8,128)(2,1)S(1)}, u32[]{:S(2)}, u32[]{:S(2)}) collective-permute-start(bf16[2,8,2,16,384]{4,3,2,1,0:T(8,128)(2,1)S(1)} %pad_maximum_fusion.2), channel_id=1, source_target_pairs={{0,1},{1,2},{2,3},{3,4},{4,5},{5,6},{6,7},{7,0},{8,9},{9,10},{10,1... | collective-permute-start | bytes 1179656 | tf_op jit(solution)/shard_map/ppermute | solution.py:325
  84.2 15.5 %collective-permute-start.18 = (bf16[2,8,2,16,384]{4,3,2,1,0:T(8,128)(2,1)S(1)}, bf16[2,8,2,16,384]{4,3,2,1,0:T(8,128)(2,1)S(1)}, u32[]{:S(2)}, u32[]{:S(2)}) collective-permute-start(bf16[2,8,2,16,384]{4,3,2,1,0:T(8,128)(2,1)S(1)} %pad_maximum_fusion.2), channel_id=1, source_target_pairs={{0,7},{1,0},{2,1},{3,2},{4,3},{5,4},{6,5},{7,6},{8,15},{9,8},{10,9... | collective-permute-start | bytes 1179656 | tf_op jit(solution)/shard_map/ppermute | solution.py:325
  87.8 14.6 %collective-permute-start.19 = (bf16[2,8,2,16,384]{4,3,2,1,0:T(8,128)(2,1)S(1)}, bf16[2,8,2,16,384]{4,3,2,1,0:T(8,128)(2,1)S(1)}, u32[]{:S(2)}, u32[]{:S(2)}) collective-permute-start(bf16[2,8,2,16,384]{4,3,2,1,0:T(8,128)(2,1)S(1)} %pad_maximum_fusion.2), channel_id=1, source_target_pairs={{0,2},{1,3},{2,4},{3,5},{4,6},{5,7},{6,0},{7,1},{8,10},{9,11},{10,... | collective-permute-start | bytes 1179656 | tf_op jit(solution)/shard_map/ppermute | solution.py:325
  89.3 10.4 %collective-permute-start.9 = (bf16[8,2,16,640]{3,2,1,0:T(8,128)(2,1)S(1)}, bf16[8,2,16,640]{3,2,1,0:T(8,128)(2,1)S(1)}, u32[]{:S(2)}, u32[]{:S(2)}) collective-permute-start(bf16[8,2,16,640]{3,2,1,0:T(8,128)(2,1)S(1)} %constant_dynamic-update-slice_fusion.6.refs_2_), channel_id=1, source_target_pairs={{0,16},{16,32},{32,48},{48,0},{1,17},{17,33},{33,49},{49,1},{2,18}... | collective-permute-start | bytes 983048 | tf_op jit(solution)/shard_map/ppermute | solution.py:325
  102.4 0.9 copy-start.10
  103.3 32.6 %copy-start.1 = (bf16[1,2,1024,256]{3,2,1,0:T(8,128)(2,1)S(1)}, bf16[1,2,1024,256]{3,2,1,0:T(8,128)(2,1)}, u32[]{:S(2)}) copy-start(bf16[1,2,1024,256]{3,2,1,0:T(8,128)(2,1)} %param.9) | copy-start | bytes 3145732
  128.8 15.9 %all-to-all-start.2 = ((f32[16,8,128]{2,1,0:T(8,128)}), f32[16,8,128]{2,1,0:T(8,128)S(1)}, u32[]{:S(2)}, u32[]{:S(2)}) async-start(f32[16,8,128]{2,1,0:T(8,128)} %turn.1), calls=%async_computation.2 | async-start | bytes 131072 | tf_op jit(solution)/shard_map/all_to_all | solution.py:368
  135.9 1.2 copy-start.2

commit v3 on v2

--- a/solution.py
+++ b/solution.py
@@ -19,16 +19,14 @@
 ROWS = 1280
 QUARTER = ROWS // POLES
 SHARD = ANC // GROUPS
-LATE = 384
-EARLY = ANC - LATE
-VMEM_LIMIT = 50 * 1024 * 1024
+MIB = 1024 * 1024
 SMEM_SPEC = pl.BlockSpec(memory_space=pltpu.SMEM)
 VMEM_SPEC = pl.BlockSpec(memory_space=pltpu.VMEM)
-ANY_SPEC = pl.BlockSpec(memory_space=pl.ANY)
-
-
-def params():
-    return pltpu.CompilerParams(vmem_limit_bytes=VMEM_LIMIT)
+HBM_SPEC = pl.BlockSpec(memory_space=pltpu.HBM)
+
+
+def params(mib=16):
+    return pltpu.CompilerParams(vmem_limit_bytes=mib * MIB)
 
 
 def mm(a, b, contract=((1,), (0,))):
@@ -91,12 +89,12 @@
 def pack(index, dft, margin, hamiltonian):
     return pl.pallas_call(
         pack_kernel,
-        in_specs=[SMEM_SPEC, VMEM_SPEC, ANY_SPEC, ANY_SPEC],
+        in_specs=[SMEM_SPEC, VMEM_SPEC, HBM_SPEC, HBM_SPEC],
         out_specs=[VMEM_SPEC] * (NX + 1),
         out_shape=[jax.ShapeDtypeStruct((PLANE * CAP, 2 * QUARTER), BF16)] * NX
         + [jax.ShapeDtypeStruct((SLOTS, COLS), BF16)],
         scratch_shapes=[pltpu.VMEM((2 * QUARTER, COLS), BF16), pltpu.SemaphoreType.DMA((2,))],
-        compiler_params=params(),
+        compiler_params=params(62),
         name="pack",
     )(index, dft, margin, hamiltonian)
 
@@ -165,14 +163,12 @@
             jax.ShapeDtypeStruct((8, COLS), F32),
         ],
         scratch_shapes=[pltpu.VMEM((2, ROWS, COLS), BF16), pltpu.VMEM((2, ANC, COLS), BF16)],
-        compiler_params=params(),
+        compiler_params=params(24),
         name="factors",
     )(index, weights, fill, lower, diag_inverse, own, mates)
 
 
-def upper_kernel(index, fill, lower, *refs):
-    early, late, (factor, base, onehot, out, slots, both, real_sum, imag_sum) = refs[:6], refs[6:10], refs[10:]
-    first, first_y, second, second_x1, second_x2, second_x3 = early
+def upper_kernel(index, fill, lower, first, first_y, second, second_1, second_2, second_3, factor, base, onehot, out, slots, both):
     grid = index[1]
     x, y, z = grid >> 4, (grid >> 3) & 1, grid & 7
     for block in range(ANC // COLS):
@@ -181,38 +177,24 @@
         for part in range(2):
             both[span, part * COLS : (part + 1) * COLS] = lower[part, span, :] * keep
 
-    def product(ref, rhs):
-        left, right = [mm(ref[:, part].reshape(-1, ref.shape[-1]), rhs) for part in range(2)]
-        return right[:, COLS:] - left[:, :COLS], -left[:, COLS:] - right[:, :COLS]
-
-    def start_of(dx, dy, dz):
-        px, py, pz = (x - dx) & (NX - 1), (y - dy) & (NY - 1), (z - dz) & (NZ - 1)
-        return pl.multiple_of(((px * NY + py) * NZ + pz) * SHARD, SHARD)
-
-    def scatter(ref, places):
-        real, imag = product(ref, both[0:EARLY, :])
-        for n, place in enumerate(places):
+    def scatter(refs, places):
+        rhs = both[...]
+        left, right = [
+            mm(jnp.concatenate([ref[:, part].reshape(-1, ANC) for ref in refs], axis=0), rhs) for part in range(2)
+        ]
+        for n, (dx, dy, dz) in enumerate(places):
+            px, py, pz = (x - dx) & (NX - 1), (y - dy) & (NY - 1), (z - dz) & (NZ - 1)
+            here = pl.ds(pl.multiple_of(((px * NY + py) * NZ + pz) * SHARD, SHARD), SHARD)
+            keep = fill[0, px].astype(F32)
             span = slice(n * SHARD, (n + 1) * SHARD)
-            start = start_of(*place)
-            real_sum[pl.ds(start, SHARD), :] = real[span]
-            imag_sum[pl.ds(start, SHARD), :] = imag[span]
+            out[0, here, :] = ((right[span, COLS:] - left[span, :COLS]) * keep).astype(BF16)
+            out[1, here, :] = ((-left[span, COLS:] - right[span, :COLS]) * keep).astype(BF16)
 
     for dy, ref in ((0, first), (1, first_y)):
-        scatter(ref, [(dx, dy, dz) for dx in range(NX) for dz in (0, 4, 1, 5)])
-    for dx, ref in enumerate((second, second_x1, second_x2, second_x3)):
-        scatter(ref, [(dx, dy, dz) for dy in range(NY) for dz in (7, 3, 2, 6)])
+        scatter([ref], [(dx, dy, dz) for dx in range(NX) for dz in (0, 4, 1, 5)])
+    for dx, refs in ((0, (second, second_1)), (2, (second_2, second_3))):
+        scatter(refs, [(dx + n, dy, dz) for n in range(2) for dy in range(NY) for dz in (7, 3, 2, 6)])
     rows = [base[which : which + 1, :] for which in range(2)]
-    tail = both[EARLY:ANC, :]
-    for n, dzs in enumerate(((0, 4), (1, 5), (7, 3), (2, 6))):
-        real, imag = product(late[n], tail)
-        places = [(dx, dy, dz) for dz in dzs for dy in range(NY) for dx in range(NX)]
-        for m, place in enumerate(places):
-            span = slice(m * SHARD, (m + 1) * SHARD)
-            start = start_of(*place)
-            keep = fill[0, (x - place[0]) & (NX - 1)].astype(F32)
-            here = pl.ds(start, SHARD)
-            out[0, here, :] = ((real[span] + real_sum[here, :]) * keep).astype(BF16)
-            out[1, here, :] = ((imag[span] + imag_sum[here, :]) * keep).astype(BF16)
     for block in range(ANC // COLS):
         span = slice(block * COLS, (block + 1) * COLS)
         real, imag = out[0, span, :].astype(F32), out[1, span, :].astype(F32)
@@ -228,23 +210,19 @@
             slots[pole * NX + px] = sums[:, px * width : (px + 1) * width]
 
 
-def upper_rows(index, fill, lower, early, late, factor, base, onehot):
+def upper_rows(index, fill, lower, pieces, factor, base, onehot):
     return pl.pallas_call(
         upper_kernel,
-        in_specs=[SMEM_SPEC] * 2 + [VMEM_SPEC] * (4 + len(early) + len(late)),
+        in_specs=[SMEM_SPEC] * 2 + [VMEM_SPEC] * (4 + len(pieces)),
         out_specs=[VMEM_SPEC] * 2,
         out_shape=[
             jax.ShapeDtypeStruct((2, ANC, COLS), BF16),
             jax.ShapeDtypeStruct((POLES * NX, 8, PLANE * CAP), F32),
         ],
-        scratch_shapes=[
-            pltpu.VMEM((ANC, 2 * COLS), BF16),
-            pltpu.VMEM((ANC, COLS), F32),
-            pltpu.VMEM((ANC, COLS), F32),
-        ],
-        compiler_params=params(),
+        scratch_shapes=[pltpu.VMEM((ANC, 2 * COLS), BF16)],
+        compiler_params=params(28),
         name="upper",
-    )(index, fill, lower, *early, *late, factor, base, onehot)
+    )(index, fill, lower, *pieces, factor, base, onehot)
 
 
 def diag_kernel(fill, lower, upper, diag_inverse, out):
@@ -335,33 +313,36 @@
     grid = (lax.axis_index("x") * NY + lax.axis_index("yhi")) * NZ + lax.axis_index("z")
     index = jnp.stack([pole, grid]).astype(I32)
     lower, inverse = lower_panels[0], diag_inverse[0]
-    early, late = ainv_anc[0, :, :, :EARLY], ainv_anc[0, :, :, EARLY:]
-
-    near, near_up, near_down, near_two = all_of_z(early)
+    shard = ainv_anc[0]
+
+    near, near_up, near_down, near_two = all_of_z(shard)
     first = jnp.concatenate([near, near_up])
     second = jnp.concatenate([near_down, near_two])
-    first = jnp.concatenate([first] + [shift(first, "x", d) for d in (1, 2, 3)])
-    second = jnp.concatenate([second, shift(second, "yhi", 1)])
+    first_1, first_2, first_3 = [shift(first, "x", d) for d in (1, 2, 3)]
+    second_y = shift(second, "yhi", 1)
+    first, second_y = lax.optimization_barrier((first, second_y))
+    first = jnp.concatenate([first, first_1, first_2, first_3])
+    second = jnp.concatenate([second, second_y])
     first_y = shift(first, "yhi", 1)
     second_x = [shift(second, "x", d) for d in (1, 2, 3)]
 
-    late = jnp.stack([late] + [shift(late, "x", d) for d in (1, 2, 3)])
-    late = jnp.concatenate([late, shift(late, "yhi", 1)])
-    late = [value.reshape(2 * NX * NY, 2, SHARD, LATE) for value in all_of_z(late)]
-
     table = dft_column.reshape(128, 128)
+    table, near = lax.optimization_barrier((table, near))
     packed = pack(index, table, margin, hamiltonian)
     slot_onehot = packed[NX]
     packed = [value.reshape(PLANE, CAP, 2 * QUARTER) for value in packed[:NX]]
     outgoing = jnp.stack([packed[0]] + [shift(packed[d], "x", d) for d in (1, 2, 3)], axis=1)
+    outgoing, near_up, near_down, near_two = lax.optimization_barrier((outgoing, near_up, near_down, near_two))
     arrived = lax.all_to_all(outgoing, ("yhi", "z"), split_axis=0, concat_axis=0, tiled=True)
     mine, column_onehot = unpack(index, table, arrived.reshape(SLOTS, 2 * QUARTER))
     mine = jnp.stack([mine, shift(mine, "ylo", 1)])
     mates = shift(mine, "core", 1)
+    second_1, second_2, second_3 = second_x
+    mates, second_1, second_2, second_3 = lax.optimization_barrier((mates, second_1, second_2, second_3))
     factor, base = factors(index, pole_weights, fill_pattern, lower, inverse, mine, mates)
 
     upper, slots = upper_rows(
-        index, fill_pattern, lower, [first, first_y, second] + second_x, late, factor, base, column_onehot
+        index, fill_pattern, lower, [first, first_y, second] + second_x, factor, base, column_onehot
     )
     diag = diag_block(fill_pattern, lower, upper, inverse)
     sums = lax.all_to_all(slots, ("ylo", "core", "x"), split_axis=0, concat_axis=0, tiled=True)

time: 146 us -> 131 us (0.90)
  waiting for transfers between devices: 28.6 us -> 47.7 us
  starting transfers between devices: 65.8 us -> 50.4 us
  blocking collectives: 17.4 us -> 8.78 us
  local copies, waits for them, and re-layouts: 11.7 us -> 5.7 us
  Pallas kernels: 17.7 us -> 13.6 us
    ppermute x25 -> x17, waiting for transfers between devices: 23.1 us -> 39.6 us  [shift(): lax.ppermute(value, axis, [(n, (n + by) % size) for n in range(size)])]
    ppermute x25 -> x17, starting transfers between devices: 52.5 us -> 36.6 us  [shift(): lax.ppermute(value, axis, [(n, (n + by) % size) for n in range(size)])]
    all_to_all x1, blocking collectives: 17.4 us -> 8.78 us  [body(): lax.all_to_all(slots, ('ylo', 'core', 'x'), split_axis=0, concat_axis=0,...]
    unnamed x33 -> x25, local copies, waits for them, and re-layouts: 7.08 us -> 3.19 us
    pallas_call x1, Pallas kernels: 7.4 us -> 4.55 us  [upper_rows(): pl.pallas_call(upper_kernel, in_specs=[SMEM_SPEC] * 2 + [VMEM_SPEC] * (4...]
    all_to_all x1, waiting for transfers between devices: 0.01 us -> 2.53 us  [body(): lax.all_to_all(outgoing, ('yhi', 'z'), split_axis=0, concat_axis=0, tiled...]
    pallas_call x1, Pallas kernels: 3.52 us -> 1.54 us  [factors(): pl.pallas_call(factor_kernel, in_specs=[SMEM_SPEC] * 3 + [VMEM_SPEC] * 4,...]
    all_to_all x1, starting transfers between devices: 6.3 us -> 8.23 us  [body(): lax.all_to_all(outgoing, ('yhi', 'z'), split_axis=0, concat_axis=0, tiled...]
  transfers between devices with their start and end apart: 27 -> 19, of which waited for: 5 -> 12; matrix products, arithmetic and copies ran while one was open for 6% -> 5% of each run, Pallas kernels for 6% -> 4%
where the time goes in v3:
time: 131 us; the launch traced here: 130 us
  starting transfers between devices  50.4 us (38%)
  waiting for transfers between devices  47.7 us (36%)
  Pallas kernels  13.6 us (10%)
  blocking collectives  8.78 us (7%)
  local copies, waits for them, and re-layouts  5.7 us (4%)
  other arithmetic  3.48 us (3%)
    ppermute x17, waiting for transfers between devices, shift(): lax.ppermute(value, axis, [(n, (n + by) % size) for n in range(size)])  39.6 us
    ppermute x17, starting transfers between devices, shift(): lax.ppermute(value, axis, [(n, (n + by) % size) for n in range(size)])  36.6 us
    all_to_all x1, blocking collectives, body(): lax.all_to_all(slots, ('ylo', 'core', 'x'), split_axis=0, concat_axis=0,...  8.78 us
    all_to_all x1, starting transfers between devices, body(): lax.all_to_all(outgoing, ('yhi', 'z'), split_axis=0, concat_axis=0, tiled...  8.23 us
    all_to_all x1, starting transfers between devices, body(): lax.all_to_all(turn(sums), ('yhi', 'z'), split_axis=0, concat_axis=0, til...  5.56 us
    all_to_all x1, waiting for transfers between devices, body(): lax.all_to_all(turn(sums), ('yhi', 'z'), split_axis=0, concat_axis=0, til...  5.55 us
    pallas_call x1, Pallas kernels, upper_rows(): pl.pallas_call(upper_kernel, in_specs=[SMEM_SPEC] * 2 + [VMEM_SPEC] * (4...  4.55 us
    pallas_call x1, Pallas kernels, pack(): pl.pallas_call(pack_kernel, in_specs=[SMEM_SPEC, VMEM_SPEC, HBM_SPEC, HBM...  3.26 us
  transfers between devices with their start and end apart: 19, of which 12 were waited for; matrix products, arithmetic and copies ran while one was open for 5% of the time, Pallas kernels for 4%

profile of v3, /device:TPU:1, one launch (start us, length us, event | category | flops | bytes accessed | tf_op | source)
XLA Modules:
  0.0 130.5 jit_solution(2645944240281277711)
XLA Ops:
  0.6 0.0 copy-start.9
  0.6 0.0 copy-start.3
  0.7 7.8 %collective-permute-start = (bf16[2,16,1024]{2,1,0:T(8,128)(2,1)}, bf16[2,16,1024]{2,1,0:T(8,128)(2,1)S(1)}, u32[]{:S(2)}, u32[]{:S(2)}) collective-permute-start(bf16[2,16,1024]{2,1,0:T(8,128)(2,1)} %bitcast.34), channel_id=1, source_target_pairs={{0,4},{1,5},{2,6},{3,7},{4,0},{5,1},{6,2},{7,3},{8,12},{9,13},{10,... | collective-permute-start | bytes 196616 | tf_op jit(solution)/shard_map/ppermute | solution.py:303
  8.5 0.6 pad_add_fusion.index
  9.0 1.4 %collective-permute-done = bf16[2,16,1024]{2,1,0:T(8,128)(2,1)S(1)} collective-permute-done((bf16[2,16,1024]{2,1,0:T(8,128)(2,1)}, bf16[2,16,1024]{2,1,0:T(8,128)(2,1)S(1)}, u32[]{:S(2)}, u32[]{:S(2)}) %collective-permute-start) | collective-permute-done | bytes 65568 | tf_op jit(solution)/shard_map/ppermute | solution.py:303
  10.4 0.9 pad_maximum_fusion.4
  11.3 3.3 %pack.1 = (bf16[128,640]{1,0:T(8,128)(2,1)}, bf16[128,640]{1,0:T(8,128)(2,1)}, bf16[128,640]{1,0:T(8,128)(2,1)}, bf16[128,640]{1,0:T(8,128)(2,1)}, bf16[512,256]{1,0:T(8,128)(2,1)}) custom-call(s32[2]{0:T(128)} %pad_add_fusion.index, s32[128,128]{1,0:T(8,128)} %bitcast.31, bf16[1280,256]{1,0:T(8,128)(2,1)} %margin.1, bf16[1280,256]{1,0:T(8,128)(2,1)} %hamiltonian.1), custom_call_target="tpu_custom_call" | custom-call | tf_op jit(solution)/shard_map/pack/pallas_call | solution.py:90
  14.6 1.3 collective-permute-start.12
  15.9 2.4 %collective-permute-start.13 = (bf16[16,8,640]{2,1,0:T(8,128)(2,1)}, bf16[16,8,640]{2,1,0:T(8,128)(2,1)S(1)}, u32[]{:S(2)}, u32[]{:S(2)}) collective-permute-start(bf16[16,8,640]{2,1,0:T(8,128)(2,1)} %bitcast.45), channel_id=1, source_target_pairs={{0,32},{16,48},{32,0},{48,16},{1,33},{17,49},{33,1},{49,17},{2,34}... | collective-permute-start | bytes 491528 | tf_op jit(solution)/shard_map/ppermute | solution.py:303
  18.3 1.2 collective-permute-start.14
  19.5 4.4 %collective-permute-start.2 = (bf16[2,2,16,1024]{3,2,1,0:T(8,128)(2,1)S(1)}, bf16[2,2,16,1024]{3,2,1,0:T(8,128)(2,1)S(1)}, u32[]{:S(2)}, u32[]{:S(2)}) collective-permute-start(bf16[2,2,16,1024]{3,2,1,0:T(8,128)(2,1)S(1)} %pad_maximum_fusion.4), channel_id=1, source_target_pairs={{0,7},{1,0},{2,1},{3,2},{4,3},{5,4},{6,5},{7,6},{8,15},{9,8},{10,9... | collective-permute-start | bytes 393224 | tf_op jit(solution)/shard_map/ppermute | solution.py:303
  23.9 0.3 collective-permute-done.13
  24.3 2.0 %pad_maximum_fusion = bf16[16,4,8,640]{3,2,1,0:T(8,128)(2,1)} fusion(bf16[16,1,8,640]{3,2,1,0:T(8,128)(2,1)S(1)} %bitcast.41, bf16[16,1,8,640]{3,2,1,0:T(8,128)(2,1)S(1)} %bitcast.40, bf16[16,1,8,640]{3,2,1,0:T(8,128)(2,1)S(1)} %bitcast.39, bf16[16,1,8,640]{3,2,1,0:T(8,128)(2,1)} %bitcast.38), kind=kLoop, calls=%fused_computation | loop fusion | flops 983040 | bytes 1310720 | tf_op jit(solution)/shard_map/stack | solution.py:334
  26.2 4.4 %collective-permute-done.3 = bf16[2,2,16,1024]{3,2,1,0:T(8,128)(2,1)S(1)} collective-permute-done((bf16[2,2,16,1024]{3,2,1,0:T(8,128)(2,1)S(1)}, bf16[2,2,16,1024]{3,2,1,0:T(8,128)(2,1)S(1)}, u32[]{:S(2)}, u32[]{:S(2)}) %collective-permute-start.3) | collective-permute-done | bytes 131104 | tf_op jit(solution)/shard_map/ppermute | solution.py:303
  30.7 0.7 collective-permute-done.1
  31.3 8.2 %all-to-all-start = ((bf16[16,4,8,640]{3,2,1,0:T(8,128)(2,1)}), bf16[16,4,8,640]{3,2,1,0:T(8,128)(2,1)S(1)}, u32[]{:S(2)}, u32[]{:S(2)}) async-start(bf16[16,4,8,640]{3,2,1,0:T(8,128)(2,1)} %pad_maximum_fusion), calls=%async_computation | async-start | bytes 1310720 | tf_op jit(solution)/shard_map/all_to_all | solution.py:336
  39.6 3.0 %collective-permute-start.4 = (bf16[4,2,16,1024]{3,2,1,0:T(8,128)(2,1)S(1)}, bf16[4,2,16,1024]{3,2,1,0:T(8,128)(2,1)}, u32[]{:S(2)}, u32[]{:S(2)}) collective-permute-start(bf16[4,2,16,1024]{3,2,1,0:T(8,128)(2,1)S(1)} %pad_maximum_fusion.3), channel_id=1, source_target_pairs={{0,8},{8,0},{1,9},{9,1},{2,10},{10,2},{3,11},{11,3},{4,12},{12,4},... | collective-permute-start | bytes 786440 | tf_op jit(solution)/shard_map/ppermute | solution.py:303
  42.6 0.4 collective-permute-start.5
  43.0 1.0 collective-permute-start.6
  44.0 1.5 %collective-permute-start.7 = (bf16[4,2,16,1024]{3,2,1,0:T(8,128)(2,1)S(1)}, bf16[4,2,16,1024]{3,2,1,0:T(8,128)(2,1)}, u32[]{:S(2)}, u32[]{:S(2)}) collective-permute-start(bf16[4,2,16,1024]{3,2,1,0:T(8,128)(2,1)S(1)} %pad_maximum_fusion.2), channel_id=1, source_target_pairs={{0,48},{16,0},{32,16},{48,32},{1,49},{17,1},{33,17},{49,33},{2,50}... | collective-permute-start | bytes 786440 | tf_op jit(solution)/shard_map/ppermute | solution.py:303
  45.5 4.7 %collective-permute-done.4 = bf16[4,2,16,1024]{3,2,1,0:T(8,128)(2,1)} collective-permute-done((bf16[4,2,16,1024]{3,2,1,0:T(8,128)(2,1)S(1)}, bf16[4,2,16,1024]{3,2,1,0:T(8,128)(2,1)}, u32[]{:S(2)}, u32[]{:S(2)}) %collective-permute-start.4) | collective-permute-done | bytes 262176 | tf_op jit(solution)/shard_map/ppermute | solution.py:303
  50.2 2.7 %collective-permute-done.5 = bf16[4,2,16,1024]{3,2,1,0:T(8,128)(2,1)S(1)} collective-permute-done((bf16[4,2,16,1024]{3,2,1,0:T(8,128)(2,1)S(1)}, bf16[4,2,16,1024]{3,2,1,0:T(8,128)(2,1)S(1)}, u32[]{:S(2)}, u32[]{:S(2)}) %collective-permute-start.5) | collective-permute-done | bytes 262176 | tf_op jit(solution)/shard_map/ppermute | solution.py:303
  52.9 2.5 %all-to-all-done = bf16[16,4,8,640]{3,2,1,0:T(8,128)(2,1)S(1)} async-done(((bf16[16,4,8,640]{3,2,1,0:T(8,128)(2,1)}), bf16[16,4,8,640]{3,2,1,0:T(8,128)(2,1)S(1)}, u32[]{:S(2)}, u32[]{:S(2)}) %all-to-all-start) | async-done | bytes 655392 | tf_op jit(solution)/shard_map/all_to_all | solution.py:336
  55.5 1.1 unpack.1
  56.6 0.8 collective-permute-start.15
  57.4 1.0 constant_dynamic-update-slice_fusion.1
  58.3 1.0 constant_dynamic-update-slice_fusion.first
  59.3 0.8 collective-permute-start.8
  60.2 0.9 constant_dynamic-update-slice_fusion.6
  61.1 1.5 %collective-permute-done.15 = bf16[640,256]{1,0:T(8,128)(2,1)S(1)} collective-permute-done((bf16[640,256]{1,0:T(8,128)(2,1)S(1)}, bf16[640,256]{1,0:T(8,128)(2,1)S(1)}, u32[]{:S(2)}, u32[]{:S(2)}) %collective-permute-start.15) | collective-permute-done | bytes 327712 | tf_op jit(solution)/shard_map/ppermute | solution.py:303
  62.6 0.1 pad_maximum_fusion.1.own
  62.7 9.2 %collective-permute-start.16 = (bf16[2,640,256]{2,1,0:T(8,128)(2,1)S(1)}, bf16[2,640,256]{2,1,0:T(8,128)(2,1)S(1)}, u32[]{:S(2)}, u32[]{:S(2)}) collective-permute-start(bf16[2,640,256]{2,1,0:T(8,128)(2,1)S(1)} %pad_maximum_fusion.1.own), channel_id=1, source_target_pairs={{0,64},{64,0},{1,65},{65,1},{2,66},{66,2},{3,67},{67,3},{4,68},{68... | collective-permute-start | bytes 1966088 | tf_op jit(solution)/shard_map/ppermute | solution.py:303
  71.9 1.0 constant_dynamic-update-slice_fusion.4.second
  72.9 0.3 collective-permute-start.10
  73.2 2.5 %collective-permute-start.11 = (bf16[8,2,16,1024]{3,2,1,0:T(8,128)(2,1)S(1)}, bf16[8,2,16,1024]{3,2,1,0:T(8,128)(2,1)S(1)}, u32[]{:S(2)}, u32[]{:S(2)}) collective-permute-start(bf16[8,2,16,1024]{3,2,1,0:T(8,128)(2,1)S(1)} %constant_dynamic-update-slice_fusion.4.second), channel_id=1, source_target_pairs={{0,48},{16,0},{32,16},{48,32},{1,49},{17,1},{33,17},{49,33},{2,50}... | collective-permute-start | bytes 1572872 | tf_op jit(solution)/shard_map/ppermute | solution.py:303
  75.7 12.4 %collective-permute-done.10.second_2 = bf16[8,2,16,1024]{3,2,1,0:T(8,128)(2,1)S(1)} collective-permute-done((bf16[8,2,16,1024]{3,2,1,0:T(8,128)(2,1)S(1)}, bf16[8,2,16,1024]{3,2,1,0:T(8,128)(2,1)S(1)}, u32[]{:S(2)}, u32[]{:S(2)}) %collective-permute-start.10) | collective-permute-done | bytes 524320 | tf_op jit(solution)/shard_map/ppermute | solution.py:303
  88.0 8.9 %collective-permute-done.11.second_3 = bf16[8,2,16,1024]{3,2,1,0:T(8,128)(2,1)S(1)} collective-permute-done((bf16[8,2,16,1024]{3,2,1,0:T(8,128)(2,1)S(1)}, bf16[8,2,16,1024]{3,2,1,0:T(8,128)(2,1)S(1)}, u32[]{:S(2)}, u32[]{:S(2)}) %collective-permute-start.11) | collective-permute-done | bytes 524320 | tf_op jit(solution)/shard_map/ppermute | solution.py:303
  97.0 2.6 %collective-permute-done.9.second_1 = bf16[8,2,16,1024]{3,2,1,0:T(8,128)(2,1)S(1)} collective-permute-done((bf16[8,2,16,1024]{3,2,1,0:T(8,128)(2,1)S(1)}, bf16[8,2,16,1024]{3,2,1,0:T(8,128)(2,1)S(1)}, u32[]{:S(2)}, u32[]{:S(2)}) %collective-permute-start.9) | collective-permute-done | bytes 524320 | tf_op jit(solution)/shard_map/ppermute | solution.py:303
  99.6 1.5 %factors.1 = (f32[4,1024,256]{2,1,0:T(8,128)S(1)}, f32[8,256]{1,0:T(8,128)S(1)}) custom-call(s32[2]{0:T(128)S(1)} %copy-done.5, f32[1,2]{1,0:T(1,128)S(1)} %copy-done.7, s32[1,4]{1,0:T(1,128)S(1)} %copy-done.6, bf16[2,1024,256]{2,1,0:T(8,128)(2,1)S(1)} %bitcast.23, bf16[2,256,256]{2,1,0:T(8,128)(2,1)S(1)} %bitcast.28, ...), custom_call_target="tpu_custom_call" | custom-call | tf_op jit(solution)/shard_map/factors/pallas_call | solution.py:157
  101.1 4.5 %upper.1 = (bf16[2,1024,256]{2,1,0:T(8,128)(2,1)}, f32[16,8,128]{2,1,0:T(8,128)S(1)}) custom-call(s32[2]{0:T(128)S(1)} %copy-done.5, s32[1,4]{1,0:T(1,128)S(1)} %copy-done.6, bf16[2,1024,256]{2,1,0:T(8,128)(2,1)S(1)} %bitcast.24, bf16[16,2,16,1024]{3,2,1,0:T(8,128)(2,1)S(1)} %constant_dynamic-update-slice_fusion.first, ...), custom_call_target="tpu_custom_call" | custom-call | tf_op jit(solution)/shard_map/upper/pallas_call | solution.py:214
  105.7 8.8 %all_to_all.15.arrived = f32[16,8,128]{2,1,0:T(8,128)S(1)} all-to-all(f32[16,8,128]{2,1,0:T(8,128)S(1)} %get-tuple-element.34), channel_id=1, replica_groups=mesh['ylo'=2,'core'=2,'x'=4,'yhi'=2,'z'=8] {'ylo','core','x'}, dimensions={0} | all-to-all | bytes 131072 | tf_op jit(solution)/shard_map/all_to_all | solution.py:348
  114.5 0.7 turn.1
  115.2 5.6 %all-to-all-start.2 = ((f32[16,8,128]{2,1,0:T(8,128)}), f32[16,8,128]{2,1,0:T(8,128)S(1)}, u32[]{:S(2)}, u32[]{:S(2)}) async-start(f32[16,8,128]{2,1,0:T(8,128)} %turn.1), calls=%async_computation.2 | async-start | bytes 131072 | tf_op jit(solution)/shard_map/all_to_all | solution.py:349
  120.8 1.2 copy-done.1
  122.0 2.1 %diag.1 = bf16[2,256,256]{2,1,0:T(8,128)(2,1)} custom-call(s32[1,4]{1,0:T(1,128)S(1)} %copy-done.6, bf16[2,1024,256]{2,1,0:T(8,128)(2,1)S(1)} %bitcast.25, bf16[2,1024,256]{2,1,0:T(8,128)(2,1)S(1)} %copy-done.1, bf16[2,256,256]{2,1,0:T(8,128)(2,1)S(1)} %bitcast.29), custom_call_target="tpu_custom_call" | custom-call | tf_op jit(solution)/shard_map/diag/pallas_call | solution.py:244
  124.1 5.6 %all-to-all-done.2.arrived = f32[16,8,128]{2,1,0:T(8,128)S(1)} async-done(((f32[16,8,128]{2,1,0:T(8,128)}), f32[16,8,128]{2,1,0:T(8,128)S(1)}, u32[]{:S(2)}, u32[]{:S(2)}) %all-to-all-start.2) | async-done | bytes 65568 | tf_op jit(solution)/shard_map/all_to_all | solution.py:349
  129.6 0.3 place.1
  129.9 0.6 fusion
  (32 shorter events, 0.2 us)
Async XLA Ops:
  0.6 41.9 %copy-start.9 = (bf16[1,2,16,1024]{3,2,1,0:T(8,128)(2,1)S(1)}, bf16[1,2,16,1024]{3,2,1,0:T(8,128)(2,1)}, u32[]{:S(2)}) copy-start(bf16[1,2,16,1024]{3,2,1,0:T(8,128)(2,1)} %param.8) | copy-start | bytes 196612
  0.6 54.8 %copy-start.3 = (s32[16384]{0:T(1024)S(1)}, s32[16384]{0:T(1024)}, u32[]{:S(2)}) copy-start(s32[16384]{0:T(1024)} %param.15) | copy-start | bytes 196612
  0.7 9.8 %collective-permute-start = (bf16[2,16,1024]{2,1,0:T(8,128)(2,1)}, bf16[2,16,1024]{2,1,0:T(8,128)(2,1)S(1)}, u32[]{:S(2)}, u32[]{:S(2)}) collective-permute-start(bf16[2,16,1024]{2,1,0:T(8,128)(2,1)} %bitcast.34), channel_id=1, source_target_pairs={{0,4},{1,5},{2,6},{3,7},{4,0},{5,1},{6,2},{7,3},{8,12},{9,13},{10,... | collective-permute-start | bytes 196616 | tf_op jit(solution)/shard_map/ppermute | solution.py:303
  9.0 46.4 %copy-start.5 = (s32[2]{0:T(128)S(1)}, s32[2]{0:T(128)}, u32[]{:S(2)}) copy-start(s32[2]{0:T(128)} %pad_add_fusion.index) | copy-start | bytes 28
  14.6 9.3 %collective-permute-start.12 = (bf16[16,8,640]{2,1,0:T(8,128)(2,1)}, bf16[16,8,640]{2,1,0:T(8,128)(2,1)S(1)}, u32[]{:S(2)}, u32[]{:S(2)}) collective-permute-start(bf16[16,8,640]{2,1,0:T(8,128)(2,1)} %bitcast.46), channel_id=1, source_target_pairs={{0,16},{16,32},{32,48},{48,0},{1,17},{17,33},{33,49},{49,1},{2,18}... | collective-permute-start | bytes 491528 | tf_op jit(solution)/shard_map/ppermute | solution.py:303
  15.9 8.4 %collective-permute-start.13 = (bf16[16,8,640]{2,1,0:T(8,128)(2,1)}, bf16[16,8,640]{2,1,0:T(8,128)(2,1)S(1)}, u32[]{:S(2)}, u32[]{:S(2)}) collective-permute-start(bf16[16,8,640]{2,1,0:T(8,128)(2,1)} %bitcast.45), channel_id=1, source_target_pairs={{0,32},{16,48},{32,0},{48,16},{1,33},{17,49},{33,1},{49,17},{2,34}... | collective-permute-start | bytes 491528 | tf_op jit(solution)/shard_map/ppermute | solution.py:303
  18.3 5.9 %collective-permute-start.14 = (bf16[16,8,640]{2,1,0:T(8,128)(2,1)}, bf16[16,8,640]{2,1,0:T(8,128)(2,1)S(1)}, u32[]{:S(2)}, u32[]{:S(2)}) collective-permute-start(bf16[16,8,640]{2,1,0:T(8,128)(2,1)} %bitcast.44), channel_id=1, source_target_pairs={{0,48},{16,0},{32,16},{48,32},{1,49},{17,1},{33,17},{49,33},{2,50}... | collective-permute-start | bytes 491528 | tf_op jit(solution)/shard_map/ppermute | solution.py:303
  19.5 6.8 %collective-permute-start.2 = (bf16[2,2,16,1024]{3,2,1,0:T(8,128)(2,1)S(1)}, bf16[2,2,16,1024]{3,2,1,0:T(8,128)(2,1)S(1)}, u32[]{:S(2)}, u32[]{:S(2)}) collective-permute-start(bf16[2,2,16,1024]{3,2,1,0:T(8,128)(2,1)S(1)} %pad_maximum_fusion.4), channel_id=1, source_target_pairs={{0,7},{1,0},{2,1},{3,2},{4,3},{5,4},{6,5},{7,6},{8,15},{9,8},{10,9... | collective-permute-start | bytes 393224 | tf_op jit(solution)/shard_map/ppermute | solution.py:303
  23.9 6.8 %collective-permute-start.3 = (bf16[2,2,16,1024]{3,2,1,0:T(8,128)(2,1)S(1)}, bf16[2,2,16,1024]{3,2,1,0:T(8,128)(2,1)S(1)}, u32[]{:S(2)}, u32[]{:S(2)}) collective-permute-start(bf16[2,2,16,1024]{3,2,1,0:T(8,128)(2,1)S(1)} %pad_maximum_fusion.4), channel_id=1, source_target_pairs={{0,2},{1,3},{2,4},{3,5},{4,6},{5,7},{6,0},{7,1},{8,10},{9,11},{10,... | collective-permute-start | bytes 393224 | tf_op jit(solution)/shard_map/ppermute | solution.py:303
  23.9 7.5 %collective-permute-start.1 = (bf16[2,2,16,1024]{3,2,1,0:T(8,128)(2,1)S(1)}, bf16[2,2,16,1024]{3,2,1,0:T(8,128)(2,1)S(1)}, u32[]{:S(2)}, u32[]{:S(2)}) collective-permute-start(bf16[2,2,16,1024]{3,2,1,0:T(8,128)(2,1)S(1)} %pad_maximum_fusion.4), channel_id=1, source_target_pairs={{0,1},{1,2},{2,3},{3,4},{4,5},{5,6},{6,7},{7,0},{8,9},{9,10},{10,1... | collective-permute-start | bytes 393224 | tf_op jit(solution)/shard_map/ppermute | solution.py:303
  24.2 75.3 %copy-start = (bf16[1,2,1024,256]{3,2,1,0:T(8,128)(2,1)S(1)}, bf16[1,2,1024,256]{3,2,1,0:T(8,128)(2,1)}, u32[]{:S(2)}) copy-start(bf16[1,2,1024,256]{3,2,1,0:T(8,128)(2,1)} %param.9) | copy-start | bytes 3145732
  24.2 75.3 %copy-start.2 = (bf16[1,2,256,256]{3,2,1,0:T(8,128)(2,1)S(1)}, bf16[1,2,256,256]{3,2,1,0:T(8,128)(2,1)}, u32[]{:S(2)}) copy-start(bf16[1,2,256,256]{3,2,1,0:T(8,128)(2,1)} %param.11) | copy-start | bytes 786436
  24.2 75.3 %copy-start.6 = (s32[1,4]{1,0:T(1,128)S(1)}, s32[1,4]{1,0:T(1,128)}, u32[]{:S(2)}) copy-start(s32[1,4]{1,0:T(1,128)} %fill.5) | copy-start | bytes 52
  24.2 75.3 %copy-start.7 = (f32[1,2]{1,0:T(1,128)S(1)}, f32[1,2]{1,0:T(1,128)}, u32[]{:S(2)}) copy-start(f32[1,2]{1,0:T(1,128)} %weights.1) | copy-start | bytes 28
  26.2 19.3 %copy-start.8 = (bf16[2,2,16,1024]{3,2,1,0:T(8,128)(2,1)}, bf16[2,2,16,1024]{3,2,1,0:T(8,128)(2,1)S(1)}, u32[]{:S(2)}) copy-start(bf16[2,2,16,1024]{3,2,1,0:T(8,128)(2,1)S(1)} %collective-permute-done.2) | copy-start | bytes 393220
  31.3 24.1 %all-to-all-start = ((bf16[16,4,8,640]{3,2,1,0:T(8,128)(2,1)}), bf16[16,4,8,640]{3,2,1,0:T(8,128)(2,1)S(1)}, u32[]{:S(2)}, u32[]{:S(2)}) async-start(bf16[16,4,8,640]{3,2,1,0:T(8,128)(2,1)} %pad_maximum_fusion), calls=%async_computation | async-start | bytes 1310720 | tf_op jit(solution)/shard_map/all_to_all | solution.py:336
  39.6 10.6 %collective-permute-start.4 = (bf16[4,2,16,1024]{3,2,1,0:T(8,128)(2,1)S(1)}, bf16[4,2,16,1024]{3,2,1,0:T(8,128)(2,1)}, u32[]{:S(2)}, u32[]{:S(2)}) collective-permute-start(bf16[4,2,16,1024]{3,2,1,0:T(8,128)(2,1)S(1)} %pad_maximum_fusion.3), channel_id=1, source_target_pairs={{0,8},{8,0},{1,9},{9,1},{2,10},{10,2},{3,11},{11,3},{4,12},{12,4},... | collective-permute-start | bytes 786440 | tf_op jit(solution)/shard_map/ppermute | solution.py:303
  42.6 10.3 %collective-permute-start.5 = (bf16[4,2,16,1024]{3,2,1,0:T(8,128)(2,1)S(1)}, bf16[4,2,16,1024]{3,2,1,0:T(8,128)(2,1)S(1)}, u32[]{:S(2)}, u32[]{:S(2)}) collective-permute-start(bf16[4,2,16,1024]{3,2,1,0:T(8,128)(2,1)S(1)} %pad_maximum_fusion.2), channel_id=1, source_target_pairs={{0,16},{16,32},{32,48},{48,0},{1,17},{17,33},{33,49},{49,1},{2,18}... | collective-permute-start | bytes 786440 | tf_op jit(solution)/shard_map/ppermute | solution.py:303
  43.0 14.4 %collective-permute-start.6 = (bf16[4,2,16,1024]{3,2,1,0:T(8,128)(2,1)S(1)}, bf16[4,2,16,1024]{3,2,1,0:T(8,128)(2,1)}, u32[]{:S(2)}, u32[]{:S(2)}) collective-permute-start(bf16[4,2,16,1024]{3,2,1,0:T(8,128)(2,1)S(1)} %pad_maximum_fusion.2), channel_id=1, source_target_pairs={{0,32},{16,48},{32,0},{48,16},{1,33},{17,49},{33,1},{49,17},{2,34}... | collective-permute-start | bytes 786440 | tf_op jit(solution)/shard_map/ppermute | solution.py:303
  44.0 14.4 %collective-permute-start.7 = (bf16[4,2,16,1024]{3,2,1,0:T(8,128)(2,1)S(1)}, bf16[4,2,16,1024]{3,2,1,0:T(8,128)(2,1)}, u32[]{:S(2)}, u32[]{:S(2)}) collective-permute-start(bf16[4,2,16,1024]{3,2,1,0:T(8,128)(2,1)S(1)} %pad_maximum_fusion.2), channel_id=1, source_target_pairs={{0,48},{16,0},{32,16},{48,32},{1,49},{17,1},{33,17},{49,33},{2,50}... | collective-permute-start | bytes 786440 | tf_op jit(solution)/shard_map/ppermute | solution.py:303
  56.6 6.0 %collective-permute-start.15 = (bf16[640,256]{1,0:T(8,128)(2,1)S(1)}, bf16[640,256]{1,0:T(8,128)(2,1)S(1)}, u32[]{:S(2)}, u32[]{:S(2)}) collective-permute-start(bf16[640,256]{1,0:T(8,128)(2,1)S(1)} %get-tuple-element.28), channel_id=1, source_target_pairs={{0,128},{128,0},{1,129},{129,1},{2,130},{130,2},{3,131},{131,3},{4... | collective-permute-start | bytes 983048 | tf_op jit(solution)/shard_map/ppermute | solution.py:303
  59.3 41.8 %collective-permute-start.8 = (bf16[16,2,16,1024]{3,2,1,0:T(8,128)(2,1)S(1)}, bf16[16,2,16,1024]{3,2,1,0:T(8,128)(2,1)S(1)}, u32[]{:S(2)}, u32[]{:S(2)}) collective-permute-start(bf16[16,2,16,1024]{3,2,1,0:T(8,128)(2,1)S(1)} %constant_dynamic-update-slice_fusion.first), channel_id=1, source_target_pairs={{0,8},{8,0},{1,9},{9,1},{2,10},{10,2},{3,11},{11,3},{4,12},{12,4},... | collective-permute-start | bytes 3145736 | tf_op jit(solution)/shard_map/ppermute | solution.py:303
  62.7 36.9 %collective-permute-start.16 = (bf16[2,640,256]{2,1,0:T(8,128)(2,1)S(1)}, bf16[2,640,256]{2,1,0:T(8,128)(2,1)S(1)}, u32[]{:S(2)}, u32[]{:S(2)}) collective-permute-start(bf16[2,640,256]{2,1,0:T(8,128)(2,1)S(1)} %pad_maximum_fusion.1.own), channel_id=1, source_target_pairs={{0,64},{64,0},{1,65},{65,1},{2,66},{66,2},{3,67},{67,3},{4,68},{68... | collective-permute-start | bytes 1966088 | tf_op jit(solution)/shard_map/ppermute | solution.py:303
  72.9 15.2 %collective-permute-start.10 = (bf16[8,2,16,1024]{3,2,1,0:T(8,128)(2,1)S(1)}, bf16[8,2,16,1024]{3,2,1,0:T(8,128)(2,1)S(1)}, u32[]{:S(2)}, u32[]{:S(2)}) collective-permute-start(bf16[8,2,16,1024]{3,2,1,0:T(8,128)(2,1)S(1)} %constant_dynamic-update-slice_fusion.4.second), channel_id=1, source_target_pairs={{0,32},{16,48},{32,0},{48,16},{1,33},{17,49},{33,1},{49,17},{2,34}... | collective-permute-start | bytes 1572872 | tf_op jit(solution)/shard_map/ppermute | solution.py:303
  73.2 23.8 %collective-permute-start.11 = (bf16[8,2,16,1024]{3,2,1,0:T(8,128)(2,1)S(1)}, bf16[8,2,16,1024]{3,2,1,0:T(8,128)(2,1)S(1)}, u32[]{:S(2)}, u32[]{:S(2)}) collective-permute-start(bf16[8,2,16,1024]{3,2,1,0:T(8,128)(2,1)S(1)} %constant_dynamic-update-slice_fusion.4.second), channel_id=1, source_target_pairs={{0,48},{16,0},{32,16},{48,32},{1,49},{17,1},{33,17},{49,33},{2,50}... | collective-permute-start | bytes 1572872 | tf_op jit(solution)/shard_map/ppermute | solution.py:303
  75.7 23.9 %collective-permute-start.9 = (bf16[8,2,16,1024]{3,2,1,0:T(8,128)(2,1)S(1)}, bf16[8,2,16,1024]{3,2,1,0:T(8,128)(2,1)S(1)}, u32[]{:S(2)}, u32[]{:S(2)}) collective-permute-start(bf16[8,2,16,1024]{3,2,1,0:T(8,128)(2,1)S(1)} %constant_dynamic-update-slice_fusion.4.second), channel_id=1, source_target_pairs={{0,16},{16,32},{32,48},{48,0},{1,17},{17,33},{33,49},{49,1},{2,18}... | collective-permute-start | bytes 1572872 | tf_op jit(solution)/shard_map/ppermute | solution.py:303
  101.1 28.5 %copy-start.4 = (bf16[512,256]{1,0:T(8,128)(2,1)S(1)}, bf16[512,256]{1,0:T(8,128)(2,1)}, u32[]{:S(2)}) copy-start(bf16[512,256]{1,0:T(8,128)(2,1)} %get-tuple-element.35.onehot) | copy-start | bytes 786436
  115.2 14.4 %all-to-all-start.2 = ((f32[16,8,128]{2,1,0:T(8,128)}), f32[16,8,128]{2,1,0:T(8,128)S(1)}, u32[]{:S(2)}, u32[]{:S(2)}) async-start(f32[16,8,128]{2,1,0:T(8,128)} %turn.1), calls=%async_computation.2 | async-start | bytes 131072 | tf_op jit(solution)/shard_map/all_to_all | solution.py:349
  120.7 1.2 copy-start.1

commit v4 on v3

--- a/solution.py
+++ b/solution.py
@@ -126,49 +126,8 @@
     )(index, dft, arrived)
 
 
-def factor_kernel(index, weights, fill, lower, diag_inverse, own, mates, out, base, rows, masked):
-    pole = index[0]
-    for part in range(2):
-        for block in range(ANC // COLS):
-            keep = fill[0, block].astype(F32).astype(BF16)
-            span = slice(block * COLS, (block + 1) * COLS)
-            masked[part, span, :] = lower[part, span, :] * keep
-    for bits, ref, n in ((0, own, 0), (2, own, 1), (1, mates, 0), (3, mates, 1)):
-        start = pl.multiple_of((pole ^ bits) * QUARTER, QUARTER)
-        for which in range(2):
-            rows[which, pl.ds(start, QUARTER), :] = ref[n, which * QUARTER : (which + 1) * QUARTER, :]
-    real, imag = weights[0, 0], weights[0, 1]
-    for which in range(2):
-        near = rows[which, 0:COLS, :]
-        near_float = near.astype(F32)
-        sums = real * diag_inverse[1].astype(F32) + imag * diag_inverse[0].astype(F32)
-        base[which : which + 1, :] = jnp.sum(sums * near_float, axis=0, keepdims=True)
-        for block in range(ANC // COLS):
-            span = slice(block * COLS, (block + 1) * COLS)
-            far = rows[which, (block + 1) * COLS : (block + 2) * COLS, :].astype(F32)
-            direct = far - mm(masked[0, span, :], near)
-            cross = mm(masked[1, span, :], near)
-            out[2 * which, span, :] = imag * direct - real * cross
-            out[2 * which + 1, span, :] = real * direct + imag * cross
-    base[2:8, :] = jnp.zeros((6, COLS), F32)
-
-
-def factors(index, weights, fill, lower, diag_inverse, own, mates):
-    return pl.pallas_call(
-        factor_kernel,
-        in_specs=[SMEM_SPEC] * 3 + [VMEM_SPEC] * 4,
-        out_specs=[VMEM_SPEC] * 2,
-        out_shape=[
-            jax.ShapeDtypeStruct((4, ANC, COLS), F32),
-            jax.ShapeDtypeStruct((8, COLS), F32),
-        ],
-        scratch_shapes=[pltpu.VMEM((2, ROWS, COLS), BF16), pltpu.VMEM((2, ANC, COLS), BF16)],
-        compiler_params=params(24),
-        name="factors",
-    )(index, weights, fill, lower, diag_inverse, own, mates)
-
-
-def upper_kernel(index, fill, lower, first, first_y, second, second_1, second_2, second_3, factor, base, onehot, out, slots, both):
+def upper_kernel(index, fill, lower, *refs):
+    early, far_y, second, second_y, far_x, (out, both) = refs[:4], refs[4], refs[5], refs[6], refs[7:10], refs[10:]
     grid = index[1]
     x, y, z = grid >> 4, (grid >> 3) & 1, grid & 7
     for block in range(ANC // COLS):
@@ -190,39 +149,68 @@
             out[0, here, :] = ((right[span, COLS:] - left[span, :COLS]) * keep).astype(BF16)
             out[1, here, :] = ((-left[span, COLS:] - right[span, :COLS]) * keep).astype(BF16)
 
-    for dy, ref in ((0, first), (1, first_y)):
-        scatter([ref], [(dx, dy, dz) for dx in range(NX) for dz in (0, 4, 1, 5)])
-    for dx, refs in ((0, (second, second_1)), (2, (second_2, second_3))):
-        scatter(refs, [(dx + n, dy, dz) for n in range(2) for dy in range(NY) for dz in (7, 3, 2, 6)])
-    rows = [base[which : which + 1, :] for which in range(2)]
-    for block in range(ANC // COLS):
-        span = slice(block * COLS, (block + 1) * COLS)
-        real, imag = out[0, span, :].astype(F32), out[1, span, :].astype(F32)
-        for which in range(2):
-            term = real * factor[2 * which, span, :] + imag * factor[2 * which + 1, span, :]
-            rows[which] = rows[which] + jnp.sum(term, axis=0, keepdims=True)
-    line = iota((8, COLS), 0)
-    values = jnp.where(line == 2 * x, rows[0], jnp.where(line == 2 * x + 1, rows[1], 0.0))
-    sums = split_matmul(values, onehot[...], ((1,), (1,)))
-    width = PLANE * CAP
-    for px in range(NX):
-        for pole in range(POLES):
-            slots[pole * NX + px] = sums[:, px * width : (px + 1) * width]
-
-
-def upper_rows(index, fill, lower, pieces, factor, base, onehot):
+    up, down = (0, 4, 1, 5), (7, 3, 2, 6)
+    scatter(early, [(dx, 0, dz) for dx in range(NX) for dz in up])
+    scatter([far_y], [(dx, 1, dz) for dx in range(NX) for dz in up])
+    scatter([second, second_y, far_x[0]], [(dx, dy, dz) for dx in range(2) for dy in range(NY) for dz in down])
+    scatter(far_x[1:], [(dx, dy, dz) for dx in (2, 3) for dy in range(NY) for dz in down])
+
+
+def upper_rows(index, fill, lower, pieces):
     return pl.pallas_call(
         upper_kernel,
-        in_specs=[SMEM_SPEC] * 2 + [VMEM_SPEC] * (4 + len(pieces)),
-        out_specs=[VMEM_SPEC] * 2,
-        out_shape=[
-            jax.ShapeDtypeStruct((2, ANC, COLS), BF16),
-            jax.ShapeDtypeStruct((POLES * NX, 8, PLANE * CAP), F32),
-        ],
+        in_specs=[SMEM_SPEC] * 2 + [VMEM_SPEC] * (1 + len(pieces)),
+        out_specs=VMEM_SPEC,
+        out_shape=jax.ShapeDtypeStruct((2, ANC, COLS), BF16),
         scratch_shapes=[pltpu.VMEM((ANC, 2 * COLS), BF16)],
         compiler_params=params(28),
         name="upper",
-    )(index, fill, lower, *pieces, factor, base, onehot)
+    )(index, fill, lower, *pieces)
+
+
+def charge_kernel(index, weights, fill, lower, diag_inverse, own, own_far, mate, mate_far, upper, onehot, slots, rows):
+    pole, x = index[0], index[1] >> 4
+    for bits, ref in ((0, own), (2, own_far), (1, mate), (3, mate_far)):
+        start = pl.multiple_of((pole ^ bits) * QUARTER, QUARTER)
+        for which in range(2):
+            rows[which, pl.ds(start, QUARTER), :] = ref[which * QUARTER : (which + 1) * QUARTER, :]
+    real, imag = weights[0, 0], weights[0, 1]
+    sums = real * diag_inverse[1].astype(F32) + imag * diag_inverse[0].astype(F32)
+    nears = [rows[which, 0:COLS, :] for which in range(2)]
+    totals = [jnp.sum(sums * near.astype(F32), axis=0, keepdims=True) for near in nears]
+    both = jnp.concatenate(nears, axis=1)
+    for block in range(ANC // COLS):
+        keep = fill[0, block].astype(F32)
+        span = slice(block * COLS, (block + 1) * COLS)
+        up_real, up_imag = upper[0, span, :].astype(F32), upper[1, span, :].astype(F32)
+        to_direct = imag * up_real + real * up_imag
+        to_cross = imag * up_imag - real * up_real
+        direct = mm(lower[0, span, :], both) * keep
+        cross = mm(lower[1, span, :], both) * keep
+        for which in range(2):
+            part = slice(which * COLS, (which + 1) * COLS)
+            far = rows[which, (block + 1) * COLS : (block + 2) * COLS, :].astype(F32)
+            term = to_direct * (far - direct[:, part]) + to_cross * cross[:, part]
+            totals[which] = totals[which] + jnp.sum(term, axis=0, keepdims=True)
+    line = iota((8, COLS), 0)
+    values = jnp.where(line == 2 * x, totals[0], jnp.where(line == 2 * x + 1, totals[1], 0.0))
+    result = split_matmul(values, onehot[...], ((1,), (1,)))
+    width = PLANE * CAP
+    for px in range(NX):
+        for n in range(POLES):
+            slots[n * NX + px] = result[:, px * width : (px + 1) * width]
+
+
+def charge_slots(index, weights, fill, lower, diag_inverse, quarters, upper, onehot):
+    return pl.pallas_call(
+        charge_kernel,
+        in_specs=[SMEM_SPEC] * 3 + [VMEM_SPEC] * (4 + len(quarters)),
+        out_specs=VMEM_SPEC,
+        out_shape=jax.ShapeDtypeStruct((POLES * NX, 8, PLANE * CAP), F32),
+        scratch_shapes=[pltpu.VMEM((2, ROWS, COLS), BF16)],
+        compiler_params=params(24),
+        name="charge",
+    )(index, weights, fill, lower, diag_inverse, *quarters, upper, onehot)
 
 
 def diag_kernel(fill, lower, upper, diag_inverse, out):
@@ -269,7 +257,7 @@
     )(arrived)
 
 
-def place_kernel(arrived, onehot, out):
+def place_kernel(arrived, onehot, *outs):
     width = PLANE * CAP
     line, lane = iota((8, width), 0), iota((8, width), 1)
     total = jnp.zeros((8, width), F32)
@@ -279,7 +267,7 @@
     wide = jnp.concatenate([jnp.where((line >> 1) == px, total, 0.0) for px in range(NX)], axis=1)
     result = split_matmul(wide, onehot[...], ((1,), (0,)))
     for which in range(2):
-        out[which : which + 1, :] = jnp.sum(
+        outs[which][...] = jnp.sum(
             jnp.where((iota((8, COLS), 0) & 1) == which, result, 0.0), axis=0, keepdims=True
         )
 
@@ -288,8 +276,8 @@
     return pl.pallas_call(
         place_kernel,
         in_specs=[VMEM_SPEC] * 2,
-        out_specs=VMEM_SPEC,
-        out_shape=jax.ShapeDtypeStruct((2, COLS), F32),
+        out_specs=[VMEM_SPEC] * 2,
+        out_shape=[jax.ShapeDtypeStruct((1, COLS), F32)] * 2,
         compiler_params=params(),
         name="place",
     )(arrived, onehot)
@@ -315,40 +303,41 @@
     lower, inverse = lower_panels[0], diag_inverse[0]
     shard = ainv_anc[0]
 
-    near, near_up, near_down, near_two = all_of_z(shard)
+    table = dft_column.reshape(128, 128)
+    z_4 = shift(shard, "z", 4)
+    *packed, slot_onehot = pack(index, table, margin, hamiltonian)
+    z_4, *packed = lax.optimization_barrier((z_4, *packed))
+
+    near = jnp.stack([shard, z_4])
+    near_up, near_down, near_two = [shift(near, "z", d) for d in (1, -1, 2)]
+    packed = [value.reshape(PLANE, CAP, 2 * QUARTER) for value in packed]
+    sent = [packed[0]] + [shift(packed[d], "x", d) for d in (1, 2, 3)]
+    near, near_up, near_down, near_two, *sent = lax.optimization_barrier((near, near_up, near_down, near_two, *sent))
+
     first = jnp.concatenate([near, near_up])
     second = jnp.concatenate([near_down, near_two])
-    first_1, first_2, first_3 = [shift(first, "x", d) for d in (1, 2, 3)]
-    second_y = shift(second, "yhi", 1)
-    first, second_y = lax.optimization_barrier((first, second_y))
-    first = jnp.concatenate([first, first_1, first_2, first_3])
-    second = jnp.concatenate([second, second_y])
-    first_y = shift(first, "yhi", 1)
-    second_x = [shift(second, "x", d) for d in (1, 2, 3)]
-
-    table = dft_column.reshape(128, 128)
-    table, near = lax.optimization_barrier((table, near))
-    packed = pack(index, table, margin, hamiltonian)
-    slot_onehot = packed[NX]
-    packed = [value.reshape(PLANE, CAP, 2 * QUARTER) for value in packed[:NX]]
-    outgoing = jnp.stack([packed[0]] + [shift(packed[d], "x", d) for d in (1, 2, 3)], axis=1)
-    outgoing, near_up, near_down, near_two = lax.optimization_barrier((outgoing, near_up, near_down, near_two))
-    arrived = lax.all_to_all(outgoing, ("yhi", "z"), split_axis=0, concat_axis=0, tiled=True)
+    first_x = [first] + [shift(first, "x", d) for d in (1, 2, 3)]
+    second_y = [second, shift(second, "yhi", 1)]
+    arrived = lax.all_to_all(jnp.stack(sent, axis=1), ("yhi", "z"), split_axis=0, concat_axis=0, tiled=True)
+    (first_x, second_y, arrived) = lax.optimization_barrier((first_x, second_y, arrived))
+
+    first_y = shift(jnp.concatenate(first_x), "yhi", 1)
+    second_all = jnp.concatenate(second_y)
+    second_x = [shift(second_all, "x", d) for d in (1, 2, 3)]
     mine, column_onehot = unpack(index, table, arrived.reshape(SLOTS, 2 * QUARTER))
-    mine = jnp.stack([mine, shift(mine, "ylo", 1)])
-    mates = shift(mine, "core", 1)
-    second_1, second_2, second_3 = second_x
-    mates, second_1, second_2, second_3 = lax.optimization_barrier((mates, second_1, second_2, second_3))
-    factor, base = factors(index, pole_weights, fill_pattern, lower, inverse, mine, mates)
-
-    upper, slots = upper_rows(
-        index, fill_pattern, lower, [first, first_y, second] + second_x, factor, base, column_onehot
-    )
+    mine_far = shift(mine, "ylo", 1)
+    (first_y, second_x, mine_far) = lax.optimization_barrier((first_y, second_x, mine_far))
+
+    mates = shift(jnp.stack([mine, mine_far]), "core", 1)
+    mate, mate_far = mates[0], mates[1]
+    upper = upper_rows(index, fill_pattern, lower, first_x + [first_y] + second_y + second_x)
+    quarters = [mine, mine_far, mate, mate_far]
+    slots = charge_slots(index, pole_weights, fill_pattern, lower, inverse, quarters, upper, column_onehot)
     diag = diag_block(fill_pattern, lower, upper, inverse)
     sums = lax.all_to_all(slots, ("ylo", "core", "x"), split_axis=0, concat_axis=0, tiled=True)
     sums = lax.all_to_all(turn(sums), ("yhi", "z"), split_axis=0, concat_axis=0, tiled=True)
-    placed = place(sums, slot_onehot)
-    return (upper[None], diag[None], placed[0], placed[1])
+    charges, energy = place(sums, slot_onehot)
+    return (upper[None], diag[None], charges.reshape(COLS), energy.reshape(COLS))
 
 
 def solution(mesh):

time: 131 us -> 119 us (0.908)
  waiting for transfers between devices: 47.7 us -> 42.9 us
  local copies, waits for them, and re-layouts: 5.7 us -> 1.36 us
  starting transfers between devices: 50.4 us -> 48.1 us
  other arithmetic: 3.48 us -> 1.76 us
    ppermute x17, waiting for transfers between devices: 39.6 us -> 33.2 us  [shift(): lax.ppermute(value, axis, [(n, (n + by) % size) for n in range(size)])]
    ppermute x17, starting transfers between devices: 36.6 us -> 32.1 us  [shift(): lax.ppermute(value, axis, [(n, (n + by) % size) for n in range(size)])]
    unnamed x25 -> x23, local copies, waits for them, and re-layouts: 3.19 us -> 1.27 us
    concatenate x2 -> x3, local copies, waits for them, and re-layouts: 1.94 us -> 0.04 us  [the longest x1 0.02 us: body(): second_all = jnp.concatenate(second_y)]
    another operation x3, other arithmetic: 2.88 us -> 1.02 us  [the longest x1 0.94 us: body(): jnp.stack(sent, axis=1)]
    all_to_all x1, starting transfers between devices: 5.56 us -> 7.37 us  [body(): lax.all_to_all(turn(sums), ('yhi', 'z'), split_axis=0, concat_axis=0, til...]
  transfers between devices with their start and end apart: 19 -> 19, of which waited for: 12 -> 8; matrix products, arithmetic and copies ran while one was open for 5% -> 1% of each run, Pallas kernels for 4% -> 9%
where the time goes in v4:
time: 119 us
  starting transfers between devices  48.1 us (40%)
  waiting for transfers between devices  42.9 us (36%)
  Pallas kernels  13.9 us (12%)
  blocking collectives  9.63 us (8%)
  other arithmetic  1.76 us (1%)
  local copies, waits for them, and re-layouts  1.36 us (1%)
    ppermute x17, waiting for transfers between devices, shift(): lax.ppermute(value, axis, [(n, (n + by) % size) for n in range(size)])  33.2 us
    ppermute x17, starting transfers between devices, shift(): lax.ppermute(value, axis, [(n, (n + by) % size) for n in range(size)])  32.1 us
    all_to_all x1, blocking collectives, body(): lax.all_to_all(slots, ('ylo', 'core', 'x'), split_axis=0, concat_axis=0,...  9.63 us
    all_to_all x1, starting transfers between devices, body(): lax.all_to_all(jnp.stack(sent, axis=1), ('yhi', 'z'), split_axis=0, conca...  8.62 us
    all_to_all x1, starting transfers between devices, body(): lax.all_to_all(turn(sums), ('yhi', 'z'), split_axis=0, concat_axis=0, til...  7.37 us
    all_to_all x1, waiting for transfers between devices, body(): lax.all_to_all(turn(sums), ('yhi', 'z'), split_axis=0, concat_axis=0, til...  6.84 us
    pallas_call x1, Pallas kernels, upper_rows(): pl.pallas_call(upper_kernel, in_specs=[SMEM_SPEC] * 2 + [VMEM_SPEC] * (1...  3.9 us
    pallas_call x1, Pallas kernels, pack(): pl.pallas_call(pack_kernel, in_specs=[SMEM_SPEC, VMEM_SPEC, HBM_SPEC, HBM...  3.28 us
  transfers between devices with their start and end apart: 19, of which 8 were waited for; matrix products, arithmetic and copies ran while one was open for 1% of the time, Pallas kernels for 9%

profile of v4, /device:TPU:1, one launch (start us, length us, event | category | flops | bytes accessed | tf_op | source)
XLA Modules:
  0.0 118.6 jit_solution(2750555466692332935)
XLA Ops:
  0.6 7.8 %collective-permute-start = (bf16[2,16,1024]{2,1,0:T(8,128)(2,1)}, bf16[2,16,1024]{2,1,0:T(8,128)(2,1)S(1)}, u32[]{:S(2)}, u32[]{:S(2)}) collective-permute-start(bf16[2,16,1024]{2,1,0:T(8,128)(2,1)} %bitcast.42), channel_id=1, source_target_pairs={{0,4},{1,5},{2,6},{3,7},{4,0},{5,1},{6,2},{7,3},{8,12},{9,13},{10,... | collective-permute-start | bytes 196616 | tf_op jit(solution)/shard_map/ppermute | solution.py:291
  8.5 0.6 pad_add_fusion.index
  9.1 3.3 %pack.1 = (bf16[128,640]{1,0:T(8,128)(2,1)}, bf16[128,640]{1,0:T(8,128)(2,1)}, bf16[128,640]{1,0:T(8,128)(2,1)}, bf16[128,640]{1,0:T(8,128)(2,1)}, bf16[512,256]{1,0:T(8,128)(2,1)}) custom-call(s32[2]{0:T(128)} %pad_add_fusion.index, s32[128,128]{1,0:T(8,128)} %bitcast.35, bf16[1280,256]{1,0:T(8,128)(2,1)} %margin.1, bf16[1280,256]{1,0:T(8,128)(2,1)} %hamiltonian.1), custom_call_target="tpu_custom_call" | custom-call | tf_op jit(solution)/shard_map/pack/pallas_call | solution.py:90
  12.4 0.0 copy-start.8
  12.4 0.0 collective-permute-done
  12.4 0.8 collective-permute-start.1
  13.2 1.2 %collective-permute-start.4 = (bf16[16,8,640]{2,1,0:T(8,128)(2,1)}, bf16[16,8,640]{2,1,0:T(8,128)(2,1)S(1)}, u32[]{:S(2)}, u32[]{:S(2)}) collective-permute-start(bf16[16,8,640]{2,1,0:T(8,128)(2,1)} %bitcast.46), channel_id=1, source_target_pairs={{0,16},{16,32},{32,48},{48,0},{1,17},{17,33},{33,49},{49,1},{2,18}... | collective-permute-start | bytes 491528 | tf_op jit(solution)/shard_map/ppermute | solution.py:291
  14.4 2.5 %collective-permute-start.5 = (bf16[16,8,640]{2,1,0:T(8,128)(2,1)}, bf16[16,8,640]{2,1,0:T(8,128)(2,1)S(1)}, u32[]{:S(2)}, u32[]{:S(2)}) collective-permute-start(bf16[16,8,640]{2,1,0:T(8,128)(2,1)} %bitcast.45), channel_id=1, source_target_pairs={{0,32},{16,48},{32,0},{48,16},{1,33},{17,49},{33,1},{49,17},{2,34}... | collective-permute-start | bytes 491528 | tf_op jit(solution)/shard_map/ppermute | solution.py:291
  16.9 1.2 collective-permute-start.6
  18.1 1.9 %collective-permute-start.2 = (bf16[2,2,16,1024]{3,2,1,0:T(8,128)(2,1)S(1)}, bf16[2,2,16,1024]{3,2,1,0:T(8,128)(2,1)S(1)}, u32[]{:S(2)}, u32[]{:S(2)}) collective-permute-start(bf16[2,2,16,1024]{3,2,1,0:T(8,128)(2,1)S(1)} %pad_maximum_fusion.3), channel_id=1, source_target_pairs={{0,7},{1,0},{2,1},{3,2},{4,3},{5,4},{6,5},{7,6},{8,15},{9,8},{10,9... | collective-permute-start | bytes 393224 | tf_op jit(solution)/shard_map/ppermute | solution.py:291
  20.0 0.0 collective-permute-done.1
  20.0 0.0 collective-permute-start.3
  20.0 1.9 %collective-permute-done.2 = bf16[2,2,16,1024]{3,2,1,0:T(8,128)(2,1)S(1)} collective-permute-done((bf16[2,2,16,1024]{3,2,1,0:T(8,128)(2,1)S(1)}, bf16[2,2,16,1024]{3,2,1,0:T(8,128)(2,1)S(1)}, u32[]{:S(2)}, u32[]{:S(2)}) %collective-permute-start.2) | collective-permute-done | bytes 131104 | tf_op jit(solution)/shard_map/ppermute | solution.py:291
  21.9 4.0 %collective-permute-done.3 = bf16[2,2,16,1024]{3,2,1,0:T(8,128)(2,1)S(1)} collective-permute-done((bf16[2,2,16,1024]{3,2,1,0:T(8,128)(2,1)S(1)}, bf16[2,2,16,1024]{3,2,1,0:T(8,128)(2,1)S(1)}, u32[]{:S(2)}, u32[]{:S(2)}) %collective-permute-start.3) | collective-permute-done | bytes 131104 | tf_op jit(solution)/shard_map/ppermute | solution.py:291
  26.0 0.9 pad_maximum_fusion.1
  26.9 8.6 %all-to-all-start = ((bf16[16,4,8,640]{3,2,1,0:T(8,128)(2,1)}), bf16[16,4,8,640]{3,2,1,0:T(8,128)(2,1)S(1)}, u32[]{:S(2)}, u32[]{:S(2)}) async-start(bf16[16,4,8,640]{3,2,1,0:T(8,128)(2,1)} %pad_maximum_fusion.1), calls=%async_computation | async-start | bytes 1310720 | tf_op jit(solution)/shard_map/all_to_all | solution.py:321
  35.6 0.4 collective-permute-start.7
  36.0 0.9 collective-permute-start.8
  36.9 1.6 %collective-permute-start.9 = (bf16[4,2,16,1024]{3,2,1,0:T(8,128)(2,1)S(1)}, bf16[4,2,16,1024]{3,2,1,0:T(8,128)(2,1)S(1)}, u32[]{:S(2)}, u32[]{:S(2)}) collective-permute-start(bf16[4,2,16,1024]{3,2,1,0:T(8,128)(2,1)S(1)} %constant_dynamic-update-slice_fusion.refs_0_), channel_id=1, source_target_pairs={{0,48},{16,0},{32,16},{48,32},{1,49},{17,1},{33,17},{49,33},{2,50}... | collective-permute-start | bytes 786440 | tf_op jit(solution)/shard_map/ppermute | solution.py:291
  38.5 3.0 %collective-permute-start.10 = (bf16[4,2,16,1024]{3,2,1,0:T(8,128)(2,1)S(1)}, bf16[4,2,16,1024]{3,2,1,0:T(8,128)(2,1)S(1)}, u32[]{:S(2)}, u32[]{:S(2)}) collective-permute-start(bf16[4,2,16,1024]{3,2,1,0:T(8,128)(2,1)S(1)} %constant_dynamic-update-slice_fusion.2.refs_5_), channel_id=1, source_target_pairs={{0,8},{8,0},{1,9},{9,1},{2,10},{10,2},{3,11},{11,3},{4,12},{12,4},... | collective-permute-start | bytes 786440 | tf_op jit(solution)/shard_map/ppermute | solution.py:291
  41.4 4.4 %collective-permute-done.7.refs_1_ = bf16[4,2,16,1024]{3,2,1,0:T(8,128)(2,1)S(1)} collective-permute-done((bf16[4,2,16,1024]{3,2,1,0:T(8,128)(2,1)S(1)}, bf16[4,2,16,1024]{3,2,1,0:T(8,128)(2,1)S(1)}, u32[]{:S(2)}, u32[]{:S(2)}) %collective-permute-start.7) | collective-permute-done | bytes 262176 | tf_op jit(solution)/shard_map/ppermute | solution.py:291
  45.8 0.4 collective-permute-done.9.refs_3_
  46.2 1.8 %collective-permute-done.10.refs_6_ = bf16[4,2,16,1024]{3,2,1,0:T(8,128)(2,1)S(1)} collective-permute-done((bf16[4,2,16,1024]{3,2,1,0:T(8,128)(2,1)S(1)}, bf16[4,2,16,1024]{3,2,1,0:T(8,128)(2,1)S(1)}, u32[]{:S(2)}, u32[]{:S(2)}) %collective-permute-start.10) | collective-permute-done | bytes 262176 | tf_op jit(solution)/shard_map/ppermute | solution.py:291
  48.0 2.9 %all-to-all-done = bf16[16,4,8,640]{3,2,1,0:T(8,128)(2,1)S(1)} async-done(((bf16[16,4,8,640]{3,2,1,0:T(8,128)(2,1)}), bf16[16,4,8,640]{3,2,1,0:T(8,128)(2,1)S(1)}, u32[]{:S(2)}, u32[]{:S(2)}) %all-to-all-start) | async-done | bytes 655392 | tf_op jit(solution)/shard_map/all_to_all | solution.py:321
  50.9 0.1 pad_maximum_fusion
  51.0 0.1 collective-permute-start.11
  51.1 0.0 copy-start.3
  51.2 0.0 copy-start
  51.2 0.4 collective-permute-start.12
  51.6 1.3 %collective-permute-start.13 = (bf16[8,2,16,1024]{3,2,1,0:T(8,128)(2,1)S(1)}, bf16[8,2,16,1024]{3,2,1,0:T(8,128)(2,1)S(1)}, u32[]{:S(2)}, u32[]{:S(2)}) collective-permute-start(bf16[8,2,16,1024]{3,2,1,0:T(8,128)(2,1)S(1)} %constant_dynamic-update-slice_fusion.4), channel_id=1, source_target_pairs={{0,32},{16,48},{32,0},{48,16},{1,33},{17,49},{33,1},{49,17},{2,34}... | collective-permute-start | bytes 1572872 | tf_op jit(solution)/shard_map/ppermute | solution.py:291
  52.9 2.0 %collective-permute-start.14 = (bf16[8,2,16,1024]{3,2,1,0:T(8,128)(2,1)S(1)}, bf16[8,2,16,1024]{3,2,1,0:T(8,128)(2,1)S(1)}, u32[]{:S(2)}, u32[]{:S(2)}) collective-permute-start(bf16[8,2,16,1024]{3,2,1,0:T(8,128)(2,1)S(1)} %constant_dynamic-update-slice_fusion.4), channel_id=1, source_target_pairs={{0,48},{16,0},{32,16},{48,32},{1,49},{17,1},{33,17},{49,33},{2,50}... | collective-permute-start | bytes 1572872 | tf_op jit(solution)/shard_map/ppermute | solution.py:291
  54.9 1.1 unpack.1
  56.0 0.5 collective-permute-start.15
  56.5 20.7 %collective-permute-done.15.own_far = bf16[640,256]{1,0:T(8,128)(2,1)S(1)} collective-permute-done((bf16[640,256]{1,0:T(8,128)(2,1)S(1)}, bf16[640,256]{1,0:T(8,128)(2,1)S(1)}, u32[]{:S(2)}, u32[]{:S(2)}) %collective-permute-start.15) | collective-permute-done | bytes 327712 | tf_op jit(solution)/shard_map/ppermute | solution.py:291
  77.2 0.1 pad_maximum_fusion.2
  77.3 0.0 copy-start.6
  77.3 6.6 %collective-permute-start.16 = (bf16[2,640,256]{2,1,0:T(8,128)(2,1)S(1)}, bf16[2,640,256]{2,1,0:T(8,128)(2,1)S(1)}, u32[]{:S(2)}, u32[]{:S(2)}) collective-permute-start(bf16[2,640,256]{2,1,0:T(8,128)(2,1)S(1)} %pad_maximum_fusion.2), channel_id=1, source_target_pairs={{0,64},{64,0},{1,65},{65,1},{2,66},{66,2},{3,67},{67,3},{4,68},{68... | collective-permute-start | bytes 1966088 | tf_op jit(solution)/shard_map/ppermute | solution.py:291
  83.9 3.9 %upper.1 = bf16[2,1024,256]{2,1,0:T(8,128)(2,1)} custom-call(s32[2]{0:T(128)S(1)} %copy-done.5, s32[1,4]{1,0:T(1,128)S(1)} %copy-done.6, bf16[2,1024,256]{2,1,0:T(8,128)(2,1)S(1)} %bitcast.26, bf16[4,2,16,1024]{3,2,1,0:T(8,128)(2,1)S(1)} %constant_dynamic-update-slice_fusion.refs_0_, bf16[4,2,16,1024]{3,2,1,0:T(8,128)(2,1)S(1)} %collective-permute-done.7.refs_1_, ...), custom_call_target="tpu_custom_call" | custom-call | tf_op jit(solution)/shard_map/upper/pallas_call | solution.py:160
  87.8 0.0 copy-start.7
  87.9 1.1 copy-done.1
  89.0 0.0 copy-done.2
  89.0 2.0 %charge.1 = f32[16,8,128]{2,1,0:T(8,128)S(1)} custom-call(s32[2]{0:T(128)S(1)} %copy-done.5, f32[1,2]{1,0:T(1,128)S(1)} %copy-done.7, s32[1,4]{1,0:T(1,128)S(1)} %copy-done.6, bf16[2,1024,256]{2,1,0:T(8,128)(2,1)S(1)} %bitcast.27, bf16[2,256,256]{2,1,0:T(8,128)(2,1)S(1)} %bitcast.33, bf16[640,256]{1,0:T(8,128)(2,1)S(1)} %get-tuple-element.62.own, ...), custom_call_target="tpu_custom_call" | custom-call | tf_op jit(solution)/shard_map/charge/pallas_call | solution.py:205
  91.1 9.6 %all_to_all.15.arrived = f32[16,8,128]{2,1,0:T(8,128)S(1)} all-to-all(f32[16,8,128]{2,1,0:T(8,128)S(1)} %charge.1), channel_id=1, replica_groups=mesh['ylo'=2,'core'=2,'x'=4,'yhi'=2,'z'=8] {'ylo','core','x'}, dimensions={0} | all-to-all | bytes 131072 | tf_op jit(solution)/shard_map/all_to_all | solution.py:337
  100.7 0.7 turn.1
  101.4 7.4 %all-to-all-start.2 = ((f32[16,8,128]{2,1,0:T(8,128)}), f32[16,8,128]{2,1,0:T(8,128)S(1)}, u32[]{:S(2)}, u32[]{:S(2)}) async-start(f32[16,8,128]{2,1,0:T(8,128)} %turn.1), calls=%async_computation.2 | async-start | bytes 131072 | tf_op jit(solution)/shard_map/all_to_all | solution.py:338
  108.8 2.0 %diag.1 = bf16[2,256,256]{2,1,0:T(8,128)(2,1)} custom-call(s32[1,4]{1,0:T(1,128)S(1)} %copy-done.6, bf16[2,1024,256]{2,1,0:T(8,128)(2,1)S(1)} %bitcast.28, bf16[2,1024,256]{2,1,0:T(8,128)(2,1)S(1)} %copy-done.1, bf16[2,256,256]{2,1,0:T(8,128)(2,1)S(1)} %bitcast.34), custom_call_target="tpu_custom_call" | custom-call | tf_op jit(solution)/shard_map/diag/pallas_call | solution.py:232
  110.9 6.8 %all-to-all-done.2.arrived = f32[16,8,128]{2,1,0:T(8,128)S(1)} async-done(((f32[16,8,128]{2,1,0:T(8,128)}), f32[16,8,128]{2,1,0:T(8,128)S(1)}, u32[]{:S(2)}, u32[]{:S(2)}) %all-to-all-start.2) | async-done | bytes 65568 | tf_op jit(solution)/shard_map/all_to_all | solution.py:338
  117.7 0.9 place.1
  (30 shorter events, 0.2 us)
Async XLA Ops:
  0.6 11.7 %collective-permute-start = (bf16[2,16,1024]{2,1,0:T(8,128)(2,1)}, bf16[2,16,1024]{2,1,0:T(8,128)(2,1)S(1)}, u32[]{:S(2)}, u32[]{:S(2)}) collective-permute-start(bf16[2,16,1024]{2,1,0:T(8,128)(2,1)} %bitcast.42), channel_id=1, source_target_pairs={{0,4},{1,5},{2,6},{3,7},{4,0},{5,1},{6,2},{7,3},{8,12},{9,13},{10,... | collective-permute-start | bytes 196616 | tf_op jit(solution)/shard_map/ppermute | solution.py:291
  9.1 3.3 %copy-start.9 = (bf16[1,2,16,1024]{3,2,1,0:T(8,128)(2,1)S(1)}, bf16[1,2,16,1024]{3,2,1,0:T(8,128)(2,1)}, u32[]{:S(2)}) copy-start(bf16[1,2,16,1024]{3,2,1,0:T(8,128)(2,1)} %param.8) | copy-start | bytes 196612
  12.4 13.6 %copy-start.8 = (bf16[128,640]{1,0:T(8,128)(2,1)S(1)}, bf16[128,640]{1,0:T(8,128)(2,1)}, u32[]{:S(2)}) copy-start(bf16[128,640]{1,0:T(8,128)(2,1)} %get-tuple-element.43) | copy-start | bytes 491524
  12.4 7.6 %collective-permute-start.1 = (bf16[2,2,16,1024]{3,2,1,0:T(8,128)(2,1)S(1)}, bf16[2,2,16,1024]{3,2,1,0:T(8,128)(2,1)S(1)}, u32[]{:S(2)}, u32[]{:S(2)}) collective-permute-start(bf16[2,2,16,1024]{3,2,1,0:T(8,128)(2,1)S(1)} %pad_maximum_fusion.3), channel_id=1, source_target_pairs={{0,1},{1,2},{2,3},{3,4},{4,5},{5,6},{6,7},{7,0},{8,9},{9,10},{10,1... | collective-permute-start | bytes 393224 | tf_op jit(solution)/shard_map/ppermute | solution.py:291
  13.2 12.7 %collective-permute-start.4 = (bf16[16,8,640]{2,1,0:T(8,128)(2,1)}, bf16[16,8,640]{2,1,0:T(8,128)(2,1)S(1)}, u32[]{:S(2)}, u32[]{:S(2)}) collective-permute-start(bf16[16,8,640]{2,1,0:T(8,128)(2,1)} %bitcast.46), channel_id=1, source_target_pairs={{0,16},{16,32},{32,48},{48,0},{1,17},{17,33},{33,49},{49,1},{2,18}... | collective-permute-start | bytes 491528 | tf_op jit(solution)/shard_map/ppermute | solution.py:291
  14.4 11.5 %collective-permute-start.5 = (bf16[16,8,640]{2,1,0:T(8,128)(2,1)}, bf16[16,8,640]{2,1,0:T(8,128)(2,1)S(1)}, u32[]{:S(2)}, u32[]{:S(2)}) collective-permute-start(bf16[16,8,640]{2,1,0:T(8,128)(2,1)} %bitcast.45), channel_id=1, source_target_pairs={{0,32},{16,48},{32,0},{48,16},{1,33},{17,49},{33,1},{49,17},{2,34}... | collective-permute-start | bytes 491528 | tf_op jit(solution)/shard_map/ppermute | solution.py:291
  16.9 9.1 %collective-permute-start.6 = (bf16[16,8,640]{2,1,0:T(8,128)(2,1)}, bf16[16,8,640]{2,1,0:T(8,128)(2,1)S(1)}, u32[]{:S(2)}, u32[]{:S(2)}) collective-permute-start(bf16[16,8,640]{2,1,0:T(8,128)(2,1)} %bitcast.44), channel_id=1, source_target_pairs={{0,48},{16,0},{32,16},{48,32},{1,49},{17,1},{33,17},{49,33},{2,50}... | collective-permute-start | bytes 491528 | tf_op jit(solution)/shard_map/ppermute | solution.py:291
  18.1 3.9 %collective-permute-start.2 = (bf16[2,2,16,1024]{3,2,1,0:T(8,128)(2,1)S(1)}, bf16[2,2,16,1024]{3,2,1,0:T(8,128)(2,1)S(1)}, u32[]{:S(2)}, u32[]{:S(2)}) collective-permute-start(bf16[2,2,16,1024]{3,2,1,0:T(8,128)(2,1)S(1)} %pad_maximum_fusion.3), channel_id=1, source_target_pairs={{0,7},{1,0},{2,1},{3,2},{4,3},{5,4},{6,5},{7,6},{8,15},{9,8},{10,9... | collective-permute-start | bytes 393224 | tf_op jit(solution)/shard_map/ppermute | solution.py:291
  20.0 6.0 %collective-permute-start.3 = (bf16[2,2,16,1024]{3,2,1,0:T(8,128)(2,1)S(1)}, bf16[2,2,16,1024]{3,2,1,0:T(8,128)(2,1)S(1)}, u32[]{:S(2)}, u32[]{:S(2)}) collective-permute-start(bf16[2,2,16,1024]{3,2,1,0:T(8,128)(2,1)S(1)} %pad_maximum_fusion.3), channel_id=1, source_target_pairs={{0,2},{1,3},{2,4},{3,5},{4,6},{5,7},{6,0},{7,1},{8,10},{9,11},{10,... | collective-permute-start | bytes 393224 | tf_op jit(solution)/shard_map/ppermute | solution.py:291
  26.9 23.9 %all-to-all-start = ((bf16[16,4,8,640]{3,2,1,0:T(8,128)(2,1)}), bf16[16,4,8,640]{3,2,1,0:T(8,128)(2,1)S(1)}, u32[]{:S(2)}, u32[]{:S(2)}) async-start(bf16[16,4,8,640]{3,2,1,0:T(8,128)(2,1)} %pad_maximum_fusion.1), calls=%async_computation | async-start | bytes 1310720 | tf_op jit(solution)/shard_map/all_to_all | solution.py:321
  35.6 10.3 %collective-permute-start.7 = (bf16[4,2,16,1024]{3,2,1,0:T(8,128)(2,1)S(1)}, bf16[4,2,16,1024]{3,2,1,0:T(8,128)(2,1)S(1)}, u32[]{:S(2)}, u32[]{:S(2)}) collective-permute-start(bf16[4,2,16,1024]{3,2,1,0:T(8,128)(2,1)S(1)} %constant_dynamic-update-slice_fusion.refs_0_), channel_id=1, source_target_pairs={{0,16},{16,32},{32,48},{48,0},{1,17},{17,33},{33,49},{49,1},{2,18}... | collective-permute-start | bytes 786440 | tf_op jit(solution)/shard_map/ppermute | solution.py:291
  36.0 9.9 %collective-permute-start.8 = (bf16[4,2,16,1024]{3,2,1,0:T(8,128)(2,1)S(1)}, bf16[4,2,16,1024]{3,2,1,0:T(8,128)(2,1)S(1)}, u32[]{:S(2)}, u32[]{:S(2)}) collective-permute-start(bf16[4,2,16,1024]{3,2,1,0:T(8,128)(2,1)S(1)} %constant_dynamic-update-slice_fusion.refs_0_), channel_id=1, source_target_pairs={{0,32},{16,48},{32,0},{48,16},{1,33},{17,49},{33,1},{49,17},{2,34}... | collective-permute-start | bytes 786440 | tf_op jit(solution)/shard_map/ppermute | solution.py:291
  36.9 9.3 %collective-permute-start.9 = (bf16[4,2,16,1024]{3,2,1,0:T(8,128)(2,1)S(1)}, bf16[4,2,16,1024]{3,2,1,0:T(8,128)(2,1)S(1)}, u32[]{:S(2)}, u32[]{:S(2)}) collective-permute-start(bf16[4,2,16,1024]{3,2,1,0:T(8,128)(2,1)S(1)} %constant_dynamic-update-slice_fusion.refs_0_), channel_id=1, source_target_pairs={{0,48},{16,0},{32,16},{48,32},{1,49},{17,1},{33,17},{49,33},{2,50}... | collective-permute-start | bytes 786440 | tf_op jit(solution)/shard_map/ppermute | solution.py:291
  38.5 9.5 %collective-permute-start.10 = (bf16[4,2,16,1024]{3,2,1,0:T(8,128)(2,1)S(1)}, bf16[4,2,16,1024]{3,2,1,0:T(8,128)(2,1)S(1)}, u32[]{:S(2)}, u32[]{:S(2)}) collective-permute-start(bf16[4,2,16,1024]{3,2,1,0:T(8,128)(2,1)S(1)} %constant_dynamic-update-slice_fusion.2.refs_5_), channel_id=1, source_target_pairs={{0,8},{8,0},{1,9},{9,1},{2,10},{10,2},{3,11},{11,3},{4,12},{12,4},... | collective-permute-start | bytes 786440 | tf_op jit(solution)/shard_map/ppermute | solution.py:291
  51.0 26.2 %collective-permute-start.11 = (bf16[16,2,16,1024]{3,2,1,0:T(8,128)(2,1)S(1)}, bf16[16,2,16,1024]{3,2,1,0:T(8,128)(2,1)S(1)}, u32[]{:S(2)}, u32[]{:S(2)}) collective-permute-start(bf16[16,2,16,1024]{3,2,1,0:T(8,128)(2,1)S(1)} %pad_maximum_fusion), channel_id=1, source_target_pairs={{0,8},{8,0},{1,9},{9,1},{2,10},{10,2},{3,11},{11,3},{4,12},{12,4},... | collective-permute-start | bytes 3145736 | tf_op jit(solution)/shard_map/ppermute | solution.py:291
  51.1 3.8 %copy-start.3 = (s32[16384]{0:T(1024)S(1)}, s32[16384]{0:T(1024)}, u32[]{:S(2)}) copy-start(s32[16384]{0:T(1024)} %param.15) | copy-start | bytes 196612
  51.1 3.8 %copy-start.5 = (s32[2]{0:T(128)S(1)}, s32[2]{0:T(128)}, u32[]{:S(2)}) copy-start(s32[2]{0:T(128)} %pad_add_fusion.index) | copy-start | bytes 28
  51.2 32.7 %copy-start = (bf16[1,2,1024,256]{3,2,1,0:T(8,128)(2,1)S(1)}, bf16[1,2,1024,256]{3,2,1,0:T(8,128)(2,1)}, u32[]{:S(2)}) copy-start(bf16[1,2,1024,256]{3,2,1,0:T(8,128)(2,1)} %param.9) | copy-start | bytes 3145732
  51.2 26.0 %collective-permute-start.12 = (bf16[8,2,16,1024]{3,2,1,0:T(8,128)(2,1)S(1)}, bf16[8,2,16,1024]{3,2,1,0:T(8,128)(2,1)S(1)}, u32[]{:S(2)}, u32[]{:S(2)}) collective-permute-start(bf16[8,2,16,1024]{3,2,1,0:T(8,128)(2,1)S(1)} %constant_dynamic-update-slice_fusion.4), channel_id=1, source_target_pairs={{0,16},{16,32},{32,48},{48,0},{1,17},{17,33},{33,49},{49,1},{2,18}... | collective-permute-start | bytes 1572872 | tf_op jit(solution)/shard_map/ppermute | solution.py:291
  51.6 25.6 %collective-permute-start.13 = (bf16[8,2,16,1024]{3,2,1,0:T(8,128)(2,1)S(1)}, bf16[8,2,16,1024]{3,2,1,0:T(8,128)(2,1)S(1)}, u32[]{:S(2)}, u32[]{:S(2)}) collective-permute-start(bf16[8,2,16,1024]{3,2,1,0:T(8,128)(2,1)S(1)} %constant_dynamic-update-slice_fusion.4), channel_id=1, source_target_pairs={{0,32},{16,48},{32,0},{48,16},{1,33},{17,49},{33,1},{49,17},{2,34}... | collective-permute-start | bytes 1572872 | tf_op jit(solution)/shard_map/ppermute | solution.py:291
  52.9 24.3 %collective-permute-start.14 = (bf16[8,2,16,1024]{3,2,1,0:T(8,128)(2,1)S(1)}, bf16[8,2,16,1024]{3,2,1,0:T(8,128)(2,1)S(1)}, u32[]{:S(2)}, u32[]{:S(2)}) collective-permute-start(bf16[8,2,16,1024]{3,2,1,0:T(8,128)(2,1)S(1)} %constant_dynamic-update-slice_fusion.4), channel_id=1, source_target_pairs={{0,48},{16,0},{32,16},{48,32},{1,49},{17,1},{33,17},{49,33},{2,50}... | collective-permute-start | bytes 1572872 | tf_op jit(solution)/shard_map/ppermute | solution.py:291
  56.0 21.1 %collective-permute-start.15 = (bf16[640,256]{1,0:T(8,128)(2,1)S(1)}, bf16[640,256]{1,0:T(8,128)(2,1)S(1)}, u32[]{:S(2)}, u32[]{:S(2)}) collective-permute-start(bf16[640,256]{1,0:T(8,128)(2,1)S(1)} %get-tuple-element.62.own), channel_id=1, source_target_pairs={{0,128},{128,0},{1,129},{129,1},{2,130},{130,2},{3,131},{131,3},{4... | collective-permute-start | bytes 983048 | tf_op jit(solution)/shard_map/ppermute | solution.py:291
  77.3 6.6 %copy-start.6 = (s32[1,4]{1,0:T(1,128)S(1)}, s32[1,4]{1,0:T(1,128)}, u32[]{:S(2)}) copy-start(s32[1,4]{1,0:T(1,128)} %fill.5) | copy-start | bytes 52
  77.3 10.5 %collective-permute-start.16 = (bf16[2,640,256]{2,1,0:T(8,128)(2,1)S(1)}, bf16[2,640,256]{2,1,0:T(8,128)(2,1)S(1)}, u32[]{:S(2)}, u32[]{:S(2)}) collective-permute-start(bf16[2,640,256]{2,1,0:T(8,128)(2,1)S(1)} %pad_maximum_fusion.2), channel_id=1, source_target_pairs={{0,64},{64,0},{1,65},{65,1},{2,66},{66,2},{3,67},{67,3},{4,68},{68... | collective-permute-start | bytes 1966088 | tf_op jit(solution)/shard_map/ppermute | solution.py:291
  87.8 1.2 %copy-start.1 = (bf16[2,1024,256]{2,1,0:T(8,128)(2,1)S(1)}, bf16[2,1024,256]{2,1,0:T(8,128)(2,1)}, u32[]{:S(2)}) copy-start(bf16[2,1024,256]{2,1,0:T(8,128)(2,1)} %upper.1) | copy-start | bytes 3145732
  87.8 1.3 %copy-start.2 = (bf16[1,2,256,256]{3,2,1,0:T(8,128)(2,1)S(1)}, bf16[1,2,256,256]{3,2,1,0:T(8,128)(2,1)}, u32[]{:S(2)}) copy-start(bf16[1,2,256,256]{3,2,1,0:T(8,128)(2,1)} %param.11) | copy-start | bytes 786436
  87.8 1.2 %copy-start.7 = (f32[1,2]{1,0:T(1,128)S(1)}, f32[1,2]{1,0:T(1,128)}, u32[]{:S(2)}) copy-start(f32[1,2]{1,0:T(1,128)} %weights.1) | copy-start | bytes 28
  101.4 16.3 %all-to-all-start.2 = ((f32[16,8,128]{2,1,0:T(8,128)}), f32[16,8,128]{2,1,0:T(8,128)S(1)}, u32[]{:S(2)}, u32[]{:S(2)}) async-start(f32[16,8,128]{2,1,0:T(8,128)} %turn.1), calls=%async_computation.2 | async-start | bytes 131072 | tf_op jit(solution)/shard_map/all_to_all | solution.py:338
  108.8 8.9 %copy-start.4 = (bf16[512,256]{1,0:T(8,128)(2,1)S(1)}, bf16[512,256]{1,0:T(8,128)(2,1)}, u32[]{:S(2)}) copy-start(bf16[512,256]{1,0:T(8,128)(2,1)} %get-tuple-element.69.onehot) | copy-start | bytes 786436

commit v5 on v4

--- a/solution.py
+++ b/solution.py
@@ -126,46 +126,82 @@
     )(index, dft, arrived)
 
 
-def upper_kernel(index, fill, lower, *refs):
-    early, far_y, second, second_y, far_x, (out, both) = refs[:4], refs[4], refs[5], refs[6], refs[7:10], refs[10:]
-    grid = index[1]
-    x, y, z = grid >> 4, (grid >> 3) & 1, grid & 7
+UP, DOWN = (0, 4, 1, 5), (7, 3, 2, 6)
+
+
+def product(refs, rhs):
+    left, right = [
+        mm(jnp.concatenate([ref[:, part].reshape(-1, ANC) for ref in refs], axis=0), rhs[...]) for part in range(2)
+    ]
+    return right[:, COLS:] - left[:, :COLS], -left[:, COLS:] - right[:, :COLS]
+
+
+def start_kernel(fill, lower, *refs):
+    first, second, (rhs, out) = refs[:4], refs[4:6], refs[6:]
     for block in range(ANC // COLS):
         keep = fill[0, block].astype(F32).astype(BF16)
         span = slice(block * COLS, (block + 1) * COLS)
         for part in range(2):
-            both[span, part * COLS : (part + 1) * COLS] = lower[part, span, :] * keep
-
-    def scatter(refs, places):
-        rhs = both[...]
-        left, right = [
-            mm(jnp.concatenate([ref[:, part].reshape(-1, ANC) for ref in refs], axis=0), rhs) for part in range(2)
-        ]
+            rhs[span, part * COLS : (part + 1) * COLS] = lower[part, span, :] * keep
+    rows = 0
+    for group in (first, second):
+        real, imag = product(group, rhs)
+        span = slice(rows, rows + real.shape[0])
+        out[0, span, :] = real.astype(BF16)
+        out[1, span, :] = imag.astype(BF16)
+        rows = rows + real.shape[0]
+
+
+def start_rows(fill, lower, pieces):
+    rows = sum(value.shape[0] for value in pieces) * SHARD
+    return pl.pallas_call(
+        start_kernel,
+        in_specs=[SMEM_SPEC] + [VMEM_SPEC] * (1 + len(pieces)),
+        out_specs=[VMEM_SPEC] * 2,
+        out_shape=[
+            jax.ShapeDtypeStruct((ANC, 2 * COLS), BF16),
+            jax.ShapeDtypeStruct((2, rows, COLS), BF16),
+        ],
+        compiler_params=params(16),
+        name="start",
+    )(fill, lower, *pieces)
+
+
+def upper_kernel(index, fill, rhs, early, first_y, second_1, second_2, second_3, *outs):
+    grid = index[1]
+    x, y, z = grid >> 4, (grid >> 3) & 1, grid & 7
+
+    def scatter(real, imag, places):
         for n, (dx, dy, dz) in enumerate(places):
             px, py, pz = (x - dx) & (NX - 1), (y - dy) & (NY - 1), (z - dz) & (NZ - 1)
             here = pl.ds(pl.multiple_of(((px * NY + py) * NZ + pz) * SHARD, SHARD), SHARD)
             keep = fill[0, px].astype(F32)
             span = slice(n * SHARD, (n + 1) * SHARD)
-            out[0, here, :] = ((right[span, COLS:] - left[span, :COLS]) * keep).astype(BF16)
-            out[1, here, :] = ((-left[span, COLS:] - right[span, :COLS]) * keep).astype(BF16)
-
-    up, down = (0, 4, 1, 5), (7, 3, 2, 6)
-    scatter(early, [(dx, 0, dz) for dx in range(NX) for dz in up])
-    scatter([far_y], [(dx, 1, dz) for dx in range(NX) for dz in up])
-    scatter([second, second_y, far_x[0]], [(dx, dy, dz) for dx in range(2) for dy in range(NY) for dz in down])
-    scatter(far_x[1:], [(dx, dy, dz) for dx in (2, 3) for dy in range(NY) for dz in down])
-
-
-def upper_rows(index, fill, lower, pieces):
+            for part, value in enumerate((real, imag)):
+                rows = (value[span].astype(F32) * keep).astype(BF16)
+                for out in outs:
+                    out[part, here, :] = rows
+
+    def places(dxs, dys, dzs):
+        return [(dx, dy, dz) for dx in dxs for dy in dys for dz in dzs]
+
+    scatter(early[0], early[1], places(range(NX), (0,), UP) + places((0,), range(NY), DOWN))
+    real, imag = product([first_y], rhs)
+    scatter(real, imag, places(range(NX), (1,), UP))
+    real, imag = product([second_1, second_2, second_3], rhs)
+    scatter(real, imag, places((1, 2, 3), range(NY), DOWN))
+
+
+def upper_rows(index, fill, rhs, early, pieces):
+    shape = jax.ShapeDtypeStruct((2, ANC, COLS), BF16)
     return pl.pallas_call(
         upper_kernel,
-        in_specs=[SMEM_SPEC] * 2 + [VMEM_SPEC] * (1 + len(pieces)),
-        out_specs=VMEM_SPEC,
-        out_shape=jax.ShapeDtypeStruct((2, ANC, COLS), BF16),
-        scratch_shapes=[pltpu.VMEM((ANC, 2 * COLS), BF16)],
-        compiler_params=params(28),
+        in_specs=[SMEM_SPEC] * 2 + [VMEM_SPEC] * (2 + len(pieces)),
+        out_specs=[VMEM_SPEC] * 2,
+        out_shape=[shape, shape],
+        compiler_params=params(20),
         name="upper",
-    )(index, fill, lower, *pieces)
+    )(index, fill, rhs, early, *pieces)
 
 
 def charge_kernel(index, weights, fill, lower, diag_inverse, own, own_far, mate, mate_far, upper, onehot, slots, rows):
@@ -304,14 +340,14 @@
     shard = ainv_anc[0]
 
     table = dft_column.reshape(128, 128)
+    *packed, slot_onehot = pack(index, table, margin, hamiltonian)
     z_4 = shift(shard, "z", 4)
-    *packed, slot_onehot = pack(index, table, margin, hamiltonian)
     z_4, *packed = lax.optimization_barrier((z_4, *packed))
 
     near = jnp.stack([shard, z_4])
-    near_up, near_down, near_two = [shift(near, "z", d) for d in (1, -1, 2)]
     packed = [value.reshape(PLANE, CAP, 2 * QUARTER) for value in packed]
     sent = [packed[0]] + [shift(packed[d], "x", d) for d in (1, 2, 3)]
+    near_up, near_down, near_two = [shift(near, "z", d) for d in (1, -1, 2)]
     near, near_up, near_down, near_two, *sent = lax.optimization_barrier((near, near_up, near_down, near_two, *sent))
 
     first = jnp.concatenate([near, near_up])
@@ -326,14 +362,15 @@
     second_x = [shift(second_all, "x", d) for d in (1, 2, 3)]
     mine, column_onehot = unpack(index, table, arrived.reshape(SLOTS, 2 * QUARTER))
     mine_far = shift(mine, "ylo", 1)
-    (first_y, second_x, mine_far) = lax.optimization_barrier((first_y, second_x, mine_far))
+    rhs, early = start_rows(fill_pattern, lower, first_x + second_y)
+    first_y, second_x, mine_far, early = lax.optimization_barrier((first_y, second_x, mine_far, early))
 
     mates = shift(jnp.stack([mine, mine_far]), "core", 1)
     mate, mate_far = mates[0], mates[1]
-    upper = upper_rows(index, fill_pattern, lower, first_x + [first_y] + second_y + second_x)
+    upper, upper_again = upper_rows(index, fill_pattern, rhs, early, [first_y] + second_x)
     quarters = [mine, mine_far, mate, mate_far]
-    slots = charge_slots(index, pole_weights, fill_pattern, lower, inverse, quarters, upper, column_onehot)
-    diag = diag_block(fill_pattern, lower, upper, inverse)
+    slots = charge_slots(index, pole_weights, fill_pattern, lower, inverse, quarters, upper_again, column_onehot)
+    diag = diag_block(fill_pattern, lower, upper_again, inverse)
     sums = lax.all_to_all(slots, ("ylo", "core", "x"), split_axis=0, concat_axis=0, tiled=True)
     sums = lax.all_to_all(turn(sums), ("yhi", "z"), split_axis=0, concat_axis=0, tiled=True)
     charges, energy = place(sums, slot_onehot)

time: 119 us -> 115 us (0.966)
  waiting for transfers between devices: 42.9 us -> 32.1 us
  starting transfers between devices: 48.1 us -> 55 us
    ppermute x17, waiting for transfers between devices: 33.2 us -> 25.2 us  [shift(): lax.ppermute(value, axis, [(n, (n + by) % size) for n in range(size)])]
    ppermute x17, starting transfers between devices: 32.1 us -> 39.8 us  [shift(): lax.ppermute(value, axis, [(n, (n + by) % size) for n in range(size)])]
    all_to_all x1, waiting for transfers between devices: 2.88 us -> 0.01 us  [body(): lax.all_to_all(jnp.stack(sent, axis=1), ('yhi', 'z'), split_axis=0, conca...]
    all_to_all x1, starting transfers between devices: 8.62 us -> 7.09 us  [body(): lax.all_to_all(jnp.stack(sent, axis=1), ('yhi', 'z'), split_axis=0, conca...]
    pallas_call x1 -> x2, Pallas kernels: 3.9 us -> 4.67 us  [the longest x1 3.06 us: upper_rows(): pl.pallas_call(upper_kernel, in_specs=[SMEM_SPEC] * 2 + [VMEM_SPEC] * (2...]
  transfers between devices with their start and end apart: 19 -> 19, of which waited for: 8 -> 6; matrix products, arithmetic and copies ran while one was open for 1% -> 1% of each run, Pallas kernels for 9% -> 10%
where the time goes in v5:
time: 115 us
  starting transfers between devices  55 us (48%)
  waiting for transfers between devices  32.1 us (28%)
  Pallas kernels  14.7 us (13%)
  blocking collectives  9.48 us (8%)
  other arithmetic  1.8 us (2%)
  local copies, waits for them, and re-layouts  1.21 us (1%)
    ppermute x17, starting transfers between devices, shift(): lax.ppermute(value, axis, [(n, (n + by) % size) for n in range(size)])  39.8 us
    ppermute x17, waiting for transfers between devices, shift(): lax.ppermute(value, axis, [(n, (n + by) % size) for n in range(size)])  25.2 us
    all_to_all x1, blocking collectives, body(): lax.all_to_all(slots, ('ylo', 'core', 'x'), split_axis=0, concat_axis=0,...  9.48 us
    all_to_all x1, starting transfers between devices, body(): lax.all_to_all(turn(sums), ('yhi', 'z'), split_axis=0, concat_axis=0, til...  8.07 us
    all_to_all x1, starting transfers between devices, body(): lax.all_to_all(jnp.stack(sent, axis=1), ('yhi', 'z'), split_axis=0, conca...  7.09 us
    all_to_all x1, waiting for transfers between devices, body(): lax.all_to_all(turn(sums), ('yhi', 'z'), split_axis=0, concat_axis=0, til...  6.84 us
    pallas_call x1, Pallas kernels, pack(): pl.pallas_call(pack_kernel, in_specs=[SMEM_SPEC, VMEM_SPEC, HBM_SPEC, HBM...  3.29 us
    pallas_call x1, Pallas kernels, upper_rows(): pl.pallas_call(upper_kernel, in_specs=[SMEM_SPEC] * 2 + [VMEM_SPEC] * (2...  3.06 us
  transfers between devices with their start and end apart: 19, of which 6 were waited for; matrix products, arithmetic and copies ran while one was open for 1% of the time, Pallas kernels for 10%

profile of v5, /device:TPU:1, one launch (start us, length us, event | category | flops | bytes accessed | tf_op | source)
XLA Modules:
  0.0 115.0 jit_solution(5037119962670660720)
XLA Ops:
  0.6 7.8 %collective-permute-start = (bf16[2,16,1024]{2,1,0:T(8,128)(2,1)}, bf16[2,16,1024]{2,1,0:T(8,128)(2,1)S(1)}, u32[]{:S(2)}, u32[]{:S(2)}) collective-permute-start(bf16[2,16,1024]{2,1,0:T(8,128)(2,1)} %bitcast.41), channel_id=1, source_target_pairs={{0,4},{1,5},{2,6},{3,7},{4,0},{5,1},{6,2},{7,3},{8,12},{9,13},{10,... | collective-permute-start | bytes 196616 | tf_op jit(solution)/shard_map/ppermute | solution.py:327
  8.5 0.6 pad_add_fusion.index
  9.1 3.3 %pack.1 = (bf16[128,640]{1,0:T(8,128)(2,1)}, bf16[128,640]{1,0:T(8,128)(2,1)}, bf16[128,640]{1,0:T(8,128)(2,1)}, bf16[128,640]{1,0:T(8,128)(2,1)}, bf16[512,256]{1,0:T(8,128)(2,1)}) custom-call(s32[2]{0:T(128)} %pad_add_fusion.index, s32[128,128]{1,0:T(8,128)} %bitcast.34, bf16[1280,256]{1,0:T(8,128)(2,1)} %margin.1, bf16[1280,256]{1,0:T(8,128)(2,1)} %hamiltonian.1), custom_call_target="tpu_custom_call" | custom-call | tf_op jit(solution)/shard_map/pack/pallas_call | solution.py:90
  12.4 0.0 copy-start.7
  12.5 1.3 %collective-permute-start.3 = (bf16[2,2,16,1024]{3,2,1,0:T(8,128)(2,1)S(1)}, bf16[2,2,16,1024]{3,2,1,0:T(8,128)(2,1)S(1)}, u32[]{:S(2)}, u32[]{:S(2)}) collective-permute-start(bf16[2,2,16,1024]{3,2,1,0:T(8,128)(2,1)S(1)} %pad_maximum_fusion.3), channel_id=1, source_target_pairs={{0,2},{1,3},{2,4},{3,5},{4,6},{5,7},{6,0},{7,1},{8,10},{9,11},{10,... | collective-permute-start | bytes 393224 | tf_op jit(solution)/shard_map/ppermute | solution.py:327
  13.7 1.2 %collective-permute-start.4 = (bf16[16,8,640]{2,1,0:T(8,128)(2,1)}, bf16[16,8,640]{2,1,0:T(8,128)(2,1)S(1)}, u32[]{:S(2)}, u32[]{:S(2)}) collective-permute-start(bf16[16,8,640]{2,1,0:T(8,128)(2,1)} %bitcast.46), channel_id=1, source_target_pairs={{0,16},{16,32},{32,48},{48,0},{1,17},{17,33},{33,49},{49,1},{2,18}... | collective-permute-start | bytes 491528 | tf_op jit(solution)/shard_map/ppermute | solution.py:327
  14.9 2.4 %collective-permute-start.5 = (bf16[16,8,640]{2,1,0:T(8,128)(2,1)}, bf16[16,8,640]{2,1,0:T(8,128)(2,1)S(1)}, u32[]{:S(2)}, u32[]{:S(2)}) collective-permute-start(bf16[16,8,640]{2,1,0:T(8,128)(2,1)} %bitcast.45), channel_id=1, source_target_pairs={{0,32},{16,48},{32,0},{48,16},{1,33},{17,49},{33,1},{49,17},{2,34}... | collective-permute-start | bytes 491528 | tf_op jit(solution)/shard_map/ppermute | solution.py:327
  17.4 1.2 %collective-permute-start.6 = (bf16[16,8,640]{2,1,0:T(8,128)(2,1)}, bf16[16,8,640]{2,1,0:T(8,128)(2,1)S(1)}, u32[]{:S(2)}, u32[]{:S(2)}) collective-permute-start(bf16[16,8,640]{2,1,0:T(8,128)(2,1)} %bitcast.44), channel_id=1, source_target_pairs={{0,48},{16,0},{32,16},{48,32},{1,49},{17,1},{33,17},{49,33},{2,50}... | collective-permute-start | bytes 491528 | tf_op jit(solution)/shard_map/ppermute | solution.py:327
  18.5 1.9 %collective-permute-start.2 = (bf16[2,2,16,1024]{3,2,1,0:T(8,128)(2,1)S(1)}, bf16[2,2,16,1024]{3,2,1,0:T(8,128)(2,1)S(1)}, u32[]{:S(2)}, u32[]{:S(2)}) collective-permute-start(bf16[2,2,16,1024]{3,2,1,0:T(8,128)(2,1)S(1)} %pad_maximum_fusion.3), channel_id=1, source_target_pairs={{0,7},{1,0},{2,1},{3,2},{4,3},{5,4},{6,5},{7,6},{8,15},{9,8},{10,9... | collective-permute-start | bytes 393224 | tf_op jit(solution)/shard_map/ppermute | solution.py:327
  20.5 2.2 %collective-permute-start.1 = (bf16[2,2,16,1024]{3,2,1,0:T(8,128)(2,1)S(1)}, bf16[2,2,16,1024]{3,2,1,0:T(8,128)(2,1)S(1)}, u32[]{:S(2)}, u32[]{:S(2)}) collective-permute-start(bf16[2,2,16,1024]{3,2,1,0:T(8,128)(2,1)S(1)} %pad_maximum_fusion.3), channel_id=1, source_target_pairs={{0,1},{1,2},{2,3},{3,4},{4,5},{5,6},{6,7},{7,0},{8,9},{9,10},{10,1... | collective-permute-start | bytes 393224 | tf_op jit(solution)/shard_map/ppermute | solution.py:327
  22.7 0.0 collective-permute-done.2
  22.7 3.3 %collective-permute-done.1 = bf16[2,2,16,1024]{3,2,1,0:T(8,128)(2,1)S(1)} collective-permute-done((bf16[2,2,16,1024]{3,2,1,0:T(8,128)(2,1)S(1)}, bf16[2,2,16,1024]{3,2,1,0:T(8,128)(2,1)S(1)}, u32[]{:S(2)}, u32[]{:S(2)}) %collective-permute-start.1) | collective-permute-done | bytes 131104 | tf_op jit(solution)/shard_map/ppermute | solution.py:327
  26.0 0.0 collective-permute-done.4
  26.0 0.0 collective-permute-done.5
  26.0 0.0 collective-permute-done.6
  26.0 0.9 pad_maximum_fusion.1
  26.9 7.1 %all-to-all-start = ((bf16[16,4,8,640]{3,2,1,0:T(8,128)(2,1)}), bf16[16,4,8,640]{3,2,1,0:T(8,128)(2,1)S(1)}, u32[]{:S(2)}, u32[]{:S(2)}) async-start(bf16[16,4,8,640]{3,2,1,0:T(8,128)(2,1)} %pad_maximum_fusion.1), calls=%async_computation | async-start | bytes 1310720 | tf_op jit(solution)/shard_map/all_to_all | solution.py:357
  34.1 3.0 %collective-permute-start.10 = (bf16[4,2,16,1024]{3,2,1,0:T(8,128)(2,1)S(1)}, bf16[4,2,16,1024]{3,2,1,0:T(8,128)(2,1)S(1)}, u32[]{:S(2)}, u32[]{:S(2)}) collective-permute-start(bf16[4,2,16,1024]{3,2,1,0:T(8,128)(2,1)S(1)} %constant_dynamic-update-slice_fusion.2.refs_4_), channel_id=1, source_target_pairs={{0,8},{8,0},{1,9},{9,1},{2,10},{10,2},{3,11},{11,3},{4,12},{12,4},... | collective-permute-start | bytes 786440 | tf_op jit(solution)/shard_map/ppermute | solution.py:327
  37.1 1.4 %collective-permute-start.9 = (bf16[4,2,16,1024]{3,2,1,0:T(8,128)(2,1)S(1)}, bf16[4,2,16,1024]{3,2,1,0:T(8,128)(2,1)S(1)}, u32[]{:S(2)}, u32[]{:S(2)}) collective-permute-start(bf16[4,2,16,1024]{3,2,1,0:T(8,128)(2,1)S(1)} %constant_dynamic-update-slice_fusion.refs_0_), channel_id=1, source_target_pairs={{0,48},{16,0},{32,16},{48,32},{1,49},{17,1},{33,17},{49,33},{2,50}... | collective-permute-start | bytes 786440 | tf_op jit(solution)/shard_map/ppermute | solution.py:327
  38.5 0.6 collective-permute-start.8
  39.1 0.3 collective-permute-start.7
  39.3 3.6 %collective-permute-done.10.refs_5_ = bf16[4,2,16,1024]{3,2,1,0:T(8,128)(2,1)S(1)} collective-permute-done((bf16[4,2,16,1024]{3,2,1,0:T(8,128)(2,1)S(1)}, bf16[4,2,16,1024]{3,2,1,0:T(8,128)(2,1)S(1)}, u32[]{:S(2)}, u32[]{:S(2)}) %collective-permute-start.10) | collective-permute-done | bytes 262176 | tf_op jit(solution)/shard_map/ppermute | solution.py:327
  42.9 2.6 %collective-permute-done.8.refs_2_ = bf16[4,2,16,1024]{3,2,1,0:T(8,128)(2,1)S(1)} collective-permute-done((bf16[4,2,16,1024]{3,2,1,0:T(8,128)(2,1)S(1)}, bf16[4,2,16,1024]{3,2,1,0:T(8,128)(2,1)S(1)}, u32[]{:S(2)}, u32[]{:S(2)}) %collective-permute-start.8) | collective-permute-done | bytes 262176 | tf_op jit(solution)/shard_map/ppermute | solution.py:327
  45.6 2.8 %collective-permute-done.7.refs_1_ = bf16[4,2,16,1024]{3,2,1,0:T(8,128)(2,1)S(1)} collective-permute-done((bf16[4,2,16,1024]{3,2,1,0:T(8,128)(2,1)S(1)}, bf16[4,2,16,1024]{3,2,1,0:T(8,128)(2,1)S(1)}, u32[]{:S(2)}, u32[]{:S(2)}) %collective-permute-start.7) | collective-permute-done | bytes 262176 | tf_op jit(solution)/shard_map/ppermute | solution.py:327
  48.3 0.1 pad_maximum_fusion
  48.5 0.0 copy-start
  48.5 0.4 collective-permute-start.11
  48.9 1.5 %collective-permute-start.14 = (bf16[8,2,16,1024]{3,2,1,0:T(8,128)(2,1)S(1)}, bf16[8,2,16,1024]{3,2,1,0:T(8,128)(2,1)S(1)}, u32[]{:S(2)}, u32[]{:S(2)}) collective-permute-start(bf16[8,2,16,1024]{3,2,1,0:T(8,128)(2,1)S(1)} %constant_dynamic-update-slice_fusion.4), channel_id=1, source_target_pairs={{0,48},{16,0},{32,16},{48,32},{1,49},{17,1},{33,17},{49,33},{2,50}... | collective-permute-start | bytes 1572872 | tf_op jit(solution)/shard_map/ppermute | solution.py:327
  50.4 0.0 collective-permute-start.13
  50.4 0.8 collective-permute-start.12
  51.2 1.1 unpack.1
  52.3 0.0 copy-start.5
  52.3 0.5 collective-permute-start.15
  52.8 0.2 copy-done.5
  52.9 1.6 %start.1 = (bf16[1024,512]{1,0:T(8,128)(2,1)S(1)}, bf16[2,384,256]{2,1,0:T(8,128)(2,1)S(1)}) custom-call(s32[1,4]{1,0:T(1,128)S(1)} %copy-done.5, bf16[2,1024,256]{2,1,0:T(8,128)(2,1)S(1)} %bitcast.26, bf16[4,2,16,1024]{3,2,1,0:T(8,128)(2,1)S(1)} %constant_dynamic-update-slice_fusion.refs_0_, bf16[4,2,16,1024]{3,2,1,0:T(8,128)(2,1)S(1)} %collective-permute-done.7.refs_1_, ...), custom_call_target="tpu_custom_call" | custom-call | tf_op jit(solution)/shard_map/start/pallas_call | solution.py:157
  54.6 12.9 %collective-permute-done.15.own_far = bf16[640,256]{1,0:T(8,128)(2,1)S(1)} collective-permute-done((bf16[640,256]{1,0:T(8,128)(2,1)S(1)}, bf16[640,256]{1,0:T(8,128)(2,1)S(1)}, u32[]{:S(2)}, u32[]{:S(2)}) %collective-permute-start.15) | collective-permute-done | bytes 327712 | tf_op jit(solution)/shard_map/ppermute | solution.py:327
  67.4 0.1 pad_maximum_fusion.2
  67.5 13.5 %collective-permute-start.16 = (bf16[2,640,256]{2,1,0:T(8,128)(2,1)S(1)}, bf16[2,640,256]{2,1,0:T(8,128)(2,1)S(1)}, u32[]{:S(2)}, u32[]{:S(2)}) collective-permute-start(bf16[2,640,256]{2,1,0:T(8,128)(2,1)S(1)} %pad_maximum_fusion.2), channel_id=1, source_target_pairs={{0,64},{64,0},{1,65},{65,1},{2,66},{66,2},{3,67},{67,3},{4,68},{68... | collective-permute-start | bytes 1966088 | tf_op jit(solution)/shard_map/ppermute | solution.py:327
  81.0 3.1 %upper.1 = (bf16[2,1024,256]{2,1,0:T(8,128)(2,1)}, bf16[2,1024,256]{2,1,0:T(8,128)(2,1)S(1)}) custom-call(s32[2]{0:T(128)S(1)} %copy-done.4, s32[1,4]{1,0:T(1,128)S(1)} %copy-done.5, bf16[1024,512]{1,0:T(8,128)(2,1)S(1)} %get-tuple-element.66.rhs, bf16[2,384,256]{2,1,0:T(8,128)(2,1)S(1)} %get-tuple-element.70.early, ...), custom_call_target="tpu_custom_call" | custom-call | tf_op jit(solution)/shard_map/upper/pallas_call | solution.py:197
  84.1 0.0 copy-start.6
  84.1 0.9 copy-done.1
  85.0 2.0 %charge.1 = f32[16,8,128]{2,1,0:T(8,128)S(1)} custom-call(s32[2]{0:T(128)S(1)} %copy-done.4, f32[1,2]{1,0:T(1,128)S(1)} %copy-done.6, s32[1,4]{1,0:T(1,128)S(1)} %copy-done.5, bf16[2,1024,256]{2,1,0:T(8,128)(2,1)S(1)} %bitcast.27, bf16[2,256,256]{2,1,0:T(8,128)(2,1)S(1)} %bitcast.32, bf16[640,256]{1,0:T(8,128)(2,1)S(1)} %get-tuple-element.68.own, ...), custom_call_target="tpu_custom_call" | custom-call | tf_op jit(solution)/shard_map/charge/pallas_call | solution.py:241
  87.0 9.5 %all_to_all.15.arrived = f32[16,8,128]{2,1,0:T(8,128)S(1)} all-to-all(f32[16,8,128]{2,1,0:T(8,128)S(1)} %charge.1), channel_id=1, replica_groups=mesh['ylo'=2,'core'=2,'x'=4,'yhi'=2,'z'=8] {'ylo','core','x'}, dimensions={0} | all-to-all | bytes 131072 | tf_op jit(solution)/shard_map/all_to_all | solution.py:374
  96.5 0.7 turn.1
  97.2 8.1 %all-to-all-start.2 = ((f32[16,8,128]{2,1,0:T(8,128)}), f32[16,8,128]{2,1,0:T(8,128)S(1)}, u32[]{:S(2)}, u32[]{:S(2)}) async-start(f32[16,8,128]{2,1,0:T(8,128)} %turn.1), calls=%async_computation.2 | async-start | bytes 131072 | tf_op jit(solution)/shard_map/all_to_all | solution.py:375
  105.3 2.0 %diag.1 = bf16[2,256,256]{2,1,0:T(8,128)(2,1)} custom-call(s32[1,4]{1,0:T(1,128)S(1)} %copy-done.5, bf16[2,1024,256]{2,1,0:T(8,128)(2,1)S(1)} %bitcast.28, bf16[2,1024,256]{2,1,0:T(8,128)(2,1)S(1)} %get-tuple-element.76.upper, bf16[2,256,256]{2,1,0:T(8,128)(2,1)S(1)} %bitcast.33), custom_call_target="tpu_custom_call" | custom-call | tf_op jit(solution)/shard_map/diag/pallas_call | solution.py:268
  107.3 6.8 %all-to-all-done.2.arrived = f32[16,8,128]{2,1,0:T(8,128)S(1)} async-done(((f32[16,8,128]{2,1,0:T(8,128)}), f32[16,8,128]{2,1,0:T(8,128)S(1)}, u32[]{:S(2)}, u32[]{:S(2)}) %all-to-all-start.2) | async-done | bytes 65568 | tf_op jit(solution)/shard_map/all_to_all | solution.py:375
  114.2 0.9 place.1
  (29 shorter events, 0.2 us)
Async XLA Ops:
  0.6 11.8 %collective-permute-start = (bf16[2,16,1024]{2,1,0:T(8,128)(2,1)}, bf16[2,16,1024]{2,1,0:T(8,128)(2,1)S(1)}, u32[]{:S(2)}, u32[]{:S(2)}) collective-permute-start(bf16[2,16,1024]{2,1,0:T(8,128)(2,1)} %bitcast.41), channel_id=1, source_target_pairs={{0,4},{1,5},{2,6},{3,7},{4,0},{5,1},{6,2},{7,3},{8,12},{9,13},{10,... | collective-permute-start | bytes 196616 | tf_op jit(solution)/shard_map/ppermute | solution.py:327
  9.1 3.3 %copy-start.8 = (bf16[1,2,16,1024]{3,2,1,0:T(8,128)(2,1)S(1)}, bf16[1,2,16,1024]{3,2,1,0:T(8,128)(2,1)}, u32[]{:S(2)}) copy-start(bf16[1,2,16,1024]{3,2,1,0:T(8,128)(2,1)} %param.8) | copy-start | bytes 196612
  12.4 13.6 %copy-start.7 = (bf16[128,640]{1,0:T(8,128)(2,1)S(1)}, bf16[128,640]{1,0:T(8,128)(2,1)}, u32[]{:S(2)}) copy-start(bf16[128,640]{1,0:T(8,128)(2,1)} %get-tuple-element.48) | copy-start | bytes 491524
  12.5 8.0 %collective-permute-start.3 = (bf16[2,2,16,1024]{3,2,1,0:T(8,128)(2,1)S(1)}, bf16[2,2,16,1024]{3,2,1,0:T(8,128)(2,1)S(1)}, u32[]{:S(2)}, u32[]{:S(2)}) collective-permute-start(bf16[2,2,16,1024]{3,2,1,0:T(8,128)(2,1)S(1)} %pad_maximum_fusion.3), channel_id=1, source_target_pairs={{0,2},{1,3},{2,4},{3,5},{4,6},{5,7},{6,0},{7,1},{8,10},{9,11},{10,... | collective-permute-start | bytes 393224 | tf_op jit(solution)/shard_map/ppermute | solution.py:327
  13.7 12.3 %collective-permute-start.4 = (bf16[16,8,640]{2,1,0:T(8,128)(2,1)}, bf16[16,8,640]{2,1,0:T(8,128)(2,1)S(1)}, u32[]{:S(2)}, u32[]{:S(2)}) collective-permute-start(bf16[16,8,640]{2,1,0:T(8,128)(2,1)} %bitcast.46), channel_id=1, source_target_pairs={{0,16},{16,32},{32,48},{48,0},{1,17},{17,33},{33,49},{49,1},{2,18}... | collective-permute-start | bytes 491528 | tf_op jit(solution)/shard_map/ppermute | solution.py:327
  14.9 11.0 %collective-permute-start.5 = (bf16[16,8,640]{2,1,0:T(8,128)(2,1)}, bf16[16,8,640]{2,1,0:T(8,128)(2,1)S(1)}, u32[]{:S(2)}, u32[]{:S(2)}) collective-permute-start(bf16[16,8,640]{2,1,0:T(8,128)(2,1)} %bitcast.45), channel_id=1, source_target_pairs={{0,32},{16,48},{32,0},{48,16},{1,33},{17,49},{33,1},{49,17},{2,34}... | collective-permute-start | bytes 491528 | tf_op jit(solution)/shard_map/ppermute | solution.py:327
  17.4 8.6 %collective-permute-start.6 = (bf16[16,8,640]{2,1,0:T(8,128)(2,1)}, bf16[16,8,640]{2,1,0:T(8,128)(2,1)S(1)}, u32[]{:S(2)}, u32[]{:S(2)}) collective-permute-start(bf16[16,8,640]{2,1,0:T(8,128)(2,1)} %bitcast.44), channel_id=1, source_target_pairs={{0,48},{16,0},{32,16},{48,32},{1,49},{17,1},{33,17},{49,33},{2,50}... | collective-permute-start | bytes 491528 | tf_op jit(solution)/shard_map/ppermute | solution.py:327
  18.5 4.1 %collective-permute-start.2 = (bf16[2,2,16,1024]{3,2,1,0:T(8,128)(2,1)S(1)}, bf16[2,2,16,1024]{3,2,1,0:T(8,128)(2,1)S(1)}, u32[]{:S(2)}, u32[]{:S(2)}) collective-permute-start(bf16[2,2,16,1024]{3,2,1,0:T(8,128)(2,1)S(1)} %pad_maximum_fusion.3), channel_id=1, source_target_pairs={{0,7},{1,0},{2,1},{3,2},{4,3},{5,4},{6,5},{7,6},{8,15},{9,8},{10,9... | collective-permute-start | bytes 393224 | tf_op jit(solution)/shard_map/ppermute | solution.py:327
  20.5 5.5 %collective-permute-start.1 = (bf16[2,2,16,1024]{3,2,1,0:T(8,128)(2,1)S(1)}, bf16[2,2,16,1024]{3,2,1,0:T(8,128)(2,1)S(1)}, u32[]{:S(2)}, u32[]{:S(2)}) collective-permute-start(bf16[2,2,16,1024]{3,2,1,0:T(8,128)(2,1)S(1)} %pad_maximum_fusion.3), channel_id=1, source_target_pairs={{0,1},{1,2},{2,3},{3,4},{4,5},{5,6},{6,7},{7,0},{8,9},{9,10},{10,1... | collective-permute-start | bytes 393224 | tf_op jit(solution)/shard_map/ppermute | solution.py:327
  26.9 21.4 %all-to-all-start = ((bf16[16,4,8,640]{3,2,1,0:T(8,128)(2,1)}), bf16[16,4,8,640]{3,2,1,0:T(8,128)(2,1)S(1)}, u32[]{:S(2)}, u32[]{:S(2)}) async-start(bf16[16,4,8,640]{3,2,1,0:T(8,128)(2,1)} %pad_maximum_fusion.1), calls=%async_computation | async-start | bytes 1310720 | tf_op jit(solution)/shard_map/all_to_all | solution.py:357
  34.1 8.9 %collective-permute-start.10 = (bf16[4,2,16,1024]{3,2,1,0:T(8,128)(2,1)S(1)}, bf16[4,2,16,1024]{3,2,1,0:T(8,128)(2,1)S(1)}, u32[]{:S(2)}, u32[]{:S(2)}) collective-permute-start(bf16[4,2,16,1024]{3,2,1,0:T(8,128)(2,1)S(1)} %constant_dynamic-update-slice_fusion.2.refs_4_), channel_id=1, source_target_pairs={{0,8},{8,0},{1,9},{9,1},{2,10},{10,2},{3,11},{11,3},{4,12},{12,4},... | collective-permute-start | bytes 786440 | tf_op jit(solution)/shard_map/ppermute | solution.py:327
  37.1 5.9 %collective-permute-start.9 = (bf16[4,2,16,1024]{3,2,1,0:T(8,128)(2,1)S(1)}, bf16[4,2,16,1024]{3,2,1,0:T(8,128)(2,1)S(1)}, u32[]{:S(2)}, u32[]{:S(2)}) collective-permute-start(bf16[4,2,16,1024]{3,2,1,0:T(8,128)(2,1)S(1)} %constant_dynamic-update-slice_fusion.refs_0_), channel_id=1, source_target_pairs={{0,48},{16,0},{32,16},{48,32},{1,49},{17,1},{33,17},{49,33},{2,50}... | collective-permute-start | bytes 786440 | tf_op jit(solution)/shard_map/ppermute | solution.py:327
  38.5 7.1 %collective-permute-start.8 = (bf16[4,2,16,1024]{3,2,1,0:T(8,128)(2,1)S(1)}, bf16[4,2,16,1024]{3,2,1,0:T(8,128)(2,1)S(1)}, u32[]{:S(2)}, u32[]{:S(2)}) collective-permute-start(bf16[4,2,16,1024]{3,2,1,0:T(8,128)(2,1)S(1)} %constant_dynamic-update-slice_fusion.refs_0_), channel_id=1, source_target_pairs={{0,32},{16,48},{32,0},{48,16},{1,33},{17,49},{33,1},{49,17},{2,34}... | collective-permute-start | bytes 786440 | tf_op jit(solution)/shard_map/ppermute | solution.py:327
  39.1 9.3 %collective-permute-start.7 = (bf16[4,2,16,1024]{3,2,1,0:T(8,128)(2,1)S(1)}, bf16[4,2,16,1024]{3,2,1,0:T(8,128)(2,1)S(1)}, u32[]{:S(2)}, u32[]{:S(2)}) collective-permute-start(bf16[4,2,16,1024]{3,2,1,0:T(8,128)(2,1)S(1)} %constant_dynamic-update-slice_fusion.refs_0_), channel_id=1, source_target_pairs={{0,16},{16,32},{32,48},{48,0},{1,17},{17,33},{33,49},{49,1},{2,18}... | collective-permute-start | bytes 786440 | tf_op jit(solution)/shard_map/ppermute | solution.py:327
  48.3 2.8 %copy-start.2 = (s32[16384]{0:T(1024)S(1)}, s32[16384]{0:T(1024)}, u32[]{:S(2)}) copy-start(s32[16384]{0:T(1024)} %param.15) | copy-start | bytes 196612
  48.5 4.3 %copy-start = (bf16[1,2,1024,256]{3,2,1,0:T(8,128)(2,1)S(1)}, bf16[1,2,1024,256]{3,2,1,0:T(8,128)(2,1)}, u32[]{:S(2)}) copy-start(bf16[1,2,1024,256]{3,2,1,0:T(8,128)(2,1)} %param.9) | copy-start | bytes 3145732
  48.5 19.0 %collective-permute-start.11 = (bf16[16,2,16,1024]{3,2,1,0:T(8,128)(2,1)S(1)}, bf16[16,2,16,1024]{3,2,1,0:T(8,128)(2,1)S(1)}, u32[]{:S(2)}, u32[]{:S(2)}) collective-permute-start(bf16[16,2,16,1024]{3,2,1,0:T(8,128)(2,1)S(1)} %pad_maximum_fusion), channel_id=1, source_target_pairs={{0,8},{8,0},{1,9},{9,1},{2,10},{10,2},{3,11},{11,3},{4,12},{12,4},... | collective-permute-start | bytes 3145736 | tf_op jit(solution)/shard_map/ppermute | solution.py:327
  48.9 2.3 %copy-start.4 = (s32[2]{0:T(128)S(1)}, s32[2]{0:T(128)}, u32[]{:S(2)}) copy-start(s32[2]{0:T(128)} %pad_add_fusion.index) | copy-start | bytes 28
  48.9 18.5 %collective-permute-start.14 = (bf16[8,2,16,1024]{3,2,1,0:T(8,128)(2,1)S(1)}, bf16[8,2,16,1024]{3,2,1,0:T(8,128)(2,1)S(1)}, u32[]{:S(2)}, u32[]{:S(2)}) collective-permute-start(bf16[8,2,16,1024]{3,2,1,0:T(8,128)(2,1)S(1)} %constant_dynamic-update-slice_fusion.4), channel_id=1, source_target_pairs={{0,48},{16,0},{32,16},{48,32},{1,49},{17,1},{33,17},{49,33},{2,50}... | collective-permute-start | bytes 1572872 | tf_op jit(solution)/shard_map/ppermute | solution.py:327
  50.4 17.1 %collective-permute-start.13 = (bf16[8,2,16,1024]{3,2,1,0:T(8,128)(2,1)S(1)}, bf16[8,2,16,1024]{3,2,1,0:T(8,128)(2,1)S(1)}, u32[]{:S(2)}, u32[]{:S(2)}) collective-permute-start(bf16[8,2,16,1024]{3,2,1,0:T(8,128)(2,1)S(1)} %constant_dynamic-update-slice_fusion.4), channel_id=1, source_target_pairs={{0,32},{16,48},{32,0},{48,16},{1,33},{17,49},{33,1},{49,17},{2,34}... | collective-permute-start | bytes 1572872 | tf_op jit(solution)/shard_map/ppermute | solution.py:327
  50.4 17.0 %collective-permute-start.12 = (bf16[8,2,16,1024]{3,2,1,0:T(8,128)(2,1)S(1)}, bf16[8,2,16,1024]{3,2,1,0:T(8,128)(2,1)S(1)}, u32[]{:S(2)}, u32[]{:S(2)}) collective-permute-start(bf16[8,2,16,1024]{3,2,1,0:T(8,128)(2,1)S(1)} %constant_dynamic-update-slice_fusion.4), channel_id=1, source_target_pairs={{0,16},{16,32},{32,48},{48,0},{1,17},{17,33},{33,49},{49,1},{2,18}... | collective-permute-start | bytes 1572872 | tf_op jit(solution)/shard_map/ppermute | solution.py:327
  52.3 0.7 copy-start.5
  52.3 15.1 %collective-permute-start.15 = (bf16[640,256]{1,0:T(8,128)(2,1)S(1)}, bf16[640,256]{1,0:T(8,128)(2,1)S(1)}, u32[]{:S(2)}, u32[]{:S(2)}) collective-permute-start(bf16[640,256]{1,0:T(8,128)(2,1)S(1)} %get-tuple-element.68.own), channel_id=1, source_target_pairs={{0,128},{128,0},{1,129},{129,1},{2,130},{130,2},{3,131},{131,3},{4... | collective-permute-start | bytes 983048 | tf_op jit(solution)/shard_map/ppermute | solution.py:327
  67.5 16.5 %collective-permute-start.16 = (bf16[2,640,256]{2,1,0:T(8,128)(2,1)S(1)}, bf16[2,640,256]{2,1,0:T(8,128)(2,1)S(1)}, u32[]{:S(2)}, u32[]{:S(2)}) collective-permute-start(bf16[2,640,256]{2,1,0:T(8,128)(2,1)S(1)} %pad_maximum_fusion.2), channel_id=1, source_target_pairs={{0,64},{64,0},{1,65},{65,1},{2,66},{66,2},{3,67},{67,3},{4,68},{68... | collective-permute-start | bytes 1966088 | tf_op jit(solution)/shard_map/ppermute | solution.py:327
  84.0 0.9 copy-start.1
  84.1 0.9 copy-start.6
  97.2 17.0 %all-to-all-start.2 = ((f32[16,8,128]{2,1,0:T(8,128)}), f32[16,8,128]{2,1,0:T(8,128)S(1)}, u32[]{:S(2)}, u32[]{:S(2)}) async-start(f32[16,8,128]{2,1,0:T(8,128)} %turn.1), calls=%async_computation.2 | async-start | bytes 131072 | tf_op jit(solution)/shard_map/all_to_all | solution.py:375
  105.3 8.9 %copy-start.3 = (bf16[512,256]{1,0:T(8,128)(2,1)S(1)}, bf16[512,256]{1,0:T(8,128)(2,1)}, u32[]{:S(2)}) copy-start(bf16[512,256]{1,0:T(8,128)(2,1)} %get-tuple-element.79.onehot) | copy-start | bytes 786436

commit v6 on v5

--- a/solution.py
+++ b/solution.py
@@ -19,6 +19,7 @@
 ROWS = 1280
 QUARTER = ROWS // POLES
 SHARD = ANC // GROUPS
+PART = 896
 MIB = 1024 * 1024
 SMEM_SPEC = pl.BlockSpec(memory_space=pltpu.SMEM)
 VMEM_SPEC = pl.BlockSpec(memory_space=pltpu.VMEM)
@@ -129,45 +130,52 @@
 UP, DOWN = (0, 4, 1, 5), (7, 3, 2, 6)
 
 
-def product(refs, rhs):
-    left, right = [
-        mm(jnp.concatenate([ref[:, part].reshape(-1, ANC) for ref in refs], axis=0), rhs[...]) for part in range(2)
-    ]
+def product(lefts, rhs):
+    left, right = [mm(lefts(part), rhs) for part in range(2)]
     return right[:, COLS:] - left[:, :COLS], -left[:, COLS:] - right[:, :COLS]
 
 
-def start_kernel(fill, lower, *refs):
-    first, second, (rhs, out) = refs[:4], refs[4:6], refs[6:]
+def rows_of(refs, part, columns):
+    return jnp.concatenate([ref[:, part, :, columns].reshape(-1, columns.stop - columns.start) for ref in refs], axis=0)
+
+
+WHOLE, NEAR, REST = slice(0, ANC), slice(0, PART), slice(ANC, 2 * ANC - PART)
+
+
+def start_kernel(weights, fill, lower, diag_inverse, *refs):
+    first, second, (rhs, out, sums) = refs[:4], refs[4:6], refs[6:]
     for block in range(ANC // COLS):
         keep = fill[0, block].astype(F32).astype(BF16)
         span = slice(block * COLS, (block + 1) * COLS)
         for part in range(2):
             rhs[span, part * COLS : (part + 1) * COLS] = lower[part, span, :] * keep
+    sums[...] = weights[0, 0] * diag_inverse[1].astype(F32) + weights[0, 1] * diag_inverse[0].astype(F32)
     rows = 0
-    for group in (first, second):
-        real, imag = product(group, rhs)
+    for group, columns in ((first, NEAR), (second, WHOLE)):
+        real, imag = product(lambda part: rows_of(group, part, columns), rhs[columns, :])
         span = slice(rows, rows + real.shape[0])
-        out[0, span, :] = real.astype(BF16)
-        out[1, span, :] = imag.astype(BF16)
+        out[0, span, :] = real
+        out[1, span, :] = imag
         rows = rows + real.shape[0]
 
 
-def start_rows(fill, lower, pieces):
+def start_rows(weights, fill, lower, diag_inverse, pieces):
     rows = sum(value.shape[0] for value in pieces) * SHARD
     return pl.pallas_call(
         start_kernel,
-        in_specs=[SMEM_SPEC] + [VMEM_SPEC] * (1 + len(pieces)),
-        out_specs=[VMEM_SPEC] * 2,
+        in_specs=[SMEM_SPEC] * 2 + [VMEM_SPEC] * (2 + len(pieces)),
+        out_specs=[VMEM_SPEC] * 3,
         out_shape=[
             jax.ShapeDtypeStruct((ANC, 2 * COLS), BF16),
-            jax.ShapeDtypeStruct((2, rows, COLS), BF16),
+            jax.ShapeDtypeStruct((2, rows, COLS), F32),
+            jax.ShapeDtypeStruct((COLS, COLS), F32),
         ],
         compiler_params=params(16),
         name="start",
-    )(fill, lower, *pieces)
-
-
-def upper_kernel(index, fill, rhs, early, first_y, second_1, second_2, second_3, *outs):
+    )(weights, fill, lower, diag_inverse, *pieces)
+
+
+def upper_kernel(index, fill, rhs, early, first_y, second_0, second_y, second_1, second_2, second_3, *outs):
     grid = index[1]
     x, y, z = grid >> 4, (grid >> 3) & 1, grid & 7
 
@@ -178,17 +186,22 @@
             keep = fill[0, px].astype(F32)
             span = slice(n * SHARD, (n + 1) * SHARD)
             for part, value in enumerate((real, imag)):
-                rows = (value[span].astype(F32) * keep).astype(BF16)
+                rows = (value[span] * keep).astype(BF16)
                 for out in outs:
                     out[part, here, :] = rows
 
     def places(dxs, dys, dzs):
         return [(dx, dy, dz) for dx in dxs for dy in dys for dz in dzs]
 
-    scatter(early[0], early[1], places(range(NX), (0,), UP) + places((0,), range(NY), DOWN))
-    real, imag = product([first_y], rhs)
-    scatter(real, imag, places(range(NX), (1,), UP))
-    real, imag = product([second_1, second_2, second_3], rhs)
+    far = (second_1, second_2, second_3)
+    own = NX * len(UP) * SHARD
+    real, imag = product(lambda part: rows_of([second_0] + [ref.at[0:4] for ref in far], part, REST), rhs[PART:ANC, :])
+    scatter(real + early[0, 0:own, :], imag + early[1, 0:own, :], places(range(NX), (0,), UP))
+    scatter(early[0, own:, :], early[1, own:, :], places((0,), range(NY), DOWN))
+    real, imag = product(lambda part: rows_of([second_y] + [ref.at[4:8] for ref in far], part, REST), rhs[PART:ANC, :])
+    more_real, more_imag = product(lambda part: rows_of([first_y], part, NEAR), rhs[NEAR, :])
+    scatter(real + more_real, imag + more_imag, places(range(NX), (1,), UP))
+    real, imag = product(lambda part: rows_of(far, part, WHOLE), rhs[...])
     scatter(real, imag, places((1, 2, 3), range(NY), DOWN))
 
 
@@ -204,16 +217,15 @@
     )(index, fill, rhs, early, *pieces)
 
 
-def charge_kernel(index, weights, fill, lower, diag_inverse, own, own_far, mate, mate_far, upper, onehot, slots, rows):
+def charge_kernel(index, weights, fill, lower, sums, own, own_far, mate, mate_far, upper, onehot, slots, rows):
     pole, x = index[0], index[1] >> 4
     for bits, ref in ((0, own), (2, own_far), (1, mate), (3, mate_far)):
         start = pl.multiple_of((pole ^ bits) * QUARTER, QUARTER)
         for which in range(2):
             rows[which, pl.ds(start, QUARTER), :] = ref[which * QUARTER : (which + 1) * QUARTER, :]
     real, imag = weights[0, 0], weights[0, 1]
-    sums = real * diag_inverse[1].astype(F32) + imag * diag_inverse[0].astype(F32)
     nears = [rows[which, 0:COLS, :] for which in range(2)]
-    totals = [jnp.sum(sums * near.astype(F32), axis=0, keepdims=True) for near in nears]
+    totals = [jnp.sum(sums[...] * near.astype(F32), axis=0, keepdims=True) for near in nears]
     both = jnp.concatenate(nears, axis=1)
     for block in range(ANC // COLS):
         keep = fill[0, block].astype(F32)
@@ -237,7 +249,7 @@
             slots[n * NX + px] = result[:, px * width : (px + 1) * width]
 
 
-def charge_slots(index, weights, fill, lower, diag_inverse, quarters, upper, onehot):
+def charge_slots(index, weights, fill, lower, sums, quarters, upper, onehot):
     return pl.pallas_call(
         charge_kernel,
         in_specs=[SMEM_SPEC] * 3 + [VMEM_SPEC] * (4 + len(quarters)),
@@ -246,7 +258,7 @@
         scratch_shapes=[pltpu.VMEM((2, ROWS, COLS), BF16)],
         compiler_params=params(24),
         name="charge",
-    )(index, weights, fill, lower, diag_inverse, *quarters, upper, onehot)
+    )(index, weights, fill, lower, sums, *quarters, upper, onehot)
 
 
 def diag_kernel(fill, lower, upper, diag_inverse, out):
@@ -351,7 +363,8 @@
     near, near_up, near_down, near_two, *sent = lax.optimization_barrier((near, near_up, near_down, near_two, *sent))
 
     first = jnp.concatenate([near, near_up])
-    second = jnp.concatenate([near_down, near_two])
+    second = jnp.concatenate([jnp.concatenate([near_down, near_two]), first[..., PART:]], axis=-1)
+    first = first[..., :PART]
     first_x = [first] + [shift(first, "x", d) for d in (1, 2, 3)]
     second_y = [second, shift(second, "yhi", 1)]
     arrived = lax.all_to_all(jnp.stack(sent, axis=1), ("yhi", "z"), split_axis=0, concat_axis=0, tiled=True)
@@ -362,14 +375,14 @@
     second_x = [shift(second_all, "x", d) for d in (1, 2, 3)]
     mine, column_onehot = unpack(index, table, arrived.reshape(SLOTS, 2 * QUARTER))
     mine_far = shift(mine, "ylo", 1)
-    rhs, early = start_rows(fill_pattern, lower, first_x + second_y)
+    rhs, early, sums = start_rows(pole_weights, fill_pattern, lower, inverse, first_x + second_y)
     first_y, second_x, mine_far, early = lax.optimization_barrier((first_y, second_x, mine_far, early))
 
     mates = shift(jnp.stack([mine, mine_far]), "core", 1)
     mate, mate_far = mates[0], mates[1]
-    upper, upper_again = upper_rows(index, fill_pattern, rhs, early, [first_y] + second_x)
+    upper, upper_again = upper_rows(index, fill_pattern, rhs, early, [first_y] + second_y + second_x)
     quarters = [mine, mine_far, mate, mate_far]
-    slots = charge_slots(index, pole_weights, fill_pattern, lower, inverse, quarters, upper_again, column_onehot)
+    slots = charge_slots(index, pole_weights, fill_pattern, lower, sums, quarters, upper_again, column_onehot)
     diag = diag_block(fill_pattern, lower, upper_again, inverse)
     sums = lax.all_to_all(slots, ("ylo", "core", "x"), split_axis=0, concat_axis=0, tiled=True)
     sums = lax.all_to_all(turn(sums), ("yhi", "z"), split_axis=0, concat_axis=0, tiled=True)

time: 115 us -> 115 us (level)
  starting transfers between devices: 55 us -> 46 us
  waiting for transfers between devices: 32.1 us -> 41 us
    ppermute x17, starting transfers between devices: 39.8 us -> 29.1 us  [shift(): lax.ppermute(value, axis, [(n, (n + by) % size) for n in range(size)])]
    ppermute x17, waiting for transfers between devices: 25.2 us -> 34.1 us  [shift(): lax.ppermute(value, axis, [(n, (n + by) % size) for n in range(size)])]
    all_to_all x1, starting transfers between devices: 8.07 us -> 9.86 us  [body(): lax.all_to_all(turn(sums), ('yhi', 'z'), split_axis=0, concat_axis=0, til...]
  transfers between devices with their start and end apart: 19 -> 19, of which waited for: 6 -> 7; matrix products, arithmetic and copies ran while one was open for 1% -> 1% of each run, Pallas kernels for 10% -> 10%
where the time goes in v6:
time: 115 us; the launch traced here: 114 us
  starting transfers between devices  46 us (40%)
  waiting for transfers between devices  41 us (36%)
  Pallas kernels  15 us (13%)
  blocking collectives  8.5 us (7%)
  other arithmetic  1.8 us (2%)
  local copies, waits for them, and re-layouts  1.36 us (1%)
    ppermute x17, waiting for transfers between devices, shift(): lax.ppermute(value, axis, [(n, (n + by) % size) for n in range(size)])  34.1 us
    ppermute x17, starting transfers between devices, shift(): lax.ppermute(value, axis, [(n, (n + by) % size) for n in range(size)])  29.1 us
    all_to_all x1, starting transfers between devices, body(): lax.all_to_all(turn(sums), ('yhi', 'z'), split_axis=0, concat_axis=0, til...  9.86 us
    all_to_all x1, blocking collectives, body(): lax.all_to_all(slots, ('ylo', 'core', 'x'), split_axis=0, concat_axis=0,...  8.5 us
    all_to_all x1, starting transfers between devices, body(): lax.all_to_all(jnp.stack(sent, axis=1), ('yhi', 'z'), split_axis=0, conca...  7.09 us
    all_to_all x1, waiting for transfers between devices, body(): lax.all_to_all(turn(sums), ('yhi', 'z'), split_axis=0, concat_axis=0, til...  6.84 us
    pallas_call x1, Pallas kernels, upper_rows(): pl.pallas_call(upper_kernel, in_specs=[SMEM_SPEC] * 2 + [VMEM_SPEC] * (2...  3.41 us
    pallas_call x1, Pallas kernels, pack(): pl.pallas_call(pack_kernel, in_specs=[SMEM_SPEC, VMEM_SPEC, HBM_SPEC, HBM...  3.29 us
  transfers between devices with their start and end apart: 19, of which 7 were waited for; matrix products, arithmetic and copies ran while one was open for 1% of the time, Pallas kernels for 10%

profile of v6, /device:TPU:1, one launch (start us, length us, event | category | flops | bytes accessed | tf_op | source)
XLA Modules:
  0.0 114.5 jit_solution(322161670700714239)
XLA Ops:
  0.6 7.8 %collective-permute-start = (bf16[2,16,1024]{2,1,0:T(8,128)(2,1)}, bf16[2,16,1024]{2,1,0:T(8,128)(2,1)S(1)}, u32[]{:S(2)}, u32[]{:S(2)}) collective-permute-start(bf16[2,16,1024]{2,1,0:T(8,128)(2,1)} %bitcast.41), channel_id=1, source_target_pairs={{0,4},{1,5},{2,6},{3,7},{4,0},{5,1},{6,2},{7,3},{8,12},{9,13},{10,... | collective-permute-start | bytes 196616 | tf_op jit(solution)/shard_map/ppermute | solution.py:339
  8.5 0.6 pad_add_fusion.index
  9.1 3.3 %pack.1 = (bf16[128,640]{1,0:T(8,128)(2,1)}, bf16[128,640]{1,0:T(8,128)(2,1)}, bf16[128,640]{1,0:T(8,128)(2,1)}, bf16[128,640]{1,0:T(8,128)(2,1)}, bf16[512,256]{1,0:T(8,128)(2,1)}) custom-call(s32[2]{0:T(128)} %pad_add_fusion.index, s32[128,128]{1,0:T(8,128)} %bitcast.34, bf16[1280,256]{1,0:T(8,128)(2,1)} %margin.1, bf16[1280,256]{1,0:T(8,128)(2,1)} %hamiltonian.1), custom_call_target="tpu_custom_call" | custom-call | tf_op jit(solution)/shard_map/pack/pallas_call | solution.py:91
  12.4 0.0 copy-start.9
  12.4 0.0 collective-permute-done
  12.4 1.3 %collective-permute-start.3 = (bf16[2,2,16,1024]{3,2,1,0:T(8,128)(2,1)S(1)}, bf16[2,2,16,1024]{3,2,1,0:T(8,128)(2,1)S(1)}, u32[]{:S(2)}, u32[]{:S(2)}) collective-permute-start(bf16[2,2,16,1024]{3,2,1,0:T(8,128)(2,1)S(1)} %pad_maximum_fusion.4), channel_id=1, source_target_pairs={{0,2},{1,3},{2,4},{3,5},{4,6},{5,7},{6,0},{7,1},{8,10},{9,11},{10,... | collective-permute-start | bytes 393224 | tf_op jit(solution)/shard_map/ppermute | solution.py:339
  13.7 1.2 %collective-permute-start.4 = (bf16[16,8,640]{2,1,0:T(8,128)(2,1)}, bf16[16,8,640]{2,1,0:T(8,128)(2,1)S(1)}, u32[]{:S(2)}, u32[]{:S(2)}) collective-permute-start(bf16[16,8,640]{2,1,0:T(8,128)(2,1)} %bitcast.46), channel_id=1, source_target_pairs={{0,16},{16,32},{32,48},{48,0},{1,17},{17,33},{33,49},{49,1},{2,18}... | collective-permute-start | bytes 491528 | tf_op jit(solution)/shard_map/ppermute | solution.py:339
  14.9 2.4 %collective-permute-start.5 = (bf16[16,8,640]{2,1,0:T(8,128)(2,1)}, bf16[16,8,640]{2,1,0:T(8,128)(2,1)S(1)}, u32[]{:S(2)}, u32[]{:S(2)}) collective-permute-start(bf16[16,8,640]{2,1,0:T(8,128)(2,1)} %bitcast.45), channel_id=1, source_target_pairs={{0,32},{16,48},{32,0},{48,16},{1,33},{17,49},{33,1},{49,17},{2,34}... | collective-permute-start | bytes 491528 | tf_op jit(solution)/shard_map/ppermute | solution.py:339
  17.3 1.2 %collective-permute-start.6 = (bf16[16,8,640]{2,1,0:T(8,128)(2,1)}, bf16[16,8,640]{2,1,0:T(8,128)(2,1)S(1)}, u32[]{:S(2)}, u32[]{:S(2)}) collective-permute-start(bf16[16,8,640]{2,1,0:T(8,128)(2,1)} %bitcast.44), channel_id=1, source_target_pairs={{0,48},{16,0},{32,16},{48,32},{1,49},{17,1},{33,17},{49,33},{2,50}... | collective-permute-start | bytes 491528 | tf_op jit(solution)/shard_map/ppermute | solution.py:339
  18.5 1.9 %collective-permute-start.2 = (bf16[2,2,16,1024]{3,2,1,0:T(8,128)(2,1)S(1)}, bf16[2,2,16,1024]{3,2,1,0:T(8,128)(2,1)S(1)}, u32[]{:S(2)}, u32[]{:S(2)}) collective-permute-start(bf16[2,2,16,1024]{3,2,1,0:T(8,128)(2,1)S(1)} %pad_maximum_fusion.4), channel_id=1, source_target_pairs={{0,7},{1,0},{2,1},{3,2},{4,3},{5,4},{6,5},{7,6},{8,15},{9,8},{10,9... | collective-permute-start | bytes 393224 | tf_op jit(solution)/shard_map/ppermute | solution.py:339
  20.4 2.2 %collective-permute-start.1 = (bf16[2,2,16,1024]{3,2,1,0:T(8,128)(2,1)S(1)}, bf16[2,2,16,1024]{3,2,1,0:T(8,128)(2,1)S(1)}, u32[]{:S(2)}, u32[]{:S(2)}) collective-permute-start(bf16[2,2,16,1024]{3,2,1,0:T(8,128)(2,1)S(1)} %pad_maximum_fusion.4), channel_id=1, source_target_pairs={{0,1},{1,2},{2,3},{3,4},{4,5},{5,6},{6,7},{7,0},{8,9},{9,10},{10,1... | collective-permute-start | bytes 393224 | tf_op jit(solution)/shard_map/ppermute | solution.py:339
  22.6 0.0 collective-permute-done.2
  22.6 3.3 %collective-permute-done.1 = bf16[2,2,16,1024]{3,2,1,0:T(8,128)(2,1)S(1)} collective-permute-done((bf16[2,2,16,1024]{3,2,1,0:T(8,128)(2,1)S(1)}, bf16[2,2,16,1024]{3,2,1,0:T(8,128)(2,1)S(1)}, u32[]{:S(2)}, u32[]{:S(2)}) %collective-permute-start.1) | collective-permute-done | bytes 131104 | tf_op jit(solution)/shard_map/ppermute | solution.py:339
  26.0 0.0 collective-permute-done.5
  26.0 0.0 collective-permute-done.6
  26.0 0.9 pad_maximum_fusion.1
  26.9 7.1 %all-to-all-start = ((bf16[16,4,8,640]{3,2,1,0:T(8,128)(2,1)}), bf16[16,4,8,640]{3,2,1,0:T(8,128)(2,1)S(1)}, u32[]{:S(2)}, u32[]{:S(2)}) async-start(bf16[16,4,8,640]{3,2,1,0:T(8,128)(2,1)} %pad_maximum_fusion.1), calls=%async_computation | async-start | bytes 1310720 | tf_op jit(solution)/shard_map/all_to_all | solution.py:370
  34.1 3.0 %collective-permute-start.10 = (bf16[4,2,16,1152]{3,2,1,0:T(8,128)(2,1)S(1)}, bf16[4,2,16,1152]{3,2,1,0:T(8,128)(2,1)S(1)}, u32[]{:S(2)}, u32[]{:S(2)}) collective-permute-start(bf16[4,2,16,1152]{3,2,1,0:T(8,128)(2,1)S(1)} %pad_maximum_fusion.3.refs_4_.second_0), channel_id=1, source_target_pairs={{0,8},{8,0},{1,9},{9,1},{2,10},{10,2},{3,11},{11,3},{4,12},{12,4},... | collective-permute-start | bytes 884744 | tf_op jit(solution)/shard_map/ppermute | solution.py:339
  37.1 1.4 %collective-permute-start.9 = (bf16[4,2,16,896]{3,2,1,0:T(8,128)(2,1)S(1)}, bf16[4,2,16,896]{3,2,1,0:T(8,128)(2,1)S(1)}, u32[]{:S(2)}, u32[]{:S(2)}) collective-permute-start(bf16[4,2,16,896]{3,2,1,0:T(8,128)(2,1)S(1)} %slice.16.refs_0_), channel_id=1, source_target_pairs={{0,48},{16,0},{32,16},{48,32},{1,49},{17,1},{33,17},{49,33},{2,50}... | collective-permute-start | bytes 688136 | tf_op jit(solution)/shard_map/ppermute | solution.py:339
  38.5 0.6 collective-permute-start.8
  39.1 0.3 collective-permute-start.7
  39.4 2.7 %collective-permute-done.9.refs_3_ = bf16[4,2,16,896]{3,2,1,0:T(8,128)(2,1)S(1)} collective-permute-done((bf16[4,2,16,896]{3,2,1,0:T(8,128)(2,1)S(1)}, bf16[4,2,16,896]{3,2,1,0:T(8,128)(2,1)S(1)}, u32[]{:S(2)}, u32[]{:S(2)}) %collective-permute-start.9) | collective-permute-done | bytes 229408 | tf_op jit(solution)/shard_map/ppermute | solution.py:339
  42.1 3.2 %collective-permute-done.8.refs_2_ = bf16[4,2,16,896]{3,2,1,0:T(8,128)(2,1)S(1)} collective-permute-done((bf16[4,2,16,896]{3,2,1,0:T(8,128)(2,1)S(1)}, bf16[4,2,16,896]{3,2,1,0:T(8,128)(2,1)S(1)}, u32[]{:S(2)}, u32[]{:S(2)}) %collective-permute-start.8) | collective-permute-done | bytes 229408 | tf_op jit(solution)/shard_map/ppermute | solution.py:339
  45.2 2.4 %collective-permute-done.7.refs_1_ = bf16[4,2,16,896]{3,2,1,0:T(8,128)(2,1)S(1)} collective-permute-done((bf16[4,2,16,896]{3,2,1,0:T(8,128)(2,1)S(1)}, bf16[4,2,16,896]{3,2,1,0:T(8,128)(2,1)S(1)}, u32[]{:S(2)}, u32[]{:S(2)}) %collective-permute-start.7) | collective-permute-done | bytes 229408 | tf_op jit(solution)/shard_map/ppermute | solution.py:339
  47.6 0.1 pad_maximum_fusion
  47.8 0.5 copy-done.2
  48.3 0.5 collective-permute-start.11
  48.9 0.0 copy-start.4
  48.9 1.4 %collective-permute-start.14 = (bf16[8,2,16,1152]{3,2,1,0:T(8,128)(2,1)S(1)}, bf16[8,2,16,1152]{3,2,1,0:T(8,128)(2,1)S(1)}, u32[]{:S(2)}, u32[]{:S(2)}) collective-permute-start(bf16[8,2,16,1152]{3,2,1,0:T(8,128)(2,1)S(1)} %constant_dynamic-update-slice_fusion.2), channel_id=1, source_target_pairs={{0,48},{16,0},{32,16},{48,32},{1,49},{17,1},{33,17},{49,33},{2,50}... | collective-permute-start | bytes 1769480 | tf_op jit(solution)/shard_map/ppermute | solution.py:339
  50.4 0.1 collective-permute-start.13
  50.4 0.8 collective-permute-start.12
  51.2 1.1 unpack.1
  52.3 0.5 collective-permute-start.15
  52.8 0.6 copy-done.7
  53.5 0.0 copy-done.8
  53.5 1.6 %start.1 = (bf16[1024,512]{1,0:T(8,128)(2,1)S(1)}, f32[2,384,256]{2,1,0:T(8,128)S(1)}, f32[256,256]{1,0:T(8,128)S(1)}) custom-call(f32[1,2]{1,0:T(1,128)S(1)} %copy-done.8, s32[1,4]{1,0:T(1,128)S(1)} %copy-done.7, bf16[2,1024,256]{2,1,0:T(8,128)(2,1)S(1)} %bitcast.26, bf16[2,256,256]{2,1,0:T(8,128)(2,1)S(1)} %bitcast.32, ...), custom_call_target="tpu_custom_call" | custom-call | tf_op jit(solution)/shard_map/start/pallas_call | solution.py:164
  55.1 16.0 %collective-permute-done.15.own_far = bf16[640,256]{1,0:T(8,128)(2,1)S(1)} collective-permute-done((bf16[640,256]{1,0:T(8,128)(2,1)S(1)}, bf16[640,256]{1,0:T(8,128)(2,1)S(1)}, u32[]{:S(2)}, u32[]{:S(2)}) %collective-permute-start.15) | collective-permute-done | bytes 327712 | tf_op jit(solution)/shard_map/ppermute | solution.py:339
  71.1 6.5 %collective-permute-done.12.second_1 = bf16[8,2,16,1152]{3,2,1,0:T(8,128)(2,1)S(1)} collective-permute-done((bf16[8,2,16,1152]{3,2,1,0:T(8,128)(2,1)S(1)}, bf16[8,2,16,1152]{3,2,1,0:T(8,128)(2,1)S(1)}, u32[]{:S(2)}, u32[]{:S(2)}) %collective-permute-start.12) | collective-permute-done | bytes 589856 | tf_op jit(solution)/shard_map/ppermute | solution.py:339
  77.6 0.1 pad_maximum_fusion.2
  77.7 2.5 %collective-permute-start.16 = (bf16[2,640,256]{2,1,0:T(8,128)(2,1)S(1)}, bf16[2,640,256]{2,1,0:T(8,128)(2,1)S(1)}, u32[]{:S(2)}, u32[]{:S(2)}) collective-permute-start(bf16[2,640,256]{2,1,0:T(8,128)(2,1)S(1)} %pad_maximum_fusion.2), channel_id=1, source_target_pairs={{0,64},{64,0},{1,65},{65,1},{2,66},{66,2},{3,67},{67,3},{4,68},{68... | collective-permute-start | bytes 1966088 | tf_op jit(solution)/shard_map/ppermute | solution.py:339
  80.2 3.4 %upper.1 = (bf16[2,1024,256]{2,1,0:T(8,128)(2,1)}, bf16[2,1024,256]{2,1,0:T(8,128)(2,1)S(1)}) custom-call(s32[2]{0:T(128)S(1)} %copy-done.6, s32[1,4]{1,0:T(1,128)S(1)} %copy-done.7, bf16[1024,512]{1,0:T(8,128)(2,1)S(1)} %get-tuple-element.67.rhs, f32[2,384,256]{2,1,0:T(8,128)S(1)} %get-tuple-element.71.early, ...), custom_call_target="tpu_custom_call" | custom-call | tf_op jit(solution)/shard_map/upper/pallas_call | solution.py:210
  83.7 2.0 %charge.1 = f32[16,8,128]{2,1,0:T(8,128)S(1)} custom-call(s32[2]{0:T(128)S(1)} %copy-done.6, f32[1,2]{1,0:T(1,128)S(1)} %copy-done.8, s32[1,4]{1,0:T(1,128)S(1)} %copy-done.7, bf16[2,1024,256]{2,1,0:T(8,128)(2,1)S(1)} %bitcast.27, f32[256,256]{1,0:T(8,128)S(1)} %get-tuple-element.78.sums, bf16[640,256]{1,0:T(8,128)(2,1)S(1)} %get-tuple-element.69.own, ...), custom_call_target="tpu_custom_call" | custom-call | tf_op jit(solution)/shard_map/charge/pallas_call | solution.py:253
  85.7 8.5 %all_to_all.15.arrived = f32[16,8,128]{2,1,0:T(8,128)S(1)} all-to-all(f32[16,8,128]{2,1,0:T(8,128)S(1)} %charge.1), channel_id=1, replica_groups=mesh['ylo'=2,'core'=2,'x'=4,'yhi'=2,'z'=8] {'ylo','core','x'}, dimensions={0} | all-to-all | bytes 131072 | tf_op jit(solution)/shard_map/all_to_all | solution.py:387
  94.2 0.7 turn.1
  94.9 9.9 %all-to-all-start.2 = ((f32[16,8,128]{2,1,0:T(8,128)}), f32[16,8,128]{2,1,0:T(8,128)S(1)}, u32[]{:S(2)}, u32[]{:S(2)}) async-start(f32[16,8,128]{2,1,0:T(8,128)} %turn.1), calls=%async_computation.2 | async-start | bytes 131072 | tf_op jit(solution)/shard_map/all_to_all | solution.py:388
  104.8 2.0 %diag.1 = bf16[2,256,256]{2,1,0:T(8,128)(2,1)} custom-call(s32[1,4]{1,0:T(1,128)S(1)} %copy-done.7, bf16[2,1024,256]{2,1,0:T(8,128)(2,1)S(1)} %bitcast.28, bf16[2,1024,256]{2,1,0:T(8,128)(2,1)S(1)} %get-tuple-element.77.upper, bf16[2,256,256]{2,1,0:T(8,128)(2,1)S(1)} %bitcast.33), custom_call_target="tpu_custom_call" | custom-call | tf_op jit(solution)/shard_map/diag/pallas_call | solution.py:280
  106.8 6.8 %all-to-all-done.2.arrived = f32[16,8,128]{2,1,0:T(8,128)S(1)} async-done(((f32[16,8,128]{2,1,0:T(8,128)}), f32[16,8,128]{2,1,0:T(8,128)S(1)}, u32[]{:S(2)}, u32[]{:S(2)}) %all-to-all-start.2) | async-done | bytes 65568 | tf_op jit(solution)/shard_map/all_to_all | solution.py:388
  113.6 0.9 place.1
  (34 shorter events, 0.2 us)
Async XLA Ops:
  0.6 11.7 %collective-permute-start = (bf16[2,16,1024]{2,1,0:T(8,128)(2,1)}, bf16[2,16,1024]{2,1,0:T(8,128)(2,1)S(1)}, u32[]{:S(2)}, u32[]{:S(2)}) collective-permute-start(bf16[2,16,1024]{2,1,0:T(8,128)(2,1)} %bitcast.41), channel_id=1, source_target_pairs={{0,4},{1,5},{2,6},{3,7},{4,0},{5,1},{6,2},{7,3},{8,12},{9,13},{10,... | collective-permute-start | bytes 196616 | tf_op jit(solution)/shard_map/ppermute | solution.py:339
  9.1 3.3 %copy-start.10 = (bf16[1,2,16,1024]{3,2,1,0:T(8,128)(2,1)S(1)}, bf16[1,2,16,1024]{3,2,1,0:T(8,128)(2,1)}, u32[]{:S(2)}) copy-start(bf16[1,2,16,1024]{3,2,1,0:T(8,128)(2,1)} %param.8) | copy-start | bytes 196612
  12.4 13.6 %copy-start.9 = (bf16[128,640]{1,0:T(8,128)(2,1)S(1)}, bf16[128,640]{1,0:T(8,128)(2,1)}, u32[]{:S(2)}) copy-start(bf16[128,640]{1,0:T(8,128)(2,1)} %get-tuple-element.49) | copy-start | bytes 491524
  12.4 8.0 %collective-permute-start.3 = (bf16[2,2,16,1024]{3,2,1,0:T(8,128)(2,1)S(1)}, bf16[2,2,16,1024]{3,2,1,0:T(8,128)(2,1)S(1)}, u32[]{:S(2)}, u32[]{:S(2)}) collective-permute-start(bf16[2,2,16,1024]{3,2,1,0:T(8,128)(2,1)S(1)} %pad_maximum_fusion.4), channel_id=1, source_target_pairs={{0,2},{1,3},{2,4},{3,5},{4,6},{5,7},{6,0},{7,1},{8,10},{9,11},{10,... | collective-permute-start | bytes 393224 | tf_op jit(solution)/shard_map/ppermute | solution.py:339
  13.7 12.3 %collective-permute-start.4 = (bf16[16,8,640]{2,1,0:T(8,128)(2,1)}, bf16[16,8,640]{2,1,0:T(8,128)(2,1)S(1)}, u32[]{:S(2)}, u32[]{:S(2)}) collective-permute-start(bf16[16,8,640]{2,1,0:T(8,128)(2,1)} %bitcast.46), channel_id=1, source_target_pairs={{0,16},{16,32},{32,48},{48,0},{1,17},{17,33},{33,49},{49,1},{2,18}... | collective-permute-start | bytes 491528 | tf_op jit(solution)/shard_map/ppermute | solution.py:339
  14.9 11.1 %collective-permute-start.5 = (bf16[16,8,640]{2,1,0:T(8,128)(2,1)}, bf16[16,8,640]{2,1,0:T(8,128)(2,1)S(1)}, u32[]{:S(2)}, u32[]{:S(2)}) collective-permute-start(bf16[16,8,640]{2,1,0:T(8,128)(2,1)} %bitcast.45), channel_id=1, source_target_pairs={{0,32},{16,48},{32,0},{48,16},{1,33},{17,49},{33,1},{49,17},{2,34}... | collective-permute-start | bytes 491528 | tf_op jit(solution)/shard_map/ppermute | solution.py:339
  17.3 8.6 %collective-permute-start.6 = (bf16[16,8,640]{2,1,0:T(8,128)(2,1)}, bf16[16,8,640]{2,1,0:T(8,128)(2,1)S(1)}, u32[]{:S(2)}, u32[]{:S(2)}) collective-permute-start(bf16[16,8,640]{2,1,0:T(8,128)(2,1)} %bitcast.44), channel_id=1, source_target_pairs={{0,48},{16,0},{32,16},{48,32},{1,49},{17,1},{33,17},{49,33},{2,50}... | collective-permute-start | bytes 491528 | tf_op jit(solution)/shard_map/ppermute | solution.py:339
  18.5 4.1 %collective-permute-start.2 = (bf16[2,2,16,1024]{3,2,1,0:T(8,128)(2,1)S(1)}, bf16[2,2,16,1024]{3,2,1,0:T(8,128)(2,1)S(1)}, u32[]{:S(2)}, u32[]{:S(2)}) collective-permute-start(bf16[2,2,16,1024]{3,2,1,0:T(8,128)(2,1)S(1)} %pad_maximum_fusion.4), channel_id=1, source_target_pairs={{0,7},{1,0},{2,1},{3,2},{4,3},{5,4},{6,5},{7,6},{8,15},{9,8},{10,9... | collective-permute-start | bytes 393224 | tf_op jit(solution)/shard_map/ppermute | solution.py:339
  20.4 5.5 %collective-permute-start.1 = (bf16[2,2,16,1024]{3,2,1,0:T(8,128)(2,1)S(1)}, bf16[2,2,16,1024]{3,2,1,0:T(8,128)(2,1)S(1)}, u32[]{:S(2)}, u32[]{:S(2)}) collective-permute-start(bf16[2,2,16,1024]{3,2,1,0:T(8,128)(2,1)S(1)} %pad_maximum_fusion.4), channel_id=1, source_target_pairs={{0,1},{1,2},{2,3},{3,4},{4,5},{5,6},{6,7},{7,0},{8,9},{9,10},{10,1... | collective-permute-start | bytes 393224 | tf_op jit(solution)/shard_map/ppermute | solution.py:339
  26.9 20.7 %all-to-all-start = ((bf16[16,4,8,640]{3,2,1,0:T(8,128)(2,1)}), bf16[16,4,8,640]{3,2,1,0:T(8,128)(2,1)S(1)}, u32[]{:S(2)}, u32[]{:S(2)}) async-start(bf16[16,4,8,640]{3,2,1,0:T(8,128)(2,1)} %pad_maximum_fusion.1), calls=%async_computation | async-start | bytes 1310720 | tf_op jit(solution)/shard_map/all_to_all | solution.py:370
  34.1 13.5 %collective-permute-start.10 = (bf16[4,2,16,1152]{3,2,1,0:T(8,128)(2,1)S(1)}, bf16[4,2,16,1152]{3,2,1,0:T(8,128)(2,1)S(1)}, u32[]{:S(2)}, u32[]{:S(2)}) collective-permute-start(bf16[4,2,16,1152]{3,2,1,0:T(8,128)(2,1)S(1)} %pad_maximum_fusion.3.refs_4_.second_0), channel_id=1, source_target_pairs={{0,8},{8,0},{1,9},{9,1},{2,10},{10,2},{3,11},{11,3},{4,12},{12,4},... | collective-permute-start | bytes 884744 | tf_op jit(solution)/shard_map/ppermute | solution.py:339
  37.1 4.9 %collective-permute-start.9 = (bf16[4,2,16,896]{3,2,1,0:T(8,128)(2,1)S(1)}, bf16[4,2,16,896]{3,2,1,0:T(8,128)(2,1)S(1)}, u32[]{:S(2)}, u32[]{:S(2)}) collective-permute-start(bf16[4,2,16,896]{3,2,1,0:T(8,128)(2,1)S(1)} %slice.16.refs_0_), channel_id=1, source_target_pairs={{0,48},{16,0},{32,16},{48,32},{1,49},{17,1},{33,17},{49,33},{2,50}... | collective-permute-start | bytes 688136 | tf_op jit(solution)/shard_map/ppermute | solution.py:339
  38.5 6.7 %collective-permute-start.8 = (bf16[4,2,16,896]{3,2,1,0:T(8,128)(2,1)S(1)}, bf16[4,2,16,896]{3,2,1,0:T(8,128)(2,1)S(1)}, u32[]{:S(2)}, u32[]{:S(2)}) collective-permute-start(bf16[4,2,16,896]{3,2,1,0:T(8,128)(2,1)S(1)} %slice.16.refs_0_), channel_id=1, source_target_pairs={{0,32},{16,48},{32,0},{48,16},{1,33},{17,49},{33,1},{49,17},{2,34}... | collective-permute-start | bytes 688136 | tf_op jit(solution)/shard_map/ppermute | solution.py:339
  39.1 8.5 %collective-permute-start.7 = (bf16[4,2,16,896]{3,2,1,0:T(8,128)(2,1)S(1)}, bf16[4,2,16,896]{3,2,1,0:T(8,128)(2,1)S(1)}, u32[]{:S(2)}, u32[]{:S(2)}) collective-permute-start(bf16[4,2,16,896]{3,2,1,0:T(8,128)(2,1)S(1)} %slice.16.refs_0_), channel_id=1, source_target_pairs={{0,16},{16,32},{32,48},{48,0},{1,17},{17,33},{33,49},{49,1},{2,18}... | collective-permute-start | bytes 688136 | tf_op jit(solution)/shard_map/ppermute | solution.py:339
  47.6 0.7 copy-start.2
  48.3 4.5 %copy-start = (bf16[1,2,1024,256]{3,2,1,0:T(8,128)(2,1)S(1)}, bf16[1,2,1024,256]{3,2,1,0:T(8,128)(2,1)}, u32[]{:S(2)}) copy-start(bf16[1,2,1024,256]{3,2,1,0:T(8,128)(2,1)} %param.9) | copy-start | bytes 3145732
  48.3 29.3 %collective-permute-start.11 = (bf16[16,2,16,896]{3,2,1,0:T(8,128)(2,1)S(1)}, bf16[16,2,16,896]{3,2,1,0:T(8,128)(2,1)S(1)}, u32[]{:S(2)}, u32[]{:S(2)}) collective-permute-start(bf16[16,2,16,896]{3,2,1,0:T(8,128)(2,1)S(1)} %pad_maximum_fusion), channel_id=1, source_target_pairs={{0,8},{8,0},{1,9},{9,1},{2,10},{10,2},{3,11},{11,3},{4,12},{12,4},... | collective-permute-start | bytes 2752520 | tf_op jit(solution)/shard_map/ppermute | solution.py:339
  48.9 2.3 %copy-start.4 = (s32[16384]{0:T(1024)S(1)}, s32[16384]{0:T(1024)}, u32[]{:S(2)}) copy-start(s32[16384]{0:T(1024)} %param.15) | copy-start | bytes 196612
  48.9 2.3 %copy-start.6 = (s32[2]{0:T(128)S(1)}, s32[2]{0:T(128)}, u32[]{:S(2)}) copy-start(s32[2]{0:T(128)} %pad_add_fusion.index) | copy-start | bytes 28
  48.9 22.2 %collective-permute-start.14 = (bf16[8,2,16,1152]{3,2,1,0:T(8,128)(2,1)S(1)}, bf16[8,2,16,1152]{3,2,1,0:T(8,128)(2,1)S(1)}, u32[]{:S(2)}, u32[]{:S(2)}) collective-permute-start(bf16[8,2,16,1152]{3,2,1,0:T(8,128)(2,1)S(1)} %constant_dynamic-update-slice_fusion.2), channel_id=1, source_target_pairs={{0,48},{16,0},{32,16},{48,32},{1,49},{17,1},{33,17},{49,33},{2,50}... | collective-permute-start | bytes 1769480 | tf_op jit(solution)/shard_map/ppermute | solution.py:339
  50.4 20.8 %collective-permute-start.13 = (bf16[8,2,16,1152]{3,2,1,0:T(8,128)(2,1)S(1)}, bf16[8,2,16,1152]{3,2,1,0:T(8,128)(2,1)S(1)}, u32[]{:S(2)}, u32[]{:S(2)}) collective-permute-start(bf16[8,2,16,1152]{3,2,1,0:T(8,128)(2,1)S(1)} %constant_dynamic-update-slice_fusion.2), channel_id=1, source_target_pairs={{0,32},{16,48},{32,0},{48,16},{1,33},{17,49},{33,1},{49,17},{2,34}... | collective-permute-start | bytes 1769480 | tf_op jit(solution)/shard_map/ppermute | solution.py:339
  50.4 27.2 %collective-permute-start.12 = (bf16[8,2,16,1152]{3,2,1,0:T(8,128)(2,1)S(1)}, bf16[8,2,16,1152]{3,2,1,0:T(8,128)(2,1)S(1)}, u32[]{:S(2)}, u32[]{:S(2)}) collective-permute-start(bf16[8,2,16,1152]{3,2,1,0:T(8,128)(2,1)S(1)} %constant_dynamic-update-slice_fusion.2), channel_id=1, source_target_pairs={{0,16},{16,32},{32,48},{48,0},{1,17},{17,33},{33,49},{49,1},{2,18}... | collective-permute-start | bytes 1769480 | tf_op jit(solution)/shard_map/ppermute | solution.py:339
  51.2 1.6 %copy-start.1 = (bf16[1,2,256,256]{3,2,1,0:T(8,128)(2,1)S(1)}, bf16[1,2,256,256]{3,2,1,0:T(8,128)(2,1)}, u32[]{:S(2)}) copy-start(bf16[1,2,256,256]{3,2,1,0:T(8,128)(2,1)} %param.11) | copy-start | bytes 786436
  51.2 1.6 %copy-start.3 = (bf16[4,2,16,896]{3,2,1,0:T(8,128)(2,1)S(1)}, bf16[4,2,16,896]{3,2,1,0:T(8,128)(2,1)}, u32[]{:S(2)}) copy-start(bf16[4,2,16,896]{3,2,1,0:T(8,128)(2,1)} %copy-done.2) | copy-start | bytes 688132
  52.3 18.8 %collective-permute-start.15 = (bf16[640,256]{1,0:T(8,128)(2,1)S(1)}, bf16[640,256]{1,0:T(8,128)(2,1)S(1)}, u32[]{:S(2)}, u32[]{:S(2)}) collective-permute-start(bf16[640,256]{1,0:T(8,128)(2,1)S(1)} %get-tuple-element.69.own), channel_id=1, source_target_pairs={{0,128},{128,0},{1,129},{129,1},{2,130},{130,2},{3,131},{131,3},{4... | collective-permute-start | bytes 983048 | tf_op jit(solution)/shard_map/ppermute | solution.py:339
  52.8 0.7 copy-start.7
  52.8 0.7 copy-start.8
  77.7 5.9 %collective-permute-start.16 = (bf16[2,640,256]{2,1,0:T(8,128)(2,1)S(1)}, bf16[2,640,256]{2,1,0:T(8,128)(2,1)S(1)}, u32[]{:S(2)}, u32[]{:S(2)}) collective-permute-start(bf16[2,640,256]{2,1,0:T(8,128)(2,1)S(1)} %pad_maximum_fusion.2), channel_id=1, source_target_pairs={{0,64},{64,0},{1,65},{65,1},{2,66},{66,2},{3,67},{67,3},{4,68},{68... | collective-permute-start | bytes 1966088 | tf_op jit(solution)/shard_map/ppermute | solution.py:339
  94.9 18.7 %all-to-all-start.2 = ((f32[16,8,128]{2,1,0:T(8,128)}), f32[16,8,128]{2,1,0:T(8,128)S(1)}, u32[]{:S(2)}, u32[]{:S(2)}) async-start(f32[16,8,128]{2,1,0:T(8,128)} %turn.1), calls=%async_computation.2 | async-start | bytes 131072 | tf_op jit(solution)/shard_map/all_to_all | solution.py:388
  104.8 8.9 %copy-start.5 = (bf16[512,256]{1,0:T(8,128)(2,1)S(1)}, bf16[512,256]{1,0:T(8,128)(2,1)}, u32[]{:S(2)}) copy-start(bf16[512,256]{1,0:T(8,128)(2,1)} %get-tuple-element.81.onehot) | copy-start | bytes 786436

commit v7 on v6

--- a/solution.py
+++ b/solution.py
@@ -217,7 +217,7 @@
     )(index, fill, rhs, early, *pieces)
 
 
-def charge_kernel(index, weights, fill, lower, sums, own, own_far, mate, mate_far, upper, onehot, slots, rows):
+def charge_kernel(index, weights, lower, sums, own, own_far, mate, mate_far, upper, onehot, slots, rows):
     pole, x = index[0], index[1] >> 4
     for bits, ref in ((0, own), (2, own_far), (1, mate), (3, mate_far)):
         start = pl.multiple_of((pole ^ bits) * QUARTER, QUARTER)
@@ -228,13 +228,12 @@
     totals = [jnp.sum(sums[...] * near.astype(F32), axis=0, keepdims=True) for near in nears]
     both = jnp.concatenate(nears, axis=1)
     for block in range(ANC // COLS):
-        keep = fill[0, block].astype(F32)
         span = slice(block * COLS, (block + 1) * COLS)
         up_real, up_imag = upper[0, span, :].astype(F32), upper[1, span, :].astype(F32)
         to_direct = imag * up_real + real * up_imag
         to_cross = imag * up_imag - real * up_real
-        direct = mm(lower[0, span, :], both) * keep
-        cross = mm(lower[1, span, :], both) * keep
+        direct = mm(lower[span, 0:COLS], both)
+        cross = mm(lower[span, COLS:], both)
         for which in range(2):
             part = slice(which * COLS, (which + 1) * COLS)
             far = rows[which, (block + 1) * COLS : (block + 2) * COLS, :].astype(F32)
@@ -249,26 +248,25 @@
             slots[n * NX + px] = result[:, px * width : (px + 1) * width]
 
 
-def charge_slots(index, weights, fill, lower, sums, quarters, upper, onehot):
+def charge_slots(index, weights, lower, sums, quarters, upper, onehot):
     return pl.pallas_call(
         charge_kernel,
-        in_specs=[SMEM_SPEC] * 3 + [VMEM_SPEC] * (4 + len(quarters)),
+        in_specs=[SMEM_SPEC] * 2 + [VMEM_SPEC] * (4 + len(quarters)),
         out_specs=VMEM_SPEC,
         out_shape=jax.ShapeDtypeStruct((POLES * NX, 8, PLANE * CAP), F32),
         scratch_shapes=[pltpu.VMEM((2, ROWS, COLS), BF16)],
         compiler_params=params(24),
         name="charge",
-    )(index, weights, fill, lower, sums, *quarters, upper, onehot)
-
-
-def diag_kernel(fill, lower, upper, diag_inverse, out):
+    )(index, weights, lower, sums, *quarters, upper, onehot)
+
+
+def diag_kernel(lower, upper, diag_inverse, out):
     real = diag_inverse[0].astype(F32)
     imag = diag_inverse[1].astype(F32)
     turn = ((0,), (0,))
     for block in range(ANC // COLS):
-        keep = fill[0, block].astype(F32).astype(BF16)
         span = slice(block * COLS, (block + 1) * COLS)
-        low_real, low_imag = lower[0, span, :] * keep, lower[1, span, :] * keep
+        low_real, low_imag = lower[span, 0:COLS], lower[span, COLS:]
         up_real, up_imag = upper[0, span, :], upper[1, span, :]
         real = real - mm(low_real, up_real, turn) + mm(low_imag, up_imag, turn)
         imag = imag - mm(low_real, up_imag, turn) - mm(low_imag, up_real, turn)
@@ -276,15 +274,15 @@
     out[1] = imag.astype(BF16)
 
 
-def diag_block(fill, lower, upper, diag_inverse):
+def diag_block(lower, upper, diag_inverse):
     return pl.pallas_call(
         diag_kernel,
-        in_specs=[SMEM_SPEC] + [VMEM_SPEC] * 3,
+        in_specs=[VMEM_SPEC] * 3,
         out_specs=VMEM_SPEC,
         out_shape=jax.ShapeDtypeStruct((2, COLS, COLS), BF16),
         compiler_params=params(),
         name="diag",
-    )(fill, lower, upper, diag_inverse)
+    )(lower, upper, diag_inverse)
 
 
 def turn_kernel(arrived, out):
@@ -382,8 +380,8 @@
     mate, mate_far = mates[0], mates[1]
     upper, upper_again = upper_rows(index, fill_pattern, rhs, early, [first_y] + second_y + second_x)
     quarters = [mine, mine_far, mate, mate_far]
-    slots = charge_slots(index, pole_weights, fill_pattern, lower, sums, quarters, upper_again, column_onehot)
-    diag = diag_block(fill_pattern, lower, upper_again, inverse)
+    slots = charge_slots(index, pole_weights, rhs, sums, quarters, upper_again, column_onehot)
+    diag = diag_block(rhs, upper_again, inverse)
     sums = lax.all_to_all(slots, ("ylo", "core", "x"), split_axis=0, concat_axis=0, tiled=True)
     sums = lax.all_to_all(turn(sums), ("yhi", "z"), split_axis=0, concat_axis=0, tiled=True)
     charges, energy = place(sums, slot_onehot)

time: 115 us -> 114 us (level)
  transfers between devices with their start and end apart: 19 -> 19, of which waited for: 7 -> 7; matrix products, arithmetic and copies ran while one was open for 1% -> 1% of each run, Pallas kernels for 10% -> 9%
where the time goes in v7:
time: 114 us
  starting transfers between devices  46.1 us (40%)
  waiting for transfers between devices  41.6 us (36%)
  Pallas kernels  14.2 us (12%)
  blocking collectives  8.48 us (7%)
  other arithmetic  1.83 us (2%)
    ppermute x17, waiting for transfers between devices, shift(): lax.ppermute(value, axis, [(n, (n + by) % size) for n in range(size)])  34.2 us
    ppermute x17, starting transfers between devices, shift(): lax.ppermute(value, axis, [(n, (n + by) % size) for n in range(size)])  29.5 us
    all_to_all x1, starting transfers between devices, body(): lax.all_to_all(turn(sums), ('yhi', 'z'), split_axis=0, concat_axis=0, til...  9.55 us
    all_to_all x1, blocking collectives, body(): lax.all_to_all(slots, ('ylo', 'core', 'x'), split_axis=0, concat_axis=0,...  8.48 us
    all_to_all x1, waiting for transfers between devices, body(): lax.all_to_all(turn(sums), ('yhi', 'z'), split_axis=0, concat_axis=0, til...  7.4 us
    all_to_all x1, starting transfers between devices, body(): lax.all_to_all(jnp.stack(sent, axis=1), ('yhi', 'z'), split_axis=0, conca...  7.09 us
    pallas_call x1, Pallas kernels, upper_rows(): pl.pallas_call(upper_kernel, in_specs=[SMEM_SPEC] * 2 + [VMEM_SPEC] * (2...  3.34 us
    pallas_call x1, Pallas kernels, pack(): pl.pallas_call(pack_kernel, in_specs=[SMEM_SPEC, VMEM_SPEC, HBM_SPEC, HBM...  3.29 us
  transfers between devices with their start and end apart: 19, of which 7 were waited for; matrix products, arithmetic and copies ran while one was open for 1% of the time, Pallas kernels for 9%

profile of v7, /device:TPU:1, one launch (start us, length us, event | category | flops | bytes accessed | tf_op | source)
XLA Modules:
  0.0 114.0 jit_solution(5546480377628993781)
XLA Ops:
  0.6 7.8 %collective-permute-start = (bf16[2,16,1024]{2,1,0:T(8,128)(2,1)}, bf16[2,16,1024]{2,1,0:T(8,128)(2,1)S(1)}, u32[]{:S(2)}, u32[]{:S(2)}) collective-permute-start(bf16[2,16,1024]{2,1,0:T(8,128)(2,1)} %bitcast.39), channel_id=1, source_target_pairs={{0,4},{1,5},{2,6},{3,7},{4,0},{5,1},{6,2},{7,3},{8,12},{9,13},{10,... | collective-permute-start | bytes 196616 | tf_op jit(solution)/shard_map/ppermute | solution.py:337
  8.5 0.6 pad_add_fusion.index
  9.1 3.3 %pack.1 = (bf16[128,640]{1,0:T(8,128)(2,1)}, bf16[128,640]{1,0:T(8,128)(2,1)}, bf16[128,640]{1,0:T(8,128)(2,1)}, bf16[128,640]{1,0:T(8,128)(2,1)}, bf16[512,256]{1,0:T(8,128)(2,1)}) custom-call(s32[2]{0:T(128)} %pad_add_fusion.index, s32[128,128]{1,0:T(8,128)} %bitcast.32, bf16[1280,256]{1,0:T(8,128)(2,1)} %margin.1, bf16[1280,256]{1,0:T(8,128)(2,1)} %hamiltonian.1), custom_call_target="tpu_custom_call" | custom-call | tf_op jit(solution)/shard_map/pack/pallas_call | solution.py:91
  12.4 0.0 copy-start.7
  12.5 1.3 %collective-permute-start.3 = (bf16[2,2,16,1024]{3,2,1,0:T(8,128)(2,1)S(1)}, bf16[2,2,16,1024]{3,2,1,0:T(8,128)(2,1)S(1)}, u32[]{:S(2)}, u32[]{:S(2)}) collective-permute-start(bf16[2,2,16,1024]{3,2,1,0:T(8,128)(2,1)S(1)} %pad_maximum_fusion.4), channel_id=1, source_target_pairs={{0,2},{1,3},{2,4},{3,5},{4,6},{5,7},{6,0},{7,1},{8,10},{9,11},{10,... | collective-permute-start | bytes 393224 | tf_op jit(solution)/shard_map/ppermute | solution.py:337
  13.7 1.2 %collective-permute-start.4 = (bf16[16,8,640]{2,1,0:T(8,128)(2,1)}, bf16[16,8,640]{2,1,0:T(8,128)(2,1)S(1)}, u32[]{:S(2)}, u32[]{:S(2)}) collective-permute-start(bf16[16,8,640]{2,1,0:T(8,128)(2,1)} %bitcast.44), channel_id=1, source_target_pairs={{0,16},{16,32},{32,48},{48,0},{1,17},{17,33},{33,49},{49,1},{2,18}... | collective-permute-start | bytes 491528 | tf_op jit(solution)/shard_map/ppermute | solution.py:337
  14.9 2.4 %collective-permute-start.5 = (bf16[16,8,640]{2,1,0:T(8,128)(2,1)}, bf16[16,8,640]{2,1,0:T(8,128)(2,1)S(1)}, u32[]{:S(2)}, u32[]{:S(2)}) collective-permute-start(bf16[16,8,640]{2,1,0:T(8,128)(2,1)} %bitcast.43), channel_id=1, source_target_pairs={{0,32},{16,48},{32,0},{48,16},{1,33},{17,49},{33,1},{49,17},{2,34}... | collective-permute-start | bytes 491528 | tf_op jit(solution)/shard_map/ppermute | solution.py:337
  17.4 1.2 %collective-permute-start.6 = (bf16[16,8,640]{2,1,0:T(8,128)(2,1)}, bf16[16,8,640]{2,1,0:T(8,128)(2,1)S(1)}, u32[]{:S(2)}, u32[]{:S(2)}) collective-permute-start(bf16[16,8,640]{2,1,0:T(8,128)(2,1)} %bitcast.42), channel_id=1, source_target_pairs={{0,48},{16,0},{32,16},{48,32},{1,49},{17,1},{33,17},{49,33},{2,50}... | collective-permute-start | bytes 491528 | tf_op jit(solution)/shard_map/ppermute | solution.py:337
  18.5 1.9 %collective-permute-start.2 = (bf16[2,2,16,1024]{3,2,1,0:T(8,128)(2,1)S(1)}, bf16[2,2,16,1024]{3,2,1,0:T(8,128)(2,1)S(1)}, u32[]{:S(2)}, u32[]{:S(2)}) collective-permute-start(bf16[2,2,16,1024]{3,2,1,0:T(8,128)(2,1)S(1)} %pad_maximum_fusion.4), channel_id=1, source_target_pairs={{0,7},{1,0},{2,1},{3,2},{4,3},{5,4},{6,5},{7,6},{8,15},{9,8},{10,9... | collective-permute-start | bytes 393224 | tf_op jit(solution)/shard_map/ppermute | solution.py:337
  20.5 2.2 %collective-permute-start.1 = (bf16[2,2,16,1024]{3,2,1,0:T(8,128)(2,1)S(1)}, bf16[2,2,16,1024]{3,2,1,0:T(8,128)(2,1)S(1)}, u32[]{:S(2)}, u32[]{:S(2)}) collective-permute-start(bf16[2,2,16,1024]{3,2,1,0:T(8,128)(2,1)S(1)} %pad_maximum_fusion.4), channel_id=1, source_target_pairs={{0,1},{1,2},{2,3},{3,4},{4,5},{5,6},{6,7},{7,0},{8,9},{9,10},{10,1... | collective-permute-start | bytes 393224 | tf_op jit(solution)/shard_map/ppermute | solution.py:337
  22.7 0.0 collective-permute-done.2
  22.7 3.3 %collective-permute-done.1 = bf16[2,2,16,1024]{3,2,1,0:T(8,128)(2,1)S(1)} collective-permute-done((bf16[2,2,16,1024]{3,2,1,0:T(8,128)(2,1)S(1)}, bf16[2,2,16,1024]{3,2,1,0:T(8,128)(2,1)S(1)}, u32[]{:S(2)}, u32[]{:S(2)}) %collective-permute-start.1) | collective-permute-done | bytes 131104 | tf_op jit(solution)/shard_map/ppermute | solution.py:337
  26.0 0.0 collective-permute-done.4
  26.0 0.0 collective-permute-done.5
  26.0 0.0 collective-permute-done.6
  26.0 0.9 pad_maximum_fusion.1
  26.9 7.1 %all-to-all-start = ((bf16[16,4,8,640]{3,2,1,0:T(8,128)(2,1)}), bf16[16,4,8,640]{3,2,1,0:T(8,128)(2,1)S(1)}, u32[]{:S(2)}, u32[]{:S(2)}) async-start(bf16[16,4,8,640]{3,2,1,0:T(8,128)(2,1)} %pad_maximum_fusion.1), calls=%async_computation | async-start | bytes 1310720 | tf_op jit(solution)/shard_map/all_to_all | solution.py:368
  34.1 3.0 %collective-permute-start.10 = (bf16[4,2,16,1152]{3,2,1,0:T(8,128)(2,1)S(1)}, bf16[4,2,16,1152]{3,2,1,0:T(8,128)(2,1)S(1)}, u32[]{:S(2)}, u32[]{:S(2)}) collective-permute-start(bf16[4,2,16,1152]{3,2,1,0:T(8,128)(2,1)S(1)} %pad_maximum_fusion.3.refs_4_.second_0), channel_id=1, source_target_pairs={{0,8},{8,0},{1,9},{9,1},{2,10},{10,2},{3,11},{11,3},{4,12},{12,4},... | collective-permute-start | bytes 884744 | tf_op jit(solution)/shard_map/ppermute | solution.py:337
  37.1 1.4 %collective-permute-start.9 = (bf16[4,2,16,896]{3,2,1,0:T(8,128)(2,1)S(1)}, bf16[4,2,16,896]{3,2,1,0:T(8,128)(2,1)S(1)}, u32[]{:S(2)}, u32[]{:S(2)}) collective-permute-start(bf16[4,2,16,896]{3,2,1,0:T(8,128)(2,1)S(1)} %slice.16.refs_0_), channel_id=1, source_target_pairs={{0,48},{16,0},{32,16},{48,32},{1,49},{17,1},{33,17},{49,33},{2,50}... | collective-permute-start | bytes 688136 | tf_op jit(solution)/shard_map/ppermute | solution.py:337
  38.5 0.6 collective-permute-start.8
  39.1 0.3 collective-permute-start.7
  39.4 2.7 %collective-permute-done.9.refs_3_ = bf16[4,2,16,896]{3,2,1,0:T(8,128)(2,1)S(1)} collective-permute-done((bf16[4,2,16,896]{3,2,1,0:T(8,128)(2,1)S(1)}, bf16[4,2,16,896]{3,2,1,0:T(8,128)(2,1)S(1)}, u32[]{:S(2)}, u32[]{:S(2)}) %collective-permute-start.9) | collective-permute-done | bytes 229408 | tf_op jit(solution)/shard_map/ppermute | solution.py:337
  42.1 3.2 %collective-permute-done.8.refs_2_ = bf16[4,2,16,896]{3,2,1,0:T(8,128)(2,1)S(1)} collective-permute-done((bf16[4,2,16,896]{3,2,1,0:T(8,128)(2,1)S(1)}, bf16[4,2,16,896]{3,2,1,0:T(8,128)(2,1)S(1)}, u32[]{:S(2)}, u32[]{:S(2)}) %collective-permute-start.8) | collective-permute-done | bytes 229408 | tf_op jit(solution)/shard_map/ppermute | solution.py:337
  45.2 2.4 %collective-permute-done.7.refs_1_ = bf16[4,2,16,896]{3,2,1,0:T(8,128)(2,1)S(1)} collective-permute-done((bf16[4,2,16,896]{3,2,1,0:T(8,128)(2,1)S(1)}, bf16[4,2,16,896]{3,2,1,0:T(8,128)(2,1)S(1)}, u32[]{:S(2)}, u32[]{:S(2)}) %collective-permute-start.7) | collective-permute-done | bytes 229408 | tf_op jit(solution)/shard_map/ppermute | solution.py:337
  47.7 0.1 pad_maximum_fusion
  47.8 0.0 copy-start
  47.8 1.0 collective-permute-start.11
  48.9 0.0 copy-start.2
  48.9 1.5 %collective-permute-start.14 = (bf16[8,2,16,1152]{3,2,1,0:T(8,128)(2,1)S(1)}, bf16[8,2,16,1152]{3,2,1,0:T(8,128)(2,1)S(1)}, u32[]{:S(2)}, u32[]{:S(2)}) collective-permute-start(bf16[8,2,16,1152]{3,2,1,0:T(8,128)(2,1)S(1)} %constant_dynamic-update-slice_fusion.2), channel_id=1, source_target_pairs={{0,48},{16,0},{32,16},{48,32},{1,49},{17,1},{33,17},{49,33},{2,50}... | collective-permute-start | bytes 1769480 | tf_op jit(solution)/shard_map/ppermute | solution.py:337
  50.4 0.0 collective-permute-start.13
  50.4 0.8 collective-permute-start.12
  51.2 1.1 unpack.1
  52.3 0.5 collective-permute-start.15
  52.8 0.6 copy-done.5
  53.5 0.0 copy-done.6
  53.5 1.6 %start.1 = (bf16[1024,512]{1,0:T(8,128)(2,1)S(1)}, f32[2,384,256]{2,1,0:T(8,128)S(1)}, f32[256,256]{1,0:T(8,128)S(1)}) custom-call(f32[1,2]{1,0:T(1,128)S(1)} %copy-done.6, s32[1,4]{1,0:T(1,128)S(1)} %copy-done.5, bf16[2,1024,256]{2,1,0:T(8,128)(2,1)S(1)} %bitcast.29, bf16[2,256,256]{2,1,0:T(8,128)(2,1)S(1)} %bitcast.30, ...), custom_call_target="tpu_custom_call" | custom-call | tf_op jit(solution)/shard_map/start/pallas_call | solution.py:164
  55.1 16.1 %collective-permute-done.15.own_far = bf16[640,256]{1,0:T(8,128)(2,1)S(1)} collective-permute-done((bf16[640,256]{1,0:T(8,128)(2,1)S(1)}, bf16[640,256]{1,0:T(8,128)(2,1)S(1)}, u32[]{:S(2)}, u32[]{:S(2)}) %collective-permute-start.15) | collective-permute-done | bytes 327712 | tf_op jit(solution)/shard_map/ppermute | solution.py:337
  71.2 6.5 %collective-permute-done.12.second_1 = bf16[8,2,16,1152]{3,2,1,0:T(8,128)(2,1)S(1)} collective-permute-done((bf16[8,2,16,1152]{3,2,1,0:T(8,128)(2,1)S(1)}, bf16[8,2,16,1152]{3,2,1,0:T(8,128)(2,1)S(1)}, u32[]{:S(2)}, u32[]{:S(2)}) %collective-permute-start.12) | collective-permute-done | bytes 589856 | tf_op jit(solution)/shard_map/ppermute | solution.py:337
  77.7 0.1 pad_maximum_fusion.2
  77.7 2.5 %collective-permute-start.16 = (bf16[2,640,256]{2,1,0:T(8,128)(2,1)S(1)}, bf16[2,640,256]{2,1,0:T(8,128)(2,1)S(1)}, u32[]{:S(2)}, u32[]{:S(2)}) collective-permute-start(bf16[2,640,256]{2,1,0:T(8,128)(2,1)S(1)} %pad_maximum_fusion.2), channel_id=1, source_target_pairs={{0,64},{64,0},{1,65},{65,1},{2,66},{66,2},{3,67},{67,3},{4,68},{68... | collective-permute-start | bytes 1966088 | tf_op jit(solution)/shard_map/ppermute | solution.py:337
  80.2 3.3 %upper.1 = (bf16[2,1024,256]{2,1,0:T(8,128)(2,1)}, bf16[2,1024,256]{2,1,0:T(8,128)(2,1)S(1)}) custom-call(s32[2]{0:T(128)S(1)} %copy-done.4, s32[1,4]{1,0:T(1,128)S(1)} %copy-done.5, bf16[1024,512]{1,0:T(8,128)(2,1)S(1)} %get-tuple-element.67.rhs.lower, f32[2,384,256]{2,1,0:T(8,128)S(1)} %get-tuple-element.71.early, ...), custom_call_target="tpu_custom_call" | custom-call | tf_op jit(solution)/shard_map/upper/pallas_call | solution.py:210
  83.6 1.9 %charge.1 = f32[16,8,128]{2,1,0:T(8,128)S(1)} custom-call(s32[2]{0:T(128)S(1)} %copy-done.4, f32[1,2]{1,0:T(1,128)S(1)} %copy-done.6, bf16[1024,512]{1,0:T(8,128)(2,1)S(1)} %get-tuple-element.67.rhs.lower, f32[256,256]{1,0:T(8,128)S(1)} %get-tuple-element.78.sums, bf16[640,256]{1,0:T(8,128)(2,1)S(1)} %get-tuple-element.69.own, ...), custom_call_target="tpu_custom_call" | custom-call | tf_op jit(solution)/shard_map/charge/pallas_call | solution.py:252
  85.5 8.5 %all_to_all.15.arrived = f32[16,8,128]{2,1,0:T(8,128)S(1)} all-to-all(f32[16,8,128]{2,1,0:T(8,128)S(1)} %charge.1), channel_id=1, replica_groups=mesh['ylo'=2,'core'=2,'x'=4,'yhi'=2,'z'=8] {'ylo','core','x'}, dimensions={0} | all-to-all | bytes 131072 | tf_op jit(solution)/shard_map/all_to_all | solution.py:385
  94.0 0.7 turn.1
  94.7 9.6 %all-to-all-start.2 = ((f32[16,8,128]{2,1,0:T(8,128)}), f32[16,8,128]{2,1,0:T(8,128)S(1)}, u32[]{:S(2)}, u32[]{:S(2)}) async-start(f32[16,8,128]{2,1,0:T(8,128)} %turn.1), calls=%async_computation.2 | async-start | bytes 131072 | tf_op jit(solution)/shard_map/all_to_all | solution.py:386
  104.3 1.5 %diag.1 = bf16[2,256,256]{2,1,0:T(8,128)(2,1)} custom-call(bf16[1024,512]{1,0:T(8,128)(2,1)S(1)} %get-tuple-element.67.rhs.lower, bf16[2,1024,256]{2,1,0:T(8,128)(2,1)S(1)} %get-tuple-element.77.upper, bf16[2,256,256]{2,1,0:T(8,128)(2,1)S(1)} %bitcast.31), custom_call_target="tpu_custom_call" | custom-call | tf_op jit(solution)/shard_map/diag/pallas_call | solution.py:278
  105.7 7.4 %all-to-all-done.2.arrived = f32[16,8,128]{2,1,0:T(8,128)S(1)} async-done(((f32[16,8,128]{2,1,0:T(8,128)}), f32[16,8,128]{2,1,0:T(8,128)S(1)}, u32[]{:S(2)}, u32[]{:S(2)}) %all-to-all-start.2) | async-done | bytes 65568 | tf_op jit(solution)/shard_map/all_to_all | solution.py:386
  113.1 0.9 place.1
  (30 shorter events, 0.2 us)
Async XLA Ops:
  0.6 11.8 %collective-permute-start = (bf16[2,16,1024]{2,1,0:T(8,128)(2,1)}, bf16[2,16,1024]{2,1,0:T(8,128)(2,1)S(1)}, u32[]{:S(2)}, u32[]{:S(2)}) collective-permute-start(bf16[2,16,1024]{2,1,0:T(8,128)(2,1)} %bitcast.39), channel_id=1, source_target_pairs={{0,4},{1,5},{2,6},{3,7},{4,0},{5,1},{6,2},{7,3},{8,12},{9,13},{10,... | collective-permute-start | bytes 196616 | tf_op jit(solution)/shard_map/ppermute | solution.py:337
  9.1 3.3 %copy-start.8 = (bf16[1,2,16,1024]{3,2,1,0:T(8,128)(2,1)S(1)}, bf16[1,2,16,1024]{3,2,1,0:T(8,128)(2,1)}, u32[]{:S(2)}) copy-start(bf16[1,2,16,1024]{3,2,1,0:T(8,128)(2,1)} %param.8) | copy-start | bytes 196612
  12.4 13.6 %copy-start.7 = (bf16[128,640]{1,0:T(8,128)(2,1)S(1)}, bf16[128,640]{1,0:T(8,128)(2,1)}, u32[]{:S(2)}) copy-start(bf16[128,640]{1,0:T(8,128)(2,1)} %get-tuple-element.49) | copy-start | bytes 491524
  12.5 8.0 %collective-permute-start.3 = (bf16[2,2,16,1024]{3,2,1,0:T(8,128)(2,1)S(1)}, bf16[2,2,16,1024]{3,2,1,0:T(8,128)(2,1)S(1)}, u32[]{:S(2)}, u32[]{:S(2)}) collective-permute-start(bf16[2,2,16,1024]{3,2,1,0:T(8,128)(2,1)S(1)} %pad_maximum_fusion.4), channel_id=1, source_target_pairs={{0,2},{1,3},{2,4},{3,5},{4,6},{5,7},{6,0},{7,1},{8,10},{9,11},{10,... | collective-permute-start | bytes 393224 | tf_op jit(solution)/shard_map/ppermute | solution.py:337
  13.7 12.3 %collective-permute-start.4 = (bf16[16,8,640]{2,1,0:T(8,128)(2,1)}, bf16[16,8,640]{2,1,0:T(8,128)(2,1)S(1)}, u32[]{:S(2)}, u32[]{:S(2)}) collective-permute-start(bf16[16,8,640]{2,1,0:T(8,128)(2,1)} %bitcast.44), channel_id=1, source_target_pairs={{0,16},{16,32},{32,48},{48,0},{1,17},{17,33},{33,49},{49,1},{2,18}... | collective-permute-start | bytes 491528 | tf_op jit(solution)/shard_map/ppermute | solution.py:337
  14.9 11.0 %collective-permute-start.5 = (bf16[16,8,640]{2,1,0:T(8,128)(2,1)}, bf16[16,8,640]{2,1,0:T(8,128)(2,1)S(1)}, u32[]{:S(2)}, u32[]{:S(2)}) collective-permute-start(bf16[16,8,640]{2,1,0:T(8,128)(2,1)} %bitcast.43), channel_id=1, source_target_pairs={{0,32},{16,48},{32,0},{48,16},{1,33},{17,49},{33,1},{49,17},{2,34}... | collective-permute-start | bytes 491528 | tf_op jit(solution)/shard_map/ppermute | solution.py:337
  17.4 8.6 %collective-permute-start.6 = (bf16[16,8,640]{2,1,0:T(8,128)(2,1)}, bf16[16,8,640]{2,1,0:T(8,128)(2,1)S(1)}, u32[]{:S(2)}, u32[]{:S(2)}) collective-permute-start(bf16[16,8,640]{2,1,0:T(8,128)(2,1)} %bitcast.42), channel_id=1, source_target_pairs={{0,48},{16,0},{32,16},{48,32},{1,49},{17,1},{33,17},{49,33},{2,50}... | collective-permute-start | bytes 491528 | tf_op jit(solution)/shard_map/ppermute | solution.py:337
  18.5 4.1 %collective-permute-start.2 = (bf16[2,2,16,1024]{3,2,1,0:T(8,128)(2,1)S(1)}, bf16[2,2,16,1024]{3,2,1,0:T(8,128)(2,1)S(1)}, u32[]{:S(2)}, u32[]{:S(2)}) collective-permute-start(bf16[2,2,16,1024]{3,2,1,0:T(8,128)(2,1)S(1)} %pad_maximum_fusion.4), channel_id=1, source_target_pairs={{0,7},{1,0},{2,1},{3,2},{4,3},{5,4},{6,5},{7,6},{8,15},{9,8},{10,9... | collective-permute-start | bytes 393224 | tf_op jit(solution)/shard_map/ppermute | solution.py:337
  20.5 5.5 %collective-permute-start.1 = (bf16[2,2,16,1024]{3,2,1,0:T(8,128)(2,1)S(1)}, bf16[2,2,16,1024]{3,2,1,0:T(8,128)(2,1)S(1)}, u32[]{:S(2)}, u32[]{:S(2)}) collective-permute-start(bf16[2,2,16,1024]{3,2,1,0:T(8,128)(2,1)S(1)} %pad_maximum_fusion.4), channel_id=1, source_target_pairs={{0,1},{1,2},{2,3},{3,4},{4,5},{5,6},{6,7},{7,0},{8,9},{9,10},{10,1... | collective-permute-start | bytes 393224 | tf_op jit(solution)/shard_map/ppermute | solution.py:337
  26.9 20.7 %all-to-all-start = ((bf16[16,4,8,640]{3,2,1,0:T(8,128)(2,1)}), bf16[16,4,8,640]{3,2,1,0:T(8,128)(2,1)S(1)}, u32[]{:S(2)}, u32[]{:S(2)}) async-start(bf16[16,4,8,640]{3,2,1,0:T(8,128)(2,1)} %pad_maximum_fusion.1), calls=%async_computation | async-start | bytes 1310720 | tf_op jit(solution)/shard_map/all_to_all | solution.py:368
  34.1 13.5 %collective-permute-start.10 = (bf16[4,2,16,1152]{3,2,1,0:T(8,128)(2,1)S(1)}, bf16[4,2,16,1152]{3,2,1,0:T(8,128)(2,1)S(1)}, u32[]{:S(2)}, u32[]{:S(2)}) collective-permute-start(bf16[4,2,16,1152]{3,2,1,0:T(8,128)(2,1)S(1)} %pad_maximum_fusion.3.refs_4_.second_0), channel_id=1, source_target_pairs={{0,8},{8,0},{1,9},{9,1},{2,10},{10,2},{3,11},{11,3},{4,12},{12,4},... | collective-permute-start | bytes 884744 | tf_op jit(solution)/shard_map/ppermute | solution.py:337
  37.1 4.9 %collective-permute-start.9 = (bf16[4,2,16,896]{3,2,1,0:T(8,128)(2,1)S(1)}, bf16[4,2,16,896]{3,2,1,0:T(8,128)(2,1)S(1)}, u32[]{:S(2)}, u32[]{:S(2)}) collective-permute-start(bf16[4,2,16,896]{3,2,1,0:T(8,128)(2,1)S(1)} %slice.16.refs_0_), channel_id=1, source_target_pairs={{0,48},{16,0},{32,16},{48,32},{1,49},{17,1},{33,17},{49,33},{2,50}... | collective-permute-start | bytes 688136 | tf_op jit(solution)/shard_map/ppermute | solution.py:337
  38.5 6.7 %collective-permute-start.8 = (bf16[4,2,16,896]{3,2,1,0:T(8,128)(2,1)S(1)}, bf16[4,2,16,896]{3,2,1,0:T(8,128)(2,1)S(1)}, u32[]{:S(2)}, u32[]{:S(2)}) collective-permute-start(bf16[4,2,16,896]{3,2,1,0:T(8,128)(2,1)S(1)} %slice.16.refs_0_), channel_id=1, source_target_pairs={{0,32},{16,48},{32,0},{48,16},{1,33},{17,49},{33,1},{49,17},{2,34}... | collective-permute-start | bytes 688136 | tf_op jit(solution)/shard_map/ppermute | solution.py:337
  39.1 8.6 %collective-permute-start.7 = (bf16[4,2,16,896]{3,2,1,0:T(8,128)(2,1)S(1)}, bf16[4,2,16,896]{3,2,1,0:T(8,128)(2,1)S(1)}, u32[]{:S(2)}, u32[]{:S(2)}) collective-permute-start(bf16[4,2,16,896]{3,2,1,0:T(8,128)(2,1)S(1)} %slice.16.refs_0_), channel_id=1, source_target_pairs={{0,16},{16,32},{32,48},{48,0},{1,17},{17,33},{33,49},{49,1},{2,18}... | collective-permute-start | bytes 688136 | tf_op jit(solution)/shard_map/ppermute | solution.py:337
  47.8 5.0 %copy-start = (bf16[1,2,1024,256]{3,2,1,0:T(8,128)(2,1)S(1)}, bf16[1,2,1024,256]{3,2,1,0:T(8,128)(2,1)}, u32[]{:S(2)}) copy-start(bf16[1,2,1024,256]{3,2,1,0:T(8,128)(2,1)} %param.9) | copy-start | bytes 3145732
  47.8 29.9 %collective-permute-start.11 = (bf16[16,2,16,896]{3,2,1,0:T(8,128)(2,1)S(1)}, bf16[16,2,16,896]{3,2,1,0:T(8,128)(2,1)S(1)}, u32[]{:S(2)}, u32[]{:S(2)}) collective-permute-start(bf16[16,2,16,896]{3,2,1,0:T(8,128)(2,1)S(1)} %pad_maximum_fusion), channel_id=1, source_target_pairs={{0,8},{8,0},{1,9},{9,1},{2,10},{10,2},{3,11},{11,3},{4,12},{12,4},... | collective-permute-start | bytes 2752520 | tf_op jit(solution)/shard_map/ppermute | solution.py:337
  48.9 2.3 %copy-start.2 = (s32[16384]{0:T(1024)S(1)}, s32[16384]{0:T(1024)}, u32[]{:S(2)}) copy-start(s32[16384]{0:T(1024)} %param.15) | copy-start | bytes 196612
  48.9 2.3 %copy-start.4 = (s32[2]{0:T(128)S(1)}, s32[2]{0:T(128)}, u32[]{:S(2)}) copy-start(s32[2]{0:T(128)} %pad_add_fusion.index) | copy-start | bytes 28
  48.9 22.2 %collective-permute-start.14 = (bf16[8,2,16,1152]{3,2,1,0:T(8,128)(2,1)S(1)}, bf16[8,2,16,1152]{3,2,1,0:T(8,128)(2,1)S(1)}, u32[]{:S(2)}, u32[]{:S(2)}) collective-permute-start(bf16[8,2,16,1152]{3,2,1,0:T(8,128)(2,1)S(1)} %constant_dynamic-update-slice_fusion.2), channel_id=1, source_target_pairs={{0,48},{16,0},{32,16},{48,32},{1,49},{17,1},{33,17},{49,33},{2,50}... | collective-permute-start | bytes 1769480 | tf_op jit(solution)/shard_map/ppermute | solution.py:337
  50.4 20.8 %collective-permute-start.13 = (bf16[8,2,16,1152]{3,2,1,0:T(8,128)(2,1)S(1)}, bf16[8,2,16,1152]{3,2,1,0:T(8,128)(2,1)S(1)}, u32[]{:S(2)}, u32[]{:S(2)}) collective-permute-start(bf16[8,2,16,1152]{3,2,1,0:T(8,128)(2,1)S(1)} %constant_dynamic-update-slice_fusion.2), channel_id=1, source_target_pairs={{0,32},{16,48},{32,0},{48,16},{1,33},{17,49},{33,1},{49,17},{2,34}... | collective-permute-start | bytes 1769480 | tf_op jit(solution)/shard_map/ppermute | solution.py:337
  50.4 27.2 %collective-permute-start.12 = (bf16[8,2,16,1152]{3,2,1,0:T(8,128)(2,1)S(1)}, bf16[8,2,16,1152]{3,2,1,0:T(8,128)(2,1)S(1)}, u32[]{:S(2)}, u32[]{:S(2)}) collective-permute-start(bf16[8,2,16,1152]{3,2,1,0:T(8,128)(2,1)S(1)} %constant_dynamic-update-slice_fusion.2), channel_id=1, source_target_pairs={{0,16},{16,32},{32,48},{48,0},{1,17},{17,33},{33,49},{49,1},{2,18}... | collective-permute-start | bytes 1769480 | tf_op jit(solution)/shard_map/ppermute | solution.py:337
  51.2 1.6 %copy-start.1 = (bf16[1,2,256,256]{3,2,1,0:T(8,128)(2,1)S(1)}, bf16[1,2,256,256]{3,2,1,0:T(8,128)(2,1)}, u32[]{:S(2)}) copy-start(bf16[1,2,256,256]{3,2,1,0:T(8,128)(2,1)} %param.11) | copy-start | bytes 786436
  52.3 18.8 %collective-permute-start.15 = (bf16[640,256]{1,0:T(8,128)(2,1)S(1)}, bf16[640,256]{1,0:T(8,128)(2,1)S(1)}, u32[]{:S(2)}, u32[]{:S(2)}) collective-permute-start(bf16[640,256]{1,0:T(8,128)(2,1)S(1)} %get-tuple-element.69.own), channel_id=1, source_target_pairs={{0,128},{128,0},{1,129},{129,1},{2,130},{130,2},{3,131},{131,3},{4... | collective-permute-start | bytes 983048 | tf_op jit(solution)/shard_map/ppermute | solution.py:337
  52.8 0.7 copy-start.5
  52.8 0.7 copy-start.6
  77.7 5.8 %collective-permute-start.16 = (bf16[2,640,256]{2,1,0:T(8,128)(2,1)S(1)}, bf16[2,640,256]{2,1,0:T(8,128)(2,1)S(1)}, u32[]{:S(2)}, u32[]{:S(2)}) collective-permute-start(bf16[2,640,256]{2,1,0:T(8,128)(2,1)S(1)} %pad_maximum_fusion.2), channel_id=1, source_target_pairs={{0,64},{64,0},{1,65},{65,1},{2,66},{66,2},{3,67},{67,3},{4,68},{68... | collective-permute-start | bytes 1966088 | tf_op jit(solution)/shard_map/ppermute | solution.py:337
  94.7 18.4 %all-to-all-start.2 = ((f32[16,8,128]{2,1,0:T(8,128)}), f32[16,8,128]{2,1,0:T(8,128)S(1)}, u32[]{:S(2)}, u32[]{:S(2)}) async-start(f32[16,8,128]{2,1,0:T(8,128)} %turn.1), calls=%async_computation.2 | async-start | bytes 131072 | tf_op jit(solution)/shard_map/all_to_all | solution.py:386
  104.3 8.9 %copy-start.3 = (bf16[512,256]{1,0:T(8,128)(2,1)S(1)}, bf16[512,256]{1,0:T(8,128)(2,1)}, u32[]{:S(2)}) copy-start(bf16[512,256]{1,0:T(8,128)(2,1)} %get-tuple-element.81.onehot) | copy-start | bytes 786436

commit v8 on v7

--- a/solution.py
+++ b/solution.py
@@ -19,7 +19,7 @@
 ROWS = 1280
 QUARTER = ROWS // POLES
 SHARD = ANC // GROUPS
-PART = 896
+PART = 768
 MIB = 1024 * 1024
 SMEM_SPEC = pl.BlockSpec(memory_space=pltpu.SMEM)
 VMEM_SPEC = pl.BlockSpec(memory_space=pltpu.VMEM)

time: 114 us -> 115 us (level)
  waiting for transfers between devices: 41.6 us -> 45.1 us
  starting transfers between devices: 46.1 us -> 43.6 us
    ppermute x17, waiting for transfers between devices: 34.2 us -> 37.6 us  [shift(): lax.ppermute(value, axis, [(n, (n + by) % size) for n in range(size)])]
    all_to_all x1, starting transfers between devices: 9.55 us -> 7.09 us  [body(): lax.all_to_all(turn(sums), ('yhi', 'z'), split_axis=0, concat_axis=0, til...]
  transfers between devices with their start and end apart: 19 -> 19, of which waited for: 7 -> 8; matrix products, arithmetic and copies ran while one was open for 1% -> 1% of each run, Pallas kernels for 9% -> 9%
where the time goes in v8:
time: 115 us
  waiting for transfers between devices  45.1 us (39%)
  starting transfers between devices  43.6 us (38%)
  Pallas kernels  14 us (12%)
  blocking collectives  8.31 us (7%)
  other arithmetic  1.79 us (2%)
    ppermute x17, waiting for transfers between devices, shift(): lax.ppermute(value, axis, [(n, (n + by) % size) for n in range(size)])  37.6 us
    ppermute x17, starting transfers between devices, shift(): lax.ppermute(value, axis, [(n, (n + by) % size) for n in range(size)])  29.5 us
    all_to_all x1, blocking collectives, body(): lax.all_to_all(slots, ('ylo', 'core', 'x'), split_axis=0, concat_axis=0,...  8.31 us
    all_to_all x1, waiting for transfers between devices, body(): lax.all_to_all(turn(sums), ('yhi', 'z'), split_axis=0, concat_axis=0, til...  7.41 us
    all_to_all x1, starting transfers between devices, body(): lax.all_to_all(jnp.stack(sent, axis=1), ('yhi', 'z'), split_axis=0, conca...  7.09 us
    all_to_all x1, starting transfers between devices, body(): lax.all_to_all(turn(sums), ('yhi', 'z'), split_axis=0, concat_axis=0, til...  7.09 us
    pallas_call x1, Pallas kernels, pack(): pl.pallas_call(pack_kernel, in_specs=[SMEM_SPEC, VMEM_SPEC, HBM_SPEC, HBM...  3.29 us
    pallas_call x1, Pallas kernels, upper_rows(): pl.pallas_call(upper_kernel, in_specs=[SMEM_SPEC] * 2 + [VMEM_SPEC] * (2...  3.23 us
  transfers between devices with their start and end apart: 19, of which 8 were waited for; matrix products, arithmetic and copies ran while one was open for 1% of the time, Pallas kernels for 9%

profile of v8, /device:TPU:1, one launch (start us, length us, event | category | flops | bytes accessed | tf_op | source)
XLA Modules:
  0.0 114.5 jit_solution(9258020057167111502)
XLA Ops:
  0.6 7.8 %collective-permute-start = (bf16[2,16,1024]{2,1,0:T(8,128)(2,1)}, bf16[2,16,1024]{2,1,0:T(8,128)(2,1)S(1)}, u32[]{:S(2)}, u32[]{:S(2)}) collective-permute-start(bf16[2,16,1024]{2,1,0:T(8,128)(2,1)} %bitcast.39), channel_id=1, source_target_pairs={{0,4},{1,5},{2,6},{3,7},{4,0},{5,1},{6,2},{7,3},{8,12},{9,13},{10,... | collective-permute-start | bytes 196616 | tf_op jit(solution)/shard_map/ppermute | solution.py:337
  8.5 0.6 pad_add_fusion.index
  9.1 3.3 %pack.1 = (bf16[128,640]{1,0:T(8,128)(2,1)}, bf16[128,640]{1,0:T(8,128)(2,1)}, bf16[128,640]{1,0:T(8,128)(2,1)}, bf16[128,640]{1,0:T(8,128)(2,1)}, bf16[512,256]{1,0:T(8,128)(2,1)}) custom-call(s32[2]{0:T(128)} %pad_add_fusion.index, s32[128,128]{1,0:T(8,128)} %bitcast.32, bf16[1280,256]{1,0:T(8,128)(2,1)} %margin.1, bf16[1280,256]{1,0:T(8,128)(2,1)} %hamiltonian.1), custom_call_target="tpu_custom_call" | custom-call | tf_op jit(solution)/shard_map/pack/pallas_call | solution.py:91
  12.4 0.0 copy-start.7
  12.5 1.3 %collective-permute-start.3 = (bf16[2,2,16,1024]{3,2,1,0:T(8,128)(2,1)S(1)}, bf16[2,2,16,1024]{3,2,1,0:T(8,128)(2,1)S(1)}, u32[]{:S(2)}, u32[]{:S(2)}) collective-permute-start(bf16[2,2,16,1024]{3,2,1,0:T(8,128)(2,1)S(1)} %pad_maximum_fusion.4), channel_id=1, source_target_pairs={{0,2},{1,3},{2,4},{3,5},{4,6},{5,7},{6,0},{7,1},{8,10},{9,11},{10,... | collective-permute-start | bytes 393224 | tf_op jit(solution)/shard_map/ppermute | solution.py:337
  13.7 1.2 %collective-permute-start.4 = (bf16[16,8,640]{2,1,0:T(8,128)(2,1)}, bf16[16,8,640]{2,1,0:T(8,128)(2,1)S(1)}, u32[]{:S(2)}, u32[]{:S(2)}) collective-permute-start(bf16[16,8,640]{2,1,0:T(8,128)(2,1)} %bitcast.44), channel_id=1, source_target_pairs={{0,16},{16,32},{32,48},{48,0},{1,17},{17,33},{33,49},{49,1},{2,18}... | collective-permute-start | bytes 491528 | tf_op jit(solution)/shard_map/ppermute | solution.py:337
  14.9 2.4 %collective-permute-start.5 = (bf16[16,8,640]{2,1,0:T(8,128)(2,1)}, bf16[16,8,640]{2,1,0:T(8,128)(2,1)S(1)}, u32[]{:S(2)}, u32[]{:S(2)}) collective-permute-start(bf16[16,8,640]{2,1,0:T(8,128)(2,1)} %bitcast.43), channel_id=1, source_target_pairs={{0,32},{16,48},{32,0},{48,16},{1,33},{17,49},{33,1},{49,17},{2,34}... | collective-permute-start | bytes 491528 | tf_op jit(solution)/shard_map/ppermute | solution.py:337
  17.4 1.2 %collective-permute-start.6 = (bf16[16,8,640]{2,1,0:T(8,128)(2,1)}, bf16[16,8,640]{2,1,0:T(8,128)(2,1)S(1)}, u32[]{:S(2)}, u32[]{:S(2)}) collective-permute-start(bf16[16,8,640]{2,1,0:T(8,128)(2,1)} %bitcast.42), channel_id=1, source_target_pairs={{0,48},{16,0},{32,16},{48,32},{1,49},{17,1},{33,17},{49,33},{2,50}... | collective-permute-start | bytes 491528 | tf_op jit(solution)/shard_map/ppermute | solution.py:337
  18.5 1.9 %collective-permute-start.2 = (bf16[2,2,16,1024]{3,2,1,0:T(8,128)(2,1)S(1)}, bf16[2,2,16,1024]{3,2,1,0:T(8,128)(2,1)S(1)}, u32[]{:S(2)}, u32[]{:S(2)}) collective-permute-start(bf16[2,2,16,1024]{3,2,1,0:T(8,128)(2,1)S(1)} %pad_maximum_fusion.4), channel_id=1, source_target_pairs={{0,7},{1,0},{2,1},{3,2},{4,3},{5,4},{6,5},{7,6},{8,15},{9,8},{10,9... | collective-permute-start | bytes 393224 | tf_op jit(solution)/shard_map/ppermute | solution.py:337
  20.5 2.2 %collective-permute-start.1 = (bf16[2,2,16,1024]{3,2,1,0:T(8,128)(2,1)S(1)}, bf16[2,2,16,1024]{3,2,1,0:T(8,128)(2,1)S(1)}, u32[]{:S(2)}, u32[]{:S(2)}) collective-permute-start(bf16[2,2,16,1024]{3,2,1,0:T(8,128)(2,1)S(1)} %pad_maximum_fusion.4), channel_id=1, source_target_pairs={{0,1},{1,2},{2,3},{3,4},{4,5},{5,6},{6,7},{7,0},{8,9},{9,10},{10,1... | collective-permute-start | bytes 393224 | tf_op jit(solution)/shard_map/ppermute | solution.py:337
  22.7 0.0 collective-permute-done.2
  22.7 3.3 %collective-permute-done.1 = bf16[2,2,16,1024]{3,2,1,0:T(8,128)(2,1)S(1)} collective-permute-done((bf16[2,2,16,1024]{3,2,1,0:T(8,128)(2,1)S(1)}, bf16[2,2,16,1024]{3,2,1,0:T(8,128)(2,1)S(1)}, u32[]{:S(2)}, u32[]{:S(2)}) %collective-permute-start.1) | collective-permute-done | bytes 131104 | tf_op jit(solution)/shard_map/ppermute | solution.py:337
  26.0 0.0 collective-permute-done.4
  26.0 0.0 collective-permute-done.5
  26.0 0.0 collective-permute-done.6
  26.0 0.9 pad_maximum_fusion.1
  26.9 7.1 %all-to-all-start = ((bf16[16,4,8,640]{3,2,1,0:T(8,128)(2,1)}), bf16[16,4,8,640]{3,2,1,0:T(8,128)(2,1)S(1)}, u32[]{:S(2)}, u32[]{:S(2)}) async-start(bf16[16,4,8,640]{3,2,1,0:T(8,128)(2,1)} %pad_maximum_fusion.1), calls=%async_computation | async-start | bytes 1310720 | tf_op jit(solution)/shard_map/all_to_all | solution.py:368
  34.1 3.0 %collective-permute-start.10 = (bf16[4,2,16,1280]{3,2,1,0:T(8,128)(2,1)S(1)}, bf16[4,2,16,1280]{3,2,1,0:T(8,128)(2,1)S(1)}, u32[]{:S(2)}, u32[]{:S(2)}) collective-permute-start(bf16[4,2,16,1280]{3,2,1,0:T(8,128)(2,1)S(1)} %pad_maximum_fusion.3.refs_4_.second_0), channel_id=1, source_target_pairs={{0,8},{8,0},{1,9},{9,1},{2,10},{10,2},{3,11},{11,3},{4,12},{12,4},... | collective-permute-start | bytes 983048 | tf_op jit(solution)/shard_map/ppermute | solution.py:337
  37.1 1.4 %collective-permute-start.9 = (bf16[4,2,16,768]{3,2,1,0:T(8,128)(2,1)S(1)}, bf16[4,2,16,768]{3,2,1,0:T(8,128)(2,1)S(1)}, u32[]{:S(2)}, u32[]{:S(2)}) collective-permute-start(bf16[4,2,16,768]{3,2,1,0:T(8,128)(2,1)S(1)} %slice.16.refs_0_), channel_id=1, source_target_pairs={{0,48},{16,0},{32,16},{48,32},{1,49},{17,1},{33,17},{49,33},{2,50}... | collective-permute-start | bytes 589832 | tf_op jit(solution)/shard_map/ppermute | solution.py:337
  38.5 0.6 collective-permute-start.8
  39.1 0.3 collective-permute-start.7
  39.4 2.3 %collective-permute-done.9.refs_3_ = bf16[4,2,16,768]{3,2,1,0:T(8,128)(2,1)S(1)} collective-permute-done((bf16[4,2,16,768]{3,2,1,0:T(8,128)(2,1)S(1)}, bf16[4,2,16,768]{3,2,1,0:T(8,128)(2,1)S(1)}, u32[]{:S(2)}, u32[]{:S(2)}) %collective-permute-start.9) | collective-permute-done | bytes 196640 | tf_op jit(solution)/shard_map/ppermute | solution.py:337
  41.7 3.2 %collective-permute-done.8.refs_2_ = bf16[4,2,16,768]{3,2,1,0:T(8,128)(2,1)S(1)} collective-permute-done((bf16[4,2,16,768]{3,2,1,0:T(8,128)(2,1)S(1)}, bf16[4,2,16,768]{3,2,1,0:T(8,128)(2,1)S(1)}, u32[]{:S(2)}, u32[]{:S(2)}) %collective-permute-start.8) | collective-permute-done | bytes 196640 | tf_op jit(solution)/shard_map/ppermute | solution.py:337
  44.9 2.1 %collective-permute-done.7.refs_1_ = bf16[4,2,16,768]{3,2,1,0:T(8,128)(2,1)S(1)} collective-permute-done((bf16[4,2,16,768]{3,2,1,0:T(8,128)(2,1)S(1)}, bf16[4,2,16,768]{3,2,1,0:T(8,128)(2,1)S(1)}, u32[]{:S(2)}, u32[]{:S(2)}) %collective-permute-start.7) | collective-permute-done | bytes 196640 | tf_op jit(solution)/shard_map/ppermute | solution.py:337
  47.0 0.1 all-to-all-done
  47.1 0.0 copy-start.2
  47.1 0.1 pad_maximum_fusion
  47.2 0.0 copy-start
  47.2 1.6 %collective-permute-start.11 = (bf16[16,2,16,768]{3,2,1,0:T(8,128)(2,1)S(1)}, bf16[16,2,16,768]{3,2,1,0:T(8,128)(2,1)S(1)}, u32[]{:S(2)}, u32[]{:S(2)}) collective-permute-start(bf16[16,2,16,768]{3,2,1,0:T(8,128)(2,1)S(1)} %pad_maximum_fusion), channel_id=1, source_target_pairs={{0,8},{8,0},{1,9},{9,1},{2,10},{10,2},{3,11},{11,3},{4,12},{12,4},... | collective-permute-start | bytes 2359304 | tf_op jit(solution)/shard_map/ppermute | solution.py:337
  48.9 2.1 %collective-permute-start.14 = (bf16[8,2,16,1280]{3,2,1,0:T(8,128)(2,1)S(1)}, bf16[8,2,16,1280]{3,2,1,0:T(8,128)(2,1)S(1)}, u32[]{:S(2)}, u32[]{:S(2)}) collective-permute-start(bf16[8,2,16,1280]{3,2,1,0:T(8,128)(2,1)S(1)} %constant_dynamic-update-slice_fusion.2), channel_id=1, source_target_pairs={{0,48},{16,0},{32,16},{48,32},{1,49},{17,1},{33,17},{49,33},{2,50}... | collective-permute-start | bytes 1966088 | tf_op jit(solution)/shard_map/ppermute | solution.py:337
  51.0 0.7 collective-permute-start.12
  51.6 1.1 unpack.1
  52.8 0.5 collective-permute-start.15
  53.3 0.6 copy-done.5
  53.9 0.0 copy-done.6
  53.9 1.5 %start.1 = (bf16[1024,512]{1,0:T(8,128)(2,1)S(1)}, f32[2,384,256]{2,1,0:T(8,128)S(1)}, f32[256,256]{1,0:T(8,128)S(1)}) custom-call(f32[1,2]{1,0:T(1,128)S(1)} %copy-done.6, s32[1,4]{1,0:T(1,128)S(1)} %copy-done.5, bf16[2,1024,256]{2,1,0:T(8,128)(2,1)S(1)} %bitcast.29, bf16[2,256,256]{2,1,0:T(8,128)(2,1)S(1)} %bitcast.30, ...), custom_call_target="tpu_custom_call" | custom-call | tf_op jit(solution)/shard_map/start/pallas_call | solution.py:164
  55.4 14.1 %collective-permute-done.15.own_far = bf16[640,256]{1,0:T(8,128)(2,1)S(1)} collective-permute-done((bf16[640,256]{1,0:T(8,128)(2,1)S(1)}, bf16[640,256]{1,0:T(8,128)(2,1)S(1)}, u32[]{:S(2)}, u32[]{:S(2)}) %collective-permute-start.15) | collective-permute-done | bytes 327712 | tf_op jit(solution)/shard_map/ppermute | solution.py:337
  69.5 12.6 %collective-permute-done.12.second_1 = bf16[8,2,16,1280]{3,2,1,0:T(8,128)(2,1)S(1)} collective-permute-done((bf16[8,2,16,1280]{3,2,1,0:T(8,128)(2,1)S(1)}, bf16[8,2,16,1280]{3,2,1,0:T(8,128)(2,1)S(1)}, u32[]{:S(2)}, u32[]{:S(2)}) %collective-permute-start.12) | collective-permute-done | bytes 655392 | tf_op jit(solution)/shard_map/ppermute | solution.py:337
  82.1 0.1 pad_maximum_fusion.2
  82.1 1.4 %collective-permute-start.16 = (bf16[2,640,256]{2,1,0:T(8,128)(2,1)S(1)}, bf16[2,640,256]{2,1,0:T(8,128)(2,1)S(1)}, u32[]{:S(2)}, u32[]{:S(2)}) collective-permute-start(bf16[2,640,256]{2,1,0:T(8,128)(2,1)S(1)} %pad_maximum_fusion.2), channel_id=1, source_target_pairs={{0,64},{64,0},{1,65},{65,1},{2,66},{66,2},{3,67},{67,3},{4,68},{68... | collective-permute-start | bytes 1966088 | tf_op jit(solution)/shard_map/ppermute | solution.py:337
  83.5 3.2 %upper.1 = (bf16[2,1024,256]{2,1,0:T(8,128)(2,1)}, bf16[2,1024,256]{2,1,0:T(8,128)(2,1)S(1)}) custom-call(s32[2]{0:T(128)S(1)} %copy-done.4, s32[1,4]{1,0:T(1,128)S(1)} %copy-done.5, bf16[1024,512]{1,0:T(8,128)(2,1)S(1)} %get-tuple-element.67.rhs.lower, f32[2,384,256]{2,1,0:T(8,128)S(1)} %get-tuple-element.71.early, ...), custom_call_target="tpu_custom_call" | custom-call | tf_op jit(solution)/shard_map/upper/pallas_call | solution.py:210
  86.8 1.9 %charge.1 = f32[16,8,128]{2,1,0:T(8,128)S(1)} custom-call(s32[2]{0:T(128)S(1)} %copy-done.4, f32[1,2]{1,0:T(1,128)S(1)} %copy-done.6, bf16[1024,512]{1,0:T(8,128)(2,1)S(1)} %get-tuple-element.67.rhs.lower, f32[256,256]{1,0:T(8,128)S(1)} %get-tuple-element.78.sums, bf16[640,256]{1,0:T(8,128)(2,1)S(1)} %get-tuple-element.69.own, ...), custom_call_target="tpu_custom_call" | custom-call | tf_op jit(solution)/shard_map/charge/pallas_call | solution.py:252
  88.7 8.3 %all_to_all.15.arrived = f32[16,8,128]{2,1,0:T(8,128)S(1)} all-to-all(f32[16,8,128]{2,1,0:T(8,128)S(1)} %charge.1), channel_id=1, replica_groups=mesh['ylo'=2,'core'=2,'x'=4,'yhi'=2,'z'=8] {'ylo','core','x'}, dimensions={0} | all-to-all | bytes 131072 | tf_op jit(solution)/shard_map/all_to_all | solution.py:385
  97.0 0.7 turn.1
  97.7 7.1 %all-to-all-start.2 = ((f32[16,8,128]{2,1,0:T(8,128)}), f32[16,8,128]{2,1,0:T(8,128)S(1)}, u32[]{:S(2)}, u32[]{:S(2)}) async-start(f32[16,8,128]{2,1,0:T(8,128)} %turn.1), calls=%async_computation.2 | async-start | bytes 131072 | tf_op jit(solution)/shard_map/all_to_all | solution.py:386
  104.8 1.5 %diag.1 = bf16[2,256,256]{2,1,0:T(8,128)(2,1)} custom-call(bf16[1024,512]{1,0:T(8,128)(2,1)S(1)} %get-tuple-element.67.rhs.lower, bf16[2,1024,256]{2,1,0:T(8,128)(2,1)S(1)} %get-tuple-element.77.upper, bf16[2,256,256]{2,1,0:T(8,128)(2,1)S(1)} %bitcast.31), custom_call_target="tpu_custom_call" | custom-call | tf_op jit(solution)/shard_map/diag/pallas_call | solution.py:278
  106.3 7.4 %all-to-all-done.2.arrived = f32[16,8,128]{2,1,0:T(8,128)S(1)} async-done(((f32[16,8,128]{2,1,0:T(8,128)}), f32[16,8,128]{2,1,0:T(8,128)S(1)}, u32[]{:S(2)}, u32[]{:S(2)}) %all-to-all-start.2) | async-done | bytes 65568 | tf_op jit(solution)/shard_map/all_to_all | solution.py:386
  113.7 0.9 place.1
  (30 shorter events, 0.2 us)
Async XLA Ops:
  0.6 11.8 %collective-permute-start = (bf16[2,16,1024]{2,1,0:T(8,128)(2,1)}, bf16[2,16,1024]{2,1,0:T(8,128)(2,1)S(1)}, u32[]{:S(2)}, u32[]{:S(2)}) collective-permute-start(bf16[2,16,1024]{2,1,0:T(8,128)(2,1)} %bitcast.39), channel_id=1, source_target_pairs={{0,4},{1,5},{2,6},{3,7},{4,0},{5,1},{6,2},{7,3},{8,12},{9,13},{10,... | collective-permute-start | bytes 196616 | tf_op jit(solution)/shard_map/ppermute | solution.py:337
  9.1 3.3 %copy-start.8 = (bf16[1,2,16,1024]{3,2,1,0:T(8,128)(2,1)S(1)}, bf16[1,2,16,1024]{3,2,1,0:T(8,128)(2,1)}, u32[]{:S(2)}) copy-start(bf16[1,2,16,1024]{3,2,1,0:T(8,128)(2,1)} %param.8) | copy-start | bytes 196612
  12.4 13.6 %copy-start.7 = (bf16[128,640]{1,0:T(8,128)(2,1)S(1)}, bf16[128,640]{1,0:T(8,128)(2,1)}, u32[]{:S(2)}) copy-start(bf16[128,640]{1,0:T(8,128)(2,1)} %get-tuple-element.49) | copy-start | bytes 491524
  12.5 8.0 %collective-permute-start.3 = (bf16[2,2,16,1024]{3,2,1,0:T(8,128)(2,1)S(1)}, bf16[2,2,16,1024]{3,2,1,0:T(8,128)(2,1)S(1)}, u32[]{:S(2)}, u32[]{:S(2)}) collective-permute-start(bf16[2,2,16,1024]{3,2,1,0:T(8,128)(2,1)S(1)} %pad_maximum_fusion.4), channel_id=1, source_target_pairs={{0,2},{1,3},{2,4},{3,5},{4,6},{5,7},{6,0},{7,1},{8,10},{9,11},{10,... | collective-permute-start | bytes 393224 | tf_op jit(solution)/shard_map/ppermute | solution.py:337
  13.7 12.3 %collective-permute-start.4 = (bf16[16,8,640]{2,1,0:T(8,128)(2,1)}, bf16[16,8,640]{2,1,0:T(8,128)(2,1)S(1)}, u32[]{:S(2)}, u32[]{:S(2)}) collective-permute-start(bf16[16,8,640]{2,1,0:T(8,128)(2,1)} %bitcast.44), channel_id=1, source_target_pairs={{0,16},{16,32},{32,48},{48,0},{1,17},{17,33},{33,49},{49,1},{2,18}... | collective-permute-start | bytes 491528 | tf_op jit(solution)/shard_map/ppermute | solution.py:337
  14.9 11.0 %collective-permute-start.5 = (bf16[16,8,640]{2,1,0:T(8,128)(2,1)}, bf16[16,8,640]{2,1,0:T(8,128)(2,1)S(1)}, u32[]{:S(2)}, u32[]{:S(2)}) collective-permute-start(bf16[16,8,640]{2,1,0:T(8,128)(2,1)} %bitcast.43), channel_id=1, source_target_pairs={{0,32},{16,48},{32,0},{48,16},{1,33},{17,49},{33,1},{49,17},{2,34}... | collective-permute-start | bytes 491528 | tf_op jit(solution)/shard_map/ppermute | solution.py:337
  17.4 8.6 %collective-permute-start.6 = (bf16[16,8,640]{2,1,0:T(8,128)(2,1)}, bf16[16,8,640]{2,1,0:T(8,128)(2,1)S(1)}, u32[]{:S(2)}, u32[]{:S(2)}) collective-permute-start(bf16[16,8,640]{2,1,0:T(8,128)(2,1)} %bitcast.42), channel_id=1, source_target_pairs={{0,48},{16,0},{32,16},{48,32},{1,49},{17,1},{33,17},{49,33},{2,50}... | collective-permute-start | bytes 491528 | tf_op jit(solution)/shard_map/ppermute | solution.py:337
  18.5 4.1 %collective-permute-start.2 = (bf16[2,2,16,1024]{3,2,1,0:T(8,128)(2,1)S(1)}, bf16[2,2,16,1024]{3,2,1,0:T(8,128)(2,1)S(1)}, u32[]{:S(2)}, u32[]{:S(2)}) collective-permute-start(bf16[2,2,16,1024]{3,2,1,0:T(8,128)(2,1)S(1)} %pad_maximum_fusion.4), channel_id=1, source_target_pairs={{0,7},{1,0},{2,1},{3,2},{4,3},{5,4},{6,5},{7,6},{8,15},{9,8},{10,9... | collective-permute-start | bytes 393224 | tf_op jit(solution)/shard_map/ppermute | solution.py:337
  20.5 5.5 %collective-permute-start.1 = (bf16[2,2,16,1024]{3,2,1,0:T(8,128)(2,1)S(1)}, bf16[2,2,16,1024]{3,2,1,0:T(8,128)(2,1)S(1)}, u32[]{:S(2)}, u32[]{:S(2)}) collective-permute-start(bf16[2,2,16,1024]{3,2,1,0:T(8,128)(2,1)S(1)} %pad_maximum_fusion.4), channel_id=1, source_target_pairs={{0,1},{1,2},{2,3},{3,4},{4,5},{5,6},{6,7},{7,0},{8,9},{9,10},{10,1... | collective-permute-start | bytes 393224 | tf_op jit(solution)/shard_map/ppermute | solution.py:337
  26.9 20.1 %all-to-all-start = ((bf16[16,4,8,640]{3,2,1,0:T(8,128)(2,1)}), bf16[16,4,8,640]{3,2,1,0:T(8,128)(2,1)S(1)}, u32[]{:S(2)}, u32[]{:S(2)}) async-start(bf16[16,4,8,640]{3,2,1,0:T(8,128)(2,1)} %pad_maximum_fusion.1), calls=%async_computation | async-start | bytes 1310720 | tf_op jit(solution)/shard_map/all_to_all | solution.py:368
  34.1 12.8 %collective-permute-start.10 = (bf16[4,2,16,1280]{3,2,1,0:T(8,128)(2,1)S(1)}, bf16[4,2,16,1280]{3,2,1,0:T(8,128)(2,1)S(1)}, u32[]{:S(2)}, u32[]{:S(2)}) collective-permute-start(bf16[4,2,16,1280]{3,2,1,0:T(8,128)(2,1)S(1)} %pad_maximum_fusion.3.refs_4_.second_0), channel_id=1, source_target_pairs={{0,8},{8,0},{1,9},{9,1},{2,10},{10,2},{3,11},{11,3},{4,12},{12,4},... | collective-permute-start | bytes 983048 | tf_op jit(solution)/shard_map/ppermute | solution.py:337
  37.1 4.6 %collective-permute-start.9 = (bf16[4,2,16,768]{3,2,1,0:T(8,128)(2,1)S(1)}, bf16[4,2,16,768]{3,2,1,0:T(8,128)(2,1)S(1)}, u32[]{:S(2)}, u32[]{:S(2)}) collective-permute-start(bf16[4,2,16,768]{3,2,1,0:T(8,128)(2,1)S(1)} %slice.16.refs_0_), channel_id=1, source_target_pairs={{0,48},{16,0},{32,16},{48,32},{1,49},{17,1},{33,17},{49,33},{2,50}... | collective-permute-start | bytes 589832 | tf_op jit(solution)/shard_map/ppermute | solution.py:337
  38.5 6.4 %collective-permute-start.8 = (bf16[4,2,16,768]{3,2,1,0:T(8,128)(2,1)S(1)}, bf16[4,2,16,768]{3,2,1,0:T(8,128)(2,1)S(1)}, u32[]{:S(2)}, u32[]{:S(2)}) collective-permute-start(bf16[4,2,16,768]{3,2,1,0:T(8,128)(2,1)S(1)} %slice.16.refs_0_), channel_id=1, source_target_pairs={{0,32},{16,48},{32,0},{48,16},{1,33},{17,49},{33,1},{49,17},{2,34}... | collective-permute-start | bytes 589832 | tf_op jit(solution)/shard_map/ppermute | solution.py:337
  39.1 7.9 %collective-permute-start.7 = (bf16[4,2,16,768]{3,2,1,0:T(8,128)(2,1)S(1)}, bf16[4,2,16,768]{3,2,1,0:T(8,128)(2,1)S(1)}, u32[]{:S(2)}, u32[]{:S(2)}) collective-permute-start(bf16[4,2,16,768]{3,2,1,0:T(8,128)(2,1)S(1)} %slice.16.refs_0_), channel_id=1, source_target_pairs={{0,16},{16,32},{32,48},{48,0},{1,17},{17,33},{33,49},{49,1},{2,18}... | collective-permute-start | bytes 589832 | tf_op jit(solution)/shard_map/ppermute | solution.py:337
  47.1 4.5 %copy-start.2 = (s32[16384]{0:T(1024)S(1)}, s32[16384]{0:T(1024)}, u32[]{:S(2)}) copy-start(s32[16384]{0:T(1024)} %param.15) | copy-start | bytes 196612
  47.1 4.5 %copy-start.4 = (s32[2]{0:T(128)S(1)}, s32[2]{0:T(128)}, u32[]{:S(2)}) copy-start(s32[2]{0:T(128)} %pad_add_fusion.index) | copy-start | bytes 28
  47.2 6.0 %copy-start = (bf16[1,2,1024,256]{3,2,1,0:T(8,128)(2,1)S(1)}, bf16[1,2,1024,256]{3,2,1,0:T(8,128)(2,1)}, u32[]{:S(2)}) copy-start(bf16[1,2,1024,256]{3,2,1,0:T(8,128)(2,1)} %param.9) | copy-start | bytes 3145732
  47.2 34.8 %collective-permute-start.11 = (bf16[16,2,16,768]{3,2,1,0:T(8,128)(2,1)S(1)}, bf16[16,2,16,768]{3,2,1,0:T(8,128)(2,1)S(1)}, u32[]{:S(2)}, u32[]{:S(2)}) collective-permute-start(bf16[16,2,16,768]{3,2,1,0:T(8,128)(2,1)S(1)} %pad_maximum_fusion), channel_id=1, source_target_pairs={{0,8},{8,0},{1,9},{9,1},{2,10},{10,2},{3,11},{11,3},{4,12},{12,4},... | collective-permute-start | bytes 2359304 | tf_op jit(solution)/shard_map/ppermute | solution.py:337
  48.9 20.6 %collective-permute-start.14 = (bf16[8,2,16,1280]{3,2,1,0:T(8,128)(2,1)S(1)}, bf16[8,2,16,1280]{3,2,1,0:T(8,128)(2,1)S(1)}, u32[]{:S(2)}, u32[]{:S(2)}) collective-permute-start(bf16[8,2,16,1280]{3,2,1,0:T(8,128)(2,1)S(1)} %constant_dynamic-update-slice_fusion.2), channel_id=1, source_target_pairs={{0,48},{16,0},{32,16},{48,32},{1,49},{17,1},{33,17},{49,33},{2,50}... | collective-permute-start | bytes 1966088 | tf_op jit(solution)/shard_map/ppermute | solution.py:337
  50.9 18.5 %collective-permute-start.13 = (bf16[8,2,16,1280]{3,2,1,0:T(8,128)(2,1)S(1)}, bf16[8,2,16,1280]{3,2,1,0:T(8,128)(2,1)S(1)}, u32[]{:S(2)}, u32[]{:S(2)}) collective-permute-start(bf16[8,2,16,1280]{3,2,1,0:T(8,128)(2,1)S(1)} %constant_dynamic-update-slice_fusion.2), channel_id=1, source_target_pairs={{0,32},{16,48},{32,0},{48,16},{1,33},{17,49},{33,1},{49,17},{2,34}... | collective-permute-start | bytes 1966088 | tf_op jit(solution)/shard_map/ppermute | solution.py:337
  51.0 31.1 %collective-permute-start.12 = (bf16[8,2,16,1280]{3,2,1,0:T(8,128)(2,1)S(1)}, bf16[8,2,16,1280]{3,2,1,0:T(8,128)(2,1)S(1)}, u32[]{:S(2)}, u32[]{:S(2)}) collective-permute-start(bf16[8,2,16,1280]{3,2,1,0:T(8,128)(2,1)S(1)} %constant_dynamic-update-slice_fusion.2), channel_id=1, source_target_pairs={{0,16},{16,32},{32,48},{48,0},{1,17},{17,33},{33,49},{49,1},{2,18}... | collective-permute-start | bytes 1966088 | tf_op jit(solution)/shard_map/ppermute | solution.py:337
  51.6 1.6 %copy-start.1 = (bf16[1,2,256,256]{3,2,1,0:T(8,128)(2,1)S(1)}, bf16[1,2,256,256]{3,2,1,0:T(8,128)(2,1)}, u32[]{:S(2)}) copy-start(bf16[1,2,256,256]{3,2,1,0:T(8,128)(2,1)} %param.11) | copy-start | bytes 786436
  52.8 16.7 %collective-permute-start.15 = (bf16[640,256]{1,0:T(8,128)(2,1)S(1)}, bf16[640,256]{1,0:T(8,128)(2,1)S(1)}, u32[]{:S(2)}, u32[]{:S(2)}) collective-permute-start(bf16[640,256]{1,0:T(8,128)(2,1)S(1)} %get-tuple-element.69.own), channel_id=1, source_target_pairs={{0,128},{128,0},{1,129},{129,1},{2,130},{130,2},{3,131},{131,3},{4... | collective-permute-start | bytes 983048 | tf_op jit(solution)/shard_map/ppermute | solution.py:337
  53.2 0.7 copy-start.5
  53.2 0.7 copy-start.6
  82.1 4.6 %collective-permute-start.16 = (bf16[2,640,256]{2,1,0:T(8,128)(2,1)S(1)}, bf16[2,640,256]{2,1,0:T(8,128)(2,1)S(1)}, u32[]{:S(2)}, u32[]{:S(2)}) collective-permute-start(bf16[2,640,256]{2,1,0:T(8,128)(2,1)S(1)} %pad_maximum_fusion.2), channel_id=1, source_target_pairs={{0,64},{64,0},{1,65},{65,1},{2,66},{66,2},{3,67},{67,3},{4,68},{68... | collective-permute-start | bytes 1966088 | tf_op jit(solution)/shard_map/ppermute | solution.py:337
  97.7 16.0 %all-to-all-start.2 = ((f32[16,8,128]{2,1,0:T(8,128)}), f32[16,8,128]{2,1,0:T(8,128)S(1)}, u32[]{:S(2)}, u32[]{:S(2)}) async-start(f32[16,8,128]{2,1,0:T(8,128)} %turn.1), calls=%async_computation.2 | async-start | bytes 131072 | tf_op jit(solution)/shard_map/all_to_all | solution.py:386
  104.8 8.9 %copy-start.3 = (bf16[512,256]{1,0:T(8,128)(2,1)S(1)}, bf16[512,256]{1,0:T(8,128)(2,1)}, u32[]{:S(2)}) copy-start(bf16[512,256]{1,0:T(8,128)(2,1)} %get-tuple-element.81.onehot) | copy-start | bytes 786436
